TPU v7x, 256 devices: a whole 4x4x8 slice. The times are simulated.
256 devices in a mesh: curve: 128 (over x, z, y_hi, core), sub: 2 (over y_lo).
Axes of the slice: x: 4, y: 4 (y_hi: 2, y_lo: 2; y = y_hi * 2 + y_lo), z: 8, core: 2. Of those that a mesh axis runs over, the one named last changes fastest.
Arguments:
- features: bfloat16 [131072, 512], P(('curve', 'sub')), may hold values from -6 to 6
- hub_features: bfloat16 [1024, 512], P(('curve', 'sub')), may hold values from -6 to 6
- hub_order: int32 [1024], replicated, may hold values from 0 to 1023, each once
- tile_values: bfloat16 [16384, 128, 128], P(('curve', 'sub')), may hold values from -0.1875 to 0.1875
- tile_dest: int32 [256, 64], P(('curve', 'sub')), may hold values from 0 to 3
- tile_source: int32 [256, 64], P(('curve', 'sub')), may hold values from 0 to 31, as said below
- tile_count: int32 [256], P(('curve', 'sub')), may hold values from 8 to 64, as said below
- self_weight: bfloat16 [512, 512], replicated, may hold values from -0.25 to 0.25
- neighbour_weight: bfloat16 [512, 512], replicated, may hold values from -0.25 to 0.25
- cotangent: bfloat16 [131072, 512], P(('curve', 'sub')), may hold values from -6 to 6
Outputs:
- embedding: bfloat16 [131072, 512], P(('curve', 'sub'))
- feature_gradient: float32 [131072, 512], P(('curve', 'sub'))
- hub_gradient: float32 [1024, 512], P(('curve', 'sub'))
- self_gradient: float32 [512, 512], replicated
- neighbour_gradient: float32 [512, 512], replicated
Inputs may be any that keep to these rules, and one draw needn't show every extreme that they name: The first tile_count[p] slots of device p are live, the rest are unused; some device has all 64 slots live. `tile_source`: slot k of every device takes its source from the next region when k % 4 == 0, the previous region when k % 4 == 1, the own region when k % 4 == 2, and a hub block when k % 4 == 3.
All inputs are finite; a program needn't handle non-finite values.
Results may differ from a plain program's by a relative error of at most 0.0075.
Values may be sent and summed in bfloat16 or wider, within the bound.
No kernel may reach another device: no remote copies, remote signals or barrier semaphores. Data moves between devices by JAX's collectives and lax.ppermute only.
A program may use at most 128 MiB of HBM per device.

v0:
```python
import jax
import jax.numpy as jnp
from jax import lax
from jax.sharding import PartitionSpec as P


def padded(cells, sides, width):
    for axis, dim in sides:
        count = lax.axis_size(axis)
        ends = count - 1
        head = lax.slice_in_dim(cells, 0, width, axis=dim)
        tail = lax.slice_in_dim(cells, cells.shape[dim] - width, cells.shape[dim], axis=dim)
        cells = jnp.concatenate(
            [
                lax.ppermute(tail, axis, [(i, (i + 1) % count) for i in range(ends)]),
                cells,
                lax.ppermute(head, axis, [((i + 1) % count, i) for i in range(ends)]),
            ],
            axis=dim,
        )
    return cells


def shifted(value, axis, by):
    peers = lax.axis_size(axis)
    pairs = [(i, i + by) for i in range(peers) if 0 <= i + by < peers]
    return lax.ppermute(value, axis, pairs)


def silu_slope(pre_act):
    sigmoid_value = jax.nn.sigmoid(pre_act)
    return sigmoid_value * (1.0 + pre_act * (1.0 - sigmoid_value))


def local(
    features,
    hub_features,
    hub_order,
    tile_values,
    tile_dest,
    tile_source,
    tile_count,
    self_weight,
    neighbour_weight,
    cotangent,
):
    local_rows, feat_width = features.shape
    block_count = local_rows // 128
    hub_rows = hub_features.shape[0]
    region = lax.all_gather(features, "sub", axis=0, tiled=True)
    window = padded(region, (("curve", 0),), 2 * local_rows)
    all_hubs = lax.all_gather(hub_features, ("curve", "sub"), axis=0, tiled=True)
    hub_table = all_hubs[hub_order]
    table = jnp.concatenate([window, hub_table], 0).reshape(-1, 128, feat_width)
    table_blocks = table.shape[0]
    window_blocks = 6 * block_count
    dest_ids = tile_dest[0]
    source_ids = tile_source[0]
    live_count = tile_count[0]
    slot_count = dest_ids.shape[0]
    live_mask = (jnp.arange(slot_count, dtype=jnp.int32) < live_count).astype(jnp.float32)
    dest_onehot = (jnp.arange(block_count, dtype=jnp.int32)[:, None] == dest_ids[None, :]).astype(
        jnp.float32
    ) * live_mask[None, :]
    source_onehot = (
        jnp.arange(table_blocks, dtype=jnp.int32)[:, None] == source_ids[None, :]
    ).astype(jnp.float32) * live_mask[None, :]
    picked = table[source_ids]
    products = jnp.einsum("kij,kjh->kih", tile_values, picked, preferred_element_type=jnp.float32)
    aggregate = jnp.einsum("bk,kih->bih", dest_onehot, products, precision=lax.Precision.HIGHEST)
    neighbours = aggregate.reshape(local_rows, feat_width).astype(jnp.bfloat16)
    pre_act = jnp.dot(features, self_weight, preferred_element_type=jnp.float32) + jnp.dot(
        neighbours, neighbour_weight, preferred_element_type=jnp.float32
    )
    embedding = jax.nn.silu(pre_act).astype(jnp.bfloat16)
    slope_grad = (cotangent.astype(jnp.float32) * silu_slope(pre_act)).astype(jnp.bfloat16)
    self_part = lax.dot_general(
        features, slope_grad, (((0,), (0,)), ((), ())), preferred_element_type=jnp.float32
    )
    neigh_part = lax.dot_general(
        neighbours, slope_grad, (((0,), (0,)), ((), ())), preferred_element_type=jnp.float32
    )
    self_gradient, neighbour_gradient = lax.psum((self_part, neigh_part), ("curve", "sub"))
    back_neigh = (
        lax.dot_general(
            slope_grad,
            neighbour_weight,
            (((1,), (1,)), ((), ())),
            preferred_element_type=jnp.float32,
        )
        .astype(jnp.bfloat16)
        .reshape(block_count, 128, feat_width)
    )
    self_term = lax.dot_general(
        slope_grad, self_weight, (((1,), (1,)), ((), ())), preferred_element_type=jnp.float32
    )
    back_picked = back_neigh[dest_ids]
    back_products = jnp.einsum(
        "kji,kjh->kih", tile_values, back_picked, preferred_element_type=jnp.float32
    )
    table_grad = jnp.einsum(
        "tk,kih->tih", source_onehot, back_products, precision=lax.Precision.HIGHEST
    )
    window_grad = table_grad[:window_blocks].reshape(3, 2 * local_rows, feat_width)
    region_total = (
        window_grad[1]
        + shifted(window_grad[0].astype(jnp.bfloat16), "curve", -1).astype(jnp.float32)
        + shifted(window_grad[2].astype(jnp.bfloat16), "curve", 1).astype(jnp.float32)
    )
    own_rows = lax.psum_scatter(
        region_total.astype(jnp.bfloat16), "sub", scatter_dimension=0, tiled=True
    ).astype(jnp.float32)
    feature_gradient = own_rows + self_term
    hub_blocks = table_grad[window_blocks:].reshape(-1, feat_width)
    inverse = jnp.argsort(hub_order, stable=True)
    summed = lax.psum(hub_blocks[inverse], ("curve", "sub"))
    hub_gradient = lax.dynamic_slice_in_dim(
        summed, lax.axis_index(("curve", "sub")) * hub_rows, hub_rows, 0
    )
    return (embedding, feature_gradient, hub_gradient, self_gradient, neighbour_gradient)


def solution(mesh):
    in_specs = (
        P(("curve", "sub"), None),
        P(("curve", "sub"), None),
        P(),
        P(("curve", "sub"), None, None),
        P(("curve", "sub"), None),
        P(("curve", "sub"), None),
        P(("curve", "sub")),
        P(),
        P(),
        P(("curve", "sub"), None),
    )
    out_specs = (
        P(("curve", "sub"), None),
        P(("curve", "sub"), None),
        P(("curve", "sub"), None),
        P(),
        P(),
    )
    return jax.shard_map(local, mesh=mesh, in_specs=in_specs, out_specs=out_specs, check_vma=False)
```

profile of v0, /device:TPU:1, one launch (start us, length us, event | category | flops | bytes accessed | tf_op | source)
XLA Modules:
  0.0 1015.1 jit_solution(4014236700535658212)
XLA Ops:
  9.4 5.1 sort.17
  15.1 25.0 %all-gather.4.cloned.1.call-done = bf16[1024,512]{1,0:T(8,128)(2,1)} async-done(((bf16[512,512]{1,0:T(8,128)(2,1)}), bf16[1024,512]{1,0:T(8,128)(2,1)}) %all-gather.4.cloned.1.call-update) | async-done | bytes 1048592 | tf_op jit(solution)/shard_map/all_gather | solution.py:50
  40.1 4.9 collective-permute-start
  45.0 1.9 collective-permute-start.1
  48.3 2.6 fusion.22
  50.9 524.2 %all-gather.6.cloned.1.call-done = bf16[256,4,512]{2,1,0:T(4,128)(2,1)} async-done(((bf16[1,4,512]{2,1,0:T(4,128)(2,1)}), bf16[256,4,512]{2,1,0:T(4,128)(2,1)}) %all-gather.6.cloned.1.call-update) | async-done | bytes 1048592 | tf_op jit(solution)/shard_map/all_gather | solution.py:52
  576.4 5.1 gather_fusion
  581.5 3.7 pad_maximum_fusion
  585.2 7.7 gather_fusion.1
  592.9 11.5 %convolution_bitcast_fusion.1 = f32[64,128,512]{1,2,0:T(8,128)} fusion(bf16[64,128,512]{2,1,0:T(8,128)(2,1)} %gather_fusion.1, bf16[64,128,128]{2,1,0:T(8,128)(2,1)S(1)} %copy-done), kind=kOutput, calls=%fused_computation.5 | convolution fusion | flops 1073741824 | bytes 27262976 | tf_op jit(solution)/shard_map/kij,kjh->kih/dot_general | solution.py:69
  604.4 17.4 %copy.31 = f32[64,128,512]{2,0,1:T(8,128)} copy(f32[64,128,512]{1,2,0:T(8,128)} %convolution_bitcast_fusion.1) | data formatting | bytes 33554432 | tf_op jit(solution)/shard_map/kij,kjh->kih/dot_general | solution.py:69
  621.9 10.8 %convolution_convert_fusion.1 = bf16[4,128,512]{2,0,1:T(4,128)(2,1)S(1)} fusion(f32[64,128,512]{2,0,1:T(8,128)} %copy.31, f32[64]{0:T(128)S(1)} %compare_convert_fusion, s32[64]{0:T(128)S(1)} %bitcast.65), kind=kOutput, calls=%fused_computation.13 | convolution fusion | flops 201589248 | bytes 17302016 | tf_op jit(solution)/shard_map/bk,kih->bih/dot_general | solution.py:70
  632.8 1.6 multiply_convert_fusion
  634.5 1.5 fusion.24
  636.4 1.4 convolution_bitcast_fusion.2
  637.8 5.5 gather_fusion.2
  643.3 11.5 %convolution_bitcast_fusion = f32[64,128,512]{1,2,0:T(8,128)} fusion(bf16[64,128,512]{2,1,0:T(8,128)(2,1)} %gather_fusion.2, bf16[64,128,128]{2,1,0:T(8,128)(2,1)S(1)} %copy-done), kind=kOutput, calls=%fused_computation.4 | convolution fusion | flops 1073741824 | bytes 27262976 | tf_op jit(solution)/shard_map/kji,kjh->kih/dot_general | solution.py:98
  654.8 17.4 %copy.34 = f32[64,128,512]{2,0,1:T(8,128)} copy(f32[64,128,512]{1,2,0:T(8,128)} %convolution_bitcast_fusion) | data formatting | bytes 33554432 | tf_op jit(solution)/shard_map/kji,kjh->kih/dot_general | solution.py:98
  672.3 13.0 %fusion.21 = (bf16[32,128,512]{2,0,1:T(8,128)(2,1)}, f32[32,128,512]{2,0,1:T(8,128)S(1)}) fusion(f32[64,128,512]{2,0,1:T(8,128)} %copy.34, f32[64]{0:T(128)S(1)} %compare_convert_fusion, s32[64]{0:T(128)S(1)} %bitcast.66), kind=kOutput, calls=%fused_computation.47 | convolution fusion | flops 1612713984 | bytes 29360640 | tf_op jit(solution)/shard_map/tk,kih->tih/dot_general | solution.py:101
  685.3 1.8 fusion.19
  688.3 4.9 gather_fusion.3
  693.3 1.8 fusion.20
  695.5 2.2 collective-permute-start.2
  698.1 4.8 collective-permute-start.3
  704.1 10.1 collective-permute-done.2
  714.2 8.1 collective-permute-done.3
  723.8 1.4 fusion.23
  725.3 250.0 %all-reduce.3.cloned.1.call-done = (f32[1024,512]{1,0:T(8,128)}, f32[512,512]{0,1:T(8,128)}, f32[512,512]{1,0:T(8,128)}) async-done(((f32[1024,512]{1,0:T(8,128)}, f32[512,512]{0,1:T(8,128)}, f32[512,512]{1,0:T(8,128)}), (f32[1024,512]{1,0:T(8,128)}, f32[512,512]{0,1:T(8,128)}, f32[512,512]{1,0:T(8,128)})) %all-reduce.3.cloned.1.call-update) | async-done | bytes 4194320 | tf_op jit(solution)/shard_map/psum | solution.py:116
  975.2 2.5 copy.39
  979.1 24.8 %reduce-scatter.2.cloned.1.call-done = bf16[512,512]{1,0:T(8,128)(2,1)} async-done(((bf16[1024,512]{1,0:T(8,128)(2,1)}), bf16[512,512]{1,0:T(8,128)(2,1)}) %reduce-scatter.2.cloned.1.call-update) | async-done | bytes 524304 | tf_op jit(solution)/shard_map/reduce_scatter | solution.py:110
  1003.8 2.5 convert_add_fusion
  1006.3 2.3 copy.46
  (47 shorter events, 11.4 us)
Async XLA Ops:
  7.2 585.7 %copy-start = (bf16[64,128,128]{2,1,0:T(8,128)(2,1)S(1)}, bf16[64,128,128]{2,1,0:T(8,128)(2,1)}, u32[]{:S(2)}) copy-start(bf16[64,128,128]{2,1,0:T(8,128)(2,1)} %param.13) | copy-start | bytes 6291460
  7.2 32.9 %all-gather.4.cloned.1.call-start = ((), (), s32[]{:S(2)}) async-start(), calls=%async_computation.1 | async-start | bytes 1572864 | tf_op jit(solution)/shard_map/all_gather | solution.py:50
  7.9 567.2 %all-gather.6.cloned.1.call-start = ((), (), s32[]{:S(2)}) async-start(), calls=%async_computation.3 | async-start | bytes 1052672 | tf_op jit(solution)/shard_map/all_gather | solution.py:52
  8.7 966.6 %all-reduce.3.cloned.1.call-start = ((), (), s32[]{:S(2)}) async-start(), calls=%async_computation.4 | async-start | bytes 8388608 | tf_op jit(solution)/shard_map/psum | solution.py:116
  40.1 541.5 %collective-permute-start = (bf16[1024,512]{1,0:T(8,128)(2,1)}, bf16[1024,512]{1,0:T(8,128)(2,1)}, u32[]{:S(2)}, u32[]{:S(2)}) collective-permute-start(bf16[1024,512]{1,0:T(8,128)(2,1)} %all-gather.4.cloned.1.call-done), channel_id=1, source_target_pairs={{0,2},{2,4},{4,6},{6,8},{8,10},{10,12},{12,14},{14,16},{16,18},{18... | collective-permute-start | bytes 3145736 | tf_op jit(solution)/shard_map/ppermute | solution.py:15
  45.0 536.6 %collective-permute-start.1 = (bf16[1024,512]{1,0:T(8,128)(2,1)}, bf16[1024,512]{1,0:T(8,128)(2,1)}, u32[]{:S(2)}, u32[]{:S(2)}) collective-permute-start(bf16[1024,512]{1,0:T(8,128)(2,1)} %all-gather.4.cloned.1.call-done), channel_id=1, source_target_pairs={{2,0},{4,2},{6,4},{8,6},{10,8},{12,10},{14,12},{16,14},{18,16},{20... | collective-permute-start | bytes 3145736 | tf_op jit(solution)/shard_map/ppermute | solution.py:17
  604.4 17.4 %copy-start.7 = (s32[1,64]{1,0:T(1,128)S(1)}, s32[1,64]{1,0:T(1,128)}, u32[]{:S(2)}) copy-start(s32[1,64]{1,0:T(1,128)} %param.14) | copy-start | bytes 772
  621.9 10.9 %copy-start.5 = (f32[512,512]{1,0:T(8,128)S(1)}, f32[512,512]{1,0:T(8,128)}, u32[]{:S(2)}) copy-start(f32[512,512]{1,0:T(8,128)} %fusion.22) | copy-start | bytes 3145732
  621.9 10.9 %copy-start.6 = (bf16[512,512]{1,0:T(8,128)(2,1)S(1)}, bf16[512,512]{1,0:T(8,128)(2,1)}, u32[]{:S(2)}) copy-start(bf16[512,512]{1,0:T(8,128)(2,1)} %param.18) | copy-start | bytes 1572868
  621.9 11.0 %copy-start.9 = (bf16[512,512]{1,0:T(8,128)(2,1)S(1)}, bf16[512,512]{1,0:T(8,128)(2,1)}, u32[]{:S(2)}) copy-start(bf16[512,512]{1,0:T(8,128)(2,1)} %param.19) | copy-start | bytes 1572868
  632.7 3.7 copy-start.3
  654.8 17.4 %copy-start.8 = (s32[1,64]{1,0:T(1,128)S(1)}, s32[1,64]{1,0:T(1,128)}, u32[]{:S(2)}) copy-start(s32[1,64]{1,0:T(1,128)} %param.15) | copy-start | bytes 772
  693.3 310.6 %reduce-scatter.2.cloned.1.call-start = ((), (), s32[]{:S(2)}) async-start(), calls=%async_computation.2 | async-start | bytes 1572864 | tf_op jit(solution)/shard_map/reduce_scatter | solution.py:110
  693.3 9.6 copy-start.2
  695.2 28.6 %copy-start.4 = (bf16[512,512]{1,0:T(8,128)(2,1)S(1)}, bf16[512,512]{1,0:T(8,128)(2,1)}, u32[]{:S(2)}) copy-start(bf16[512,512]{1,0:T(8,128)(2,1)} %param.17) | copy-start | bytes 1572868
  695.5 18.7 %collective-permute-start.2 = (bf16[1024,512]{1,0:T(8,128)(2,1)S(1)}, bf16[1024,512]{1,0:T(8,128)(2,1)S(1)}, u32[]{:S(2)}, u32[]{:S(2)}) collective-permute-start(bf16[1024,512]{1,0:T(8,128)(2,1)S(1)} %bitcast.62), channel_id=1, source_target_pairs={{2,0},{4,2},{6,4},{8,6},{10,8},{12,10},{14,12},{16,14},{18,16},{20... | collective-permute-start | bytes 3145736 | tf_op jit(solution)/shard_map/ppermute | solution.py:27
  698.1 24.3 %collective-permute-start.3 = (bf16[1024,512]{1,0:T(8,128)(2,1)S(1)}, bf16[1024,512]{1,0:T(8,128)(2,1)S(1)}, u32[]{:S(2)}, u32[]{:S(2)}) collective-permute-start(bf16[1024,512]{1,0:T(8,128)(2,1)S(1)} %bitcast.63), channel_id=1, source_target_pairs={{0,2},{2,4},{4,6},{6,8},{8,10},{10,12},{12,14},{14,16},{16,18},{18... | collective-permute-start | bytes 3145736 | tf_op jit(solution)/shard_map/ppermute | solution.py:27
  702.9 305.7 %copy-start.1 = (bf16[64,128,128]{2,1,0:T(8,128)(2,1)S(1)}, bf16[64,128,128]{2,1,0:T(8,128)(2,1)}, u32[]{:S(2)}) copy-start(bf16[64,128,128]{2,1,0:T(8,128)(2,1)} %param.13) | copy-start | bytes 6291460
Sparse Core Ops, SparseCore 0:
  9.8 30.1 all-gather.3
  41.9 533.1 all-gather.5
  693.4 281.8 all-reduce.2
  978.3 25.4 reduce-scatter.1
where the time goes:
time: 1020 us
  waiting for transfers between devices  844 us (83%)
  local copies, waits for them, and re-layouts  72.3 us (7%)
  matrix products  55.9 us (5%)
  other arithmetic  14.7 us (1%)
  between operations  14.6 us (1%)
  starting transfers between devices  14 us (1%)
    all_gather x1, waiting for transfers between devices, local(): lax.all_gather(hub_features, ('curve', 'sub'), axis=0, tiled=True)  524 us
    psum x1, waiting for transfers between devices, local(): summed = lax.psum(hub_blocks[inverse], ('curve', 'sub'))  250 us
    all_gather x1, waiting for transfers between devices, local(): region = lax.all_gather(features, 'sub', axis=0, tiled=True)  25 us
    reduce_scatter x1, waiting for transfers between devices, local(): lax.psum_scatter(region_total.astype(jnp.bfloat16), 'sub', scatter_dimens...  24.8 us
  transfers between devices with their start and end apart: 8, of which 6 were waited for; matrix products, arithmetic and copies ran while one was open for 3% of the time, Pallas kernels for 0%

commit v1 on v0

v1 whole, which is shorter than its diff:
```python
import functools

import jax
import jax.numpy as jnp
from jax import lax
from jax.experimental import pallas as pl
from jax.experimental.pallas import tpu as pltpu
from jax.sharding import Mesh
from jax.sharding import PartitionSpec as P

BF = jnp.bfloat16
F32 = jnp.float32
BLK = 128
AXES = ("x", "z", "yh", "core", "yl")
EXTENT = (4, 8, 2, 2, 2)
WIDE = ("z", "yh", "yl")
NEAR = ("x", "core")
N_WIDE, N_NEAR = 32, 8
REGIONS = 128


def to_region(value, by, flip):
    pairs = [
        (2 * c + s, 2 * (c + by) + (s ^ flip))
        for c in range(REGIONS)
        if 0 <= c + by < REGIONS
        for s in range(2)
    ]
    return lax.ppermute(value, AXES, pairs)


OTHERS = ((-1, 0), (-1, 1), (0, 1), (1, 0), (1, 1))


def spread(value, axes, count):
    copies = jnp.broadcast_to(value[None], (count,) + value.shape)
    return lax.all_to_all(copies, axes, 0, 0, tiled=True).reshape(-1, value.shape[-1])


def collect(value, axes):
    return lax.all_to_all(value, axes, 0, 0, tiled=True).astype(F32).sum(0)


def hub_of(position):
    low = position & 7
    core = (position >> 7) & 1
    mid = (position >> 3) & 15
    high = position >> 8
    return low | (core << 3) | (mid << 4) | (high << 8)


def dot(a, b, ca=1, cb=0):
    return lax.dot_general(a, b, (((ca,), (cb,)), ((), ())), preferred_element_type=F32)


def kernel(
    dest, source, count, side,
    features, prev_same, prev_other, own_other, next_same, next_other,
    hubs, order_col, order_row, tiles, self_weight, neigh_weight, cotangent,
    embedding, own_grad, g_prev_same, g_prev_other, g_own_other, g_next_same, g_next_other, reduced,
    table, sums, grads, neigh, slope, back, hub_grads, sems,
):
    live = count[0]
    flip = 4 * side[0]
    copies = []
    for n, (ref, cat, half) in enumerate((
        (next_same, 0, 0), (next_other, 0, 1), (prev_same, 1, 0),
        (prev_other, 1, 1), (features, 2, 0), (own_other, 2, 1),
    )):
        copy = pltpu.make_async_copy(ref, table.at[cat, pl.ds(half * 4 * BLK, 4 * BLK)], sems.at[n])
        copy.start()
        copies.append(copy)
    ids = hub_of(lax.broadcasted_iota(jnp.int32, (BLK, 1024), 1))
    for j in range(8):
        rows = pl.ds(j * BLK, BLK)
        pick = (order_col[rows, :] == ids).astype(F32).astype(BF)
        table[3, rows, :] = dot(pick, hubs[...]).astype(BF)
    sums[...] = jnp.zeros_like(sums)
    grads[...] = jnp.zeros_like(grads)
    for copy in copies:
        copy.wait()

    low = (16, 0, 8, 24)

    def slot(m, cat):
        k = 4 * m + cat
        block = source[0, k] - low[cat]
        if cat < 3:
            block = block ^ flip
        mask = jnp.where(k < live, 1.0, 0.0).astype(BF)
        return k, dest[0, k], pl.ds(pl.multiple_of(block * BLK, BLK), BLK), mask

    def forward(m, carry):
        for cat in range(4):
            k, d, rows, mask = slot(m, cat)
            sums[cat, d] += dot(tiles[k] * mask, table[cat, rows, :])
        return carry

    chunks = (live + 3) // 4
    lax.fori_loop(0, chunks, forward, 0)

    for b in range(4):
        rows = pl.ds(b * BLK, BLK)
        near = (sums[0, b] + sums[1, b] + sums[2, b] + sums[3, b]).astype(BF)
        neigh[rows, :] = near
        pre = dot(table[2, rows, :], self_weight[...]) + dot(near, neigh_weight[...])
        sig = jax.nn.sigmoid(pre)
        embedding[rows, :] = (pre * sig).astype(BF)
        grad = (cotangent[rows, :].astype(F32) * (sig * (1.0 + pre * (1.0 - sig)))).astype(BF)
        slope[rows, :] = grad
        back[rows, :] = dot(grad, neigh_weight[...], 1, 1).astype(BF)
        own_grad[rows, :] = dot(grad, self_weight[...], 1, 1)
    for i in range(4):
        columns = pl.ds(i * BLK, BLK)
        reduced[i, pl.ds(BLK, BLK), :] = dot(table[2, pl.ds(0, 4 * BLK), columns], slope[...], 0, 0).astype(BF)
        reduced[4 + i, pl.ds(BLK, BLK), :] = dot(neigh[:, columns], slope[...], 0, 0).astype(BF)

    def backward(m, carry):
        for cat in range(4):
            k, d, rows, mask = slot(m, cat)
            there = pl.ds(pl.multiple_of(d * BLK, BLK), BLK)
            grads[cat, rows, :] += dot(tiles[k] * mask, back[there, :], 0, 0)
        return carry

    lax.fori_loop(0, chunks, backward, 0)
    half, rest = pl.ds(0, 4 * BLK), pl.ds(4 * BLK, 4 * BLK)
    g_next_same[...] = grads[0, half, :].astype(BF)
    g_next_other[...] = grads[0, rest, :].astype(BF)
    g_prev_same[...] = grads[1, half, :].astype(BF)
    g_prev_other[...] = grads[1, rest, :].astype(BF)
    g_own_other[...] = grads[2, rest, :].astype(BF)
    own_grad[...] += grads[2, half, :]
    hub_grads[...] = grads[3].astype(BF)
    for i in range(8):
        ids = hub_of(lax.broadcasted_iota(jnp.int32, (BLK, 1024), 0) + i * BLK)
        place = (ids == order_row[...]).astype(F32).astype(BF)
        reduced[i, pl.ds(0, BLK), :] = dot(place, hub_grads[...]).astype(BF)


def local(
    features,
    hub_features,
    hub_order,
    tile_values,
    tile_dest,
    tile_source,
    tile_count,
    self_weight,
    neighbour_weight,
    cotangent,
):
    rows, width = features.shape
    window = {o: to_region(features, -o[0], o[1]) for o in OTHERS}
    hubs = spread(spread(hub_features, WIDE, N_WIDE), NEAR, N_NEAR)
    side = lax.axis_index("yl").astype(jnp.int32).reshape(1)
    smem = pl.BlockSpec(memory_space=pltpu.SMEM)
    vmem = pl.BlockSpec(memory_space=pltpu.VMEM)
    hbm = pl.BlockSpec(memory_space=pl.ANY)
    shape = jax.ShapeDtypeStruct
    wide = shape((rows, width), BF)
    outs = pl.pallas_call(
        kernel,
        in_specs=[smem] * 4 + [hbm] * 6 + [vmem] * 7,
        out_specs=[vmem] * 8,
        out_shape=[wide, shape((rows, width), F32)] + [wide] * 5 + [shape((N_NEAR, 2 * BLK, width), BF)],
        scratch_shapes=[
            pltpu.VMEM((4, 8 * BLK, width), BF),
            pltpu.VMEM((4, 4, BLK, width), F32),
            pltpu.VMEM((4, 8 * BLK, width), F32),
            pltpu.VMEM((rows, width), BF),
            pltpu.VMEM((rows, width), BF),
            pltpu.VMEM((rows, width), BF),
            pltpu.VMEM((8 * BLK, width), BF),
            pltpu.SemaphoreType.DMA((6,)),
        ],
        compiler_params=pltpu.CompilerParams(vmem_limit_bytes=52 * 1024 * 1024),
        cost_estimate=pl.CostEstimate(flops=4 * 10**9, bytes_accessed=14 * 10**6, transcendentals=0),
    )(
        tile_dest, tile_source, tile_count, side,
        features, *(window[o] for o in OTHERS),
        hubs, hub_order.reshape(-1, 1), hub_order.reshape(1, -1), tile_values,
        self_weight, neighbour_weight, cotangent,
    )
    embedding, own_grad, sent, reduced = outs[0], outs[1], outs[2:7], outs[7]
    back = [to_region(g, o[0], o[1]) for g, o in zip(sent, OTHERS)]
    part = collect(reduced, NEAR).astype(BF)
    hub_part, weight_part = part[:BLK], part[BLK:]
    part = jnp.concatenate([hub_part.reshape(N_WIDE, 4, width), weight_part.reshape(N_WIDE, 4, width)], 1)
    part = collect(part, WIDE)
    hub_gradient = part[:4]
    weights = spread(spread(part[4:].astype(BF), WIDE, N_WIDE), NEAR, N_NEAR).astype(F32)
    feature_gradient = own_grad
    for g in back:
        feature_gradient = feature_gradient + g.astype(F32)
    return embedding, feature_gradient, hub_gradient, weights[:width], weights[width:]


def solution(mesh):
    fine = Mesh(mesh.devices.reshape(EXTENT), AXES)
    split = P(AXES)
    in_specs = (split, split, P(), split, split, split, split, P(), P(), split)
    out_specs = (split, split, split, P(), P())
    return jax.shard_map(local, mesh=fine, in_specs=in_specs, out_specs=out_specs, check_vma=False)
```

time: 1020 us -> 205 us (0.20)
  waiting for transfers between devices: 844 us -> 46.7 us
  blocking collectives: 0 us -> 92.5 us
  local copies, waits for them, and re-layouts: 72.3 us -> 7.34 us
  matrix products: 55.9 us -> 0 us
  starting transfers between devices: 14 us -> 37.8 us
  between operations: 14.6 us -> 1.47 us
  Pallas kernels: 0 us -> 12.3 us
    all_gather x2 -> x0, waiting for transfers between devices: 549 us -> none  [the longest x1 524 us: local(): lax.all_gather(hub_features, ('curve', 'sub'), axis=0, tiled=True)]
    psum x1 -> x0, waiting for transfers between devices: 250 us -> none  [local(): summed = lax.psum(hub_blocks[inverse], ('curve', 'sub'))]
    all_to_all x0 -> x4, blocking collectives: none -> 92.5 us  [the longest x2 56.6 us: collect(): return lax.all_to_all(value, axes, 0, 0, tiled=True).astype(F32).sum(0)]
    dot_general x10 -> x0, matrix products: 55.9 us -> none  [the longest x1 13 us: local(): jnp.einsum('tk,kih->tih', source_onehot, back_products, precision=lax.Pre...]
    dot_general x2 -> x0, local copies, waits for them, and re-layouts: 34.9 us -> none  [the longest x1 17.4 us: local(): jnp.einsum('kij,kjh->kih', tile_values, picked, preferred_element_type=jn...]
    ppermute x4 -> x10, waiting for transfers between devices: 18.2 us -> 46.7 us  [to_region(): return lax.ppermute(value, AXES, pairs)]
    reduce_scatter x1 -> x0, waiting for transfers between devices: 24.8 us -> none  [local(): lax.psum_scatter(region_total.astype(jnp.bfloat16), 'sub', scatter_dimens...]
    gather x4 -> x0, local copies, waits for them, and re-layouts: 23.1 us -> none  [the longest x1 7.68 us: local(): picked = table[source_ids]]
  transfers between devices with their start and end apart: 8 -> 12, of which waited for: 6 -> 8; matrix products, arithmetic and copies ran while one was open for 3% -> 2% of each run, Pallas kernels for 0% -> 0%
where the time goes in v1:
time: 205 us; the launch traced here: 203 us
  blocking collectives  92.5 us (45%)
  waiting for transfers between devices  46.7 us (23%)
  starting transfers between devices  37.8 us (18%)
  Pallas kernels  12.3 us (6%)
  local copies, waits for them, and re-layouts  7.34 us (4%)
  other arithmetic  4.8 us (2%)
    all_to_all x2, blocking collectives, collect(): return lax.all_to_all(value, axes, 0, 0, tiled=True).astype(F32).sum(0)  56.6 us
    ppermute x10, waiting for transfers between devices, to_region(): return lax.ppermute(value, AXES, pairs)  46.7 us
    all_to_all x2, blocking collectives, spread(): lax.all_to_all(copies, axes, 0, 0, tiled=True).reshape(-1, value.shape[-1])  35.8 us
    ppermute x10, starting transfers between devices, to_region(): return lax.ppermute(value, AXES, pairs)  24.8 us
    all_to_all x2, starting transfers between devices, spread(): lax.all_to_all(copies, axes, 0, 0, tiled=True).reshape(-1, value.shape[-1])  13 us
    pallas_call x1, Pallas kernels, local(): pl.pallas_call(kernel, in_specs=[smem] * 4 + [hbm] * 6 + [vmem] * 7, out_...  12.3 us
  transfers between devices with their start and end apart: 12, of which 8 were waited for; matrix products, arithmetic and copies ran while one was open for 2% of the time, Pallas kernels for 0%

profile of v1, /device:TPU:1, one launch (start us, length us, event | category | flops | bytes accessed | tf_op | source)
XLA Modules:
  0.0 202.9 jit_solution(4727740350751474760)
XLA Ops:
  0.7 0.8 broadcast_in_dim.12
  1.4 21.2 %all_to_all.30 = bf16[32,4,512]{2,1,0:T(4,128)(2,1)S(1)} all-to-all(bf16[32,4,512]{2,1,0:T(4,128)(2,1)S(1)} %broadcast_in_dim.12), channel_id=1, replica_groups=mesh['x'=4,'z'=8,'yh'=2,'core'=2,'yl'=2] {'z','yh','yl'}, dimensions={0} | all-to-all | bytes 262144 | tf_op jit(solution)/shard_map/all_to_all | solution.py:37
  22.7 1.1 broadcast_in_dim.28
  23.7 6.4 %all-to-all-start.1 = ((bf16[8,128,512]{2,1,0:T(8,128)(2,1)}), bf16[8,128,512]{2,1,0:T(8,128)(2,1)S(1)}, u32[]{:S(2)}, u32[]{:S(2)}) async-start(bf16[8,128,512]{2,1,0:T(8,128)(2,1)} %broadcast_in_dim.28), calls=%async_computation.1 | async-start | bytes 2097152 | tf_op jit(solution)/shard_map/all_to_all | solution.py:37
  30.1 1.9 collective-permute-start.3
  32.1 5.7 %collective-permute-start.1 = (bf16[512,512]{1,0:T(8,128)(2,1)S(1)}, bf16[512,512]{1,0:T(8,128)(2,1)S(1)}, u32[]{:S(2)}, u32[]{:S(2)}) collective-permute-start(bf16[512,512]{1,0:T(8,128)(2,1)S(1)} %copy-done.4), channel_id=1, source_target_pairs={{0,3},{1,2},{2,5},{3,4},{4,7},{5,6},{6,9},{7,8},{8,11},{9,10},{10,... | collective-permute-start | bytes 1572872 | tf_op jit(solution)/shard_map/ppermute | solution.py:29
  37.8 2.2 %collective-permute-start = (bf16[512,512]{1,0:T(8,128)(2,1)S(1)}, bf16[512,512]{1,0:T(8,128)(2,1)}, u32[]{:S(2)}, u32[]{:S(2)}) collective-permute-start(bf16[512,512]{1,0:T(8,128)(2,1)S(1)} %copy-done.4), channel_id=1, source_target_pairs={{0,2},{1,3},{2,4},{3,5},{4,6},{5,7},{6,8},{7,9},{8,10},{9,11},{10,... | collective-permute-start | bytes 1572872 | tf_op jit(solution)/shard_map/ppermute | solution.py:29
  40.0 2.8 %collective-permute-start.4 = (bf16[512,512]{1,0:T(8,128)(2,1)S(1)}, bf16[512,512]{1,0:T(8,128)(2,1)}, u32[]{:S(2)}, u32[]{:S(2)}) collective-permute-start(bf16[512,512]{1,0:T(8,128)(2,1)S(1)} %copy-done.4), channel_id=1, source_target_pairs={{2,1},{3,0},{4,3},{5,2},{6,5},{7,4},{8,7},{9,6},{10,9},{11,8},{12,... | collective-permute-start | bytes 1572872 | tf_op jit(solution)/shard_map/ppermute | solution.py:29
  43.4 1.0 copy.16.order_col
  44.4 2.6 %collective-permute-done.3.next_same = bf16[512,512]{1,0:T(8,128)(2,1)S(1)} collective-permute-done((bf16[512,512]{1,0:T(8,128)(2,1)S(1)}, bf16[512,512]{1,0:T(8,128)(2,1)S(1)}, u32[]{:S(2)}, u32[]{:S(2)}) %collective-permute-start.3) | collective-permute-done | bytes 524320 | tf_op jit(solution)/shard_map/ppermute | solution.py:29
  47.0 4.3 %collective-permute-done.2.own_other = bf16[512,512]{1,0:T(8,128)(2,1)S(1)} collective-permute-done((bf16[512,512]{1,0:T(8,128)(2,1)S(1)}, bf16[512,512]{1,0:T(8,128)(2,1)S(1)}, u32[]{:S(2)}, u32[]{:S(2)}) %collective-permute-start.2) | collective-permute-done | bytes 524320 | tf_op jit(solution)/shard_map/ppermute | solution.py:29
  51.4 10.9 %collective-permute-done.1.prev_other = bf16[512,512]{1,0:T(8,128)(2,1)S(1)} collective-permute-done((bf16[512,512]{1,0:T(8,128)(2,1)S(1)}, bf16[512,512]{1,0:T(8,128)(2,1)S(1)}, u32[]{:S(2)}, u32[]{:S(2)}) %collective-permute-start.1) | collective-permute-done | bytes 524320 | tf_op jit(solution)/shard_map/ppermute | solution.py:29
  62.3 3.8 %collective-permute-done.4.next_other = bf16[512,512]{1,0:T(8,128)(2,1)} collective-permute-done((bf16[512,512]{1,0:T(8,128)(2,1)S(1)}, bf16[512,512]{1,0:T(8,128)(2,1)}, u32[]{:S(2)}, u32[]{:S(2)}) %collective-permute-start.4) | collective-permute-done | bytes 524320 | tf_op jit(solution)/shard_map/ppermute | solution.py:29
  66.1 1.0 copy-done.3
  67.0 12.3 %shard_map.137 = (bf16[512,512]{1,0:T(8,128)(2,1)}, f32[512,512]{1,0:T(8,128)}, bf16[512,512]{1,0:T(8,128)(2,1)S(1)}, bf16[512,512]{1,0:T(8,128)(2,1)S(1)}, bf16...) custom-call(s32[1,64]{1,0:T(1,128)S(1)} %copy-done.1, ...), custom_call_target="tpu_custom_call" | custom-call | flops 4000000000 | bytes 14000000 | tf_op jit(solution)/shard_map/pallas_call | solution.py:161
  79.3 42.3 %all_to_all.31 = bf16[8,256,512]{2,1,0:T(8,128)(2,1)} all-to-all(bf16[8,256,512]{2,1,0:T(8,128)(2,1)} %get-tuple-element.20), channel_id=1, replica_groups=mesh['x'=4,'z'=8,'yh'=2,'core'=2,'yl'=2] {'x','core'}, dimensions={0} | all-to-all | bytes 4194304 | tf_op jit(solution)/shard_map/all_to_all | solution.py:41
  121.6 2.0 reduce_sum.21
  123.8 14.4 %all_to_all.32 = bf16[32,8,512]{2,1,0:T(8,128)(2,1)S(1)} all-to-all(bf16[32,8,512]{2,1,0:T(8,128)(2,1)S(1)} %pad_maximum_fusion), channel_id=1, replica_groups=mesh['x'=4,'z'=8,'yh'=2,'core'=2,'yl'=2] {'z','yh','yl'}, dimensions={0} | all-to-all | bytes 524288 | tf_op jit(solution)/shard_map/all_to_all | solution.py:41
  138.3 14.7 %all_to_all.33 = bf16[32,4,512]{2,1,0:T(4,128)(2,1)S(1)} all-to-all(bf16[32,4,512]{2,1,0:T(4,128)(2,1)S(1)} %broadcast_in_dim.29), channel_id=1, replica_groups=mesh['x'=4,'z'=8,'yh'=2,'core'=2,'yl'=2] {'z','yh','yl'}, dimensions={0} | all-to-all | bytes 262144 | tf_op jit(solution)/shard_map/all_to_all | solution.py:37
  153.0 1.1 broadcast_in_dim.31
  154.0 6.6 %all-to-all-start.5 = ((bf16[8,128,512]{2,1,0:T(8,128)(2,1)}), bf16[8,128,512]{2,1,0:T(8,128)(2,1)S(1)}, u32[]{:S(2)}, u32[]{:S(2)}) async-start(bf16[8,128,512]{2,1,0:T(8,128)(2,1)} %broadcast_in_dim.31), calls=%async_computation.5 | async-start | bytes 2097152 | tf_op jit(solution)/shard_map/all_to_all | solution.py:37
  160.7 2.0 collective-permute-start.5
  162.7 1.9 collective-permute-start.6
  164.6 0.8 collective-permute-start.7
  165.4 5.6 %collective-permute-start.8 = (bf16[512,512]{1,0:T(8,128)(2,1)}, bf16[512,512]{1,0:T(8,128)(2,1)S(1)}, u32[]{:S(2)}, u32[]{:S(2)}) collective-permute-start(bf16[512,512]{1,0:T(8,128)(2,1)} %get-tuple-element.18), channel_id=1, source_target_pairs={{0,2},{1,3},{2,4},{3,5},{4,6},{5,7},{6,8},{7,9},{8,10},{9,11},{10,... | collective-permute-start | bytes 1572872 | tf_op jit(solution)/shard_map/ppermute | solution.py:29
  171.0 1.9 collective-permute-start.9
  172.9 3.3 %collective-permute-done.5 = bf16[512,512]{1,0:T(8,128)(2,1)S(1)} collective-permute-done((bf16[512,512]{1,0:T(8,128)(2,1)S(1)}, bf16[512,512]{1,0:T(8,128)(2,1)S(1)}, u32[]{:S(2)}, u32[]{:S(2)}) %collective-permute-start.5) | collective-permute-done | bytes 524320 | tf_op jit(solution)/shard_map/ppermute | solution.py:29
  176.2 5.7 %collective-permute-done.6 = bf16[512,512]{1,0:T(8,128)(2,1)S(1)} collective-permute-done((bf16[512,512]{1,0:T(8,128)(2,1)S(1)}, bf16[512,512]{1,0:T(8,128)(2,1)S(1)}, u32[]{:S(2)}, u32[]{:S(2)}) %collective-permute-start.6) | collective-permute-done | bytes 524320 | tf_op jit(solution)/shard_map/ppermute | solution.py:29
  181.9 12.4 %collective-permute-done.7 = bf16[512,512]{1,0:T(8,128)(2,1)S(1)} collective-permute-done((bf16[512,512]{1,0:T(8,128)(2,1)S(1)}, bf16[512,512]{1,0:T(8,128)(2,1)S(1)}, u32[]{:S(2)}, u32[]{:S(2)}) %collective-permute-start.7) | collective-permute-done | bytes 524320 | tf_op jit(solution)/shard_map/ppermute | solution.py:29
  194.3 3.8 %collective-permute-done.8 = bf16[512,512]{1,0:T(8,128)(2,1)S(1)} collective-permute-done((bf16[512,512]{1,0:T(8,128)(2,1)}, bf16[512,512]{1,0:T(8,128)(2,1)S(1)}, u32[]{:S(2)}, u32[]{:S(2)}) %collective-permute-start.8) | collective-permute-done | bytes 524320 | tf_op jit(solution)/shard_map/ppermute | solution.py:29
  198.0 2.7 %convert_add_fusion = f32[512,512]{1,0:T(8,128)} fusion(bf16[512,512]{1,0:T(8,128)(2,1)S(1)} %collective-permute-done.9, bf16[512,512]{1,0:T(8,128)(2,1)S(1)} %collective-permute-done.8, bf16[512,512]{1,0:T(8,128)(2,1)S(1)} %collective-permute-done.7, bf16[512,512]{1,0:T(8,128)(2,1)S(1)} %collective-permute-done.6, f32[512,512]{1,0:T(8,128)} %get-tuple-element.14, ...), kind=kLoop, calls=%fused_computation | loop fusion | flops 2621440 | bytes 4718592 | tf_op jit(solution)/shard_map/add | solution.py:194
  201.3 1.6 fusion
  (32 shorter events, 1.1 us)
Async XLA Ops:
  0.6 29.4 %copy-start.4 = (bf16[512,512]{1,0:T(8,128)(2,1)S(1)}, bf16[512,512]{1,0:T(8,128)(2,1)}, u32[]{:S(2)}) copy-start(bf16[512,512]{1,0:T(8,128)(2,1)} %features.1) | copy-start | bytes 1572868
  0.6 42.7 %copy-start = (s32[1024]{0:T(1024)S(1)}, s32[1024]{0:T(1024)}, u32[]{:S(2)}) copy-start(s32[1024]{0:T(1024)} %param.12) | copy-start | bytes 12292
  22.6 44.4 %copy-start.1 = (s32[1,64]{1,0:T(1,128)S(1)}, s32[1,64]{1,0:T(1,128)}, u32[]{:S(2)}) copy-start(s32[1,64]{1,0:T(1,128)} %dest.1) | copy-start | bytes 772
  22.6 44.4 %copy-start.2 = (s32[1,64]{1,0:T(1,128)S(1)}, s32[1,64]{1,0:T(1,128)}, u32[]{:S(2)}) copy-start(s32[1,64]{1,0:T(1,128)} %source.1) | copy-start | bytes 772
  23.7 42.4 %all-to-all-start.1 = ((bf16[8,128,512]{2,1,0:T(8,128)(2,1)}), bf16[8,128,512]{2,1,0:T(8,128)(2,1)S(1)}, u32[]{:S(2)}, u32[]{:S(2)}) async-start(bf16[8,128,512]{2,1,0:T(8,128)(2,1)} %broadcast_in_dim.28), calls=%async_computation.1 | async-start | bytes 2097152 | tf_op jit(solution)/shard_map/all_to_all | solution.py:37
  30.1 16.9 %collective-permute-start.3 = (bf16[512,512]{1,0:T(8,128)(2,1)S(1)}, bf16[512,512]{1,0:T(8,128)(2,1)S(1)}, u32[]{:S(2)}, u32[]{:S(2)}) collective-permute-start(bf16[512,512]{1,0:T(8,128)(2,1)S(1)} %copy-done.4), channel_id=1, source_target_pairs={{2,0},{3,1},{4,2},{5,3},{6,4},{7,5},{8,6},{9,7},{10,8},{11,9},{12,... | collective-permute-start | bytes 1572872 | tf_op jit(solution)/shard_map/ppermute | solution.py:29
  32.0 19.4 %collective-permute-start.2 = (bf16[512,512]{1,0:T(8,128)(2,1)S(1)}, bf16[512,512]{1,0:T(8,128)(2,1)S(1)}, u32[]{:S(2)}, u32[]{:S(2)}) collective-permute-start(bf16[512,512]{1,0:T(8,128)(2,1)S(1)} %copy-done.4), channel_id=1, source_target_pairs={{0,1},{1,0},{2,3},{3,2},{4,5},{5,4},{6,7},{7,6},{8,9},{9,8},{10,11... | collective-permute-start | bytes 1572872 | tf_op jit(solution)/shard_map/ppermute | solution.py:29
  32.1 30.2 %collective-permute-start.1 = (bf16[512,512]{1,0:T(8,128)(2,1)S(1)}, bf16[512,512]{1,0:T(8,128)(2,1)S(1)}, u32[]{:S(2)}, u32[]{:S(2)}) collective-permute-start(bf16[512,512]{1,0:T(8,128)(2,1)S(1)} %copy-done.4), channel_id=1, source_target_pairs={{0,3},{1,2},{2,5},{3,4},{4,7},{5,6},{6,9},{7,8},{8,11},{9,10},{10,... | collective-permute-start | bytes 1572872 | tf_op jit(solution)/shard_map/ppermute | solution.py:29
  37.8 24.5 %collective-permute-start = (bf16[512,512]{1,0:T(8,128)(2,1)S(1)}, bf16[512,512]{1,0:T(8,128)(2,1)}, u32[]{:S(2)}, u32[]{:S(2)}) collective-permute-start(bf16[512,512]{1,0:T(8,128)(2,1)S(1)} %copy-done.4), channel_id=1, source_target_pairs={{0,2},{1,3},{2,4},{3,5},{4,6},{5,7},{6,8},{7,9},{8,10},{9,11},{10,... | collective-permute-start | bytes 1572872 | tf_op jit(solution)/shard_map/ppermute | solution.py:29
  40.0 26.1 %collective-permute-start.4 = (bf16[512,512]{1,0:T(8,128)(2,1)S(1)}, bf16[512,512]{1,0:T(8,128)(2,1)}, u32[]{:S(2)}, u32[]{:S(2)}) collective-permute-start(bf16[512,512]{1,0:T(8,128)(2,1)S(1)} %copy-done.4), channel_id=1, source_target_pairs={{2,1},{3,0},{4,3},{5,2},{6,5},{7,4},{8,7},{9,6},{10,9},{11,8},{12,... | collective-permute-start | bytes 1572872 | tf_op jit(solution)/shard_map/ppermute | solution.py:29
  47.0 19.1 %copy-start.6 = (bf16[512,512]{1,0:T(8,128)(2,1)}, bf16[512,512]{1,0:T(8,128)(2,1)S(1)}, u32[]{:S(2)}) copy-start(bf16[512,512]{1,0:T(8,128)(2,1)S(1)} %collective-permute-done.3.next_same) | copy-start | bytes 1572868
  51.4 14.7 %copy-start.7 = (bf16[512,512]{1,0:T(8,128)(2,1)}, bf16[512,512]{1,0:T(8,128)(2,1)S(1)}, u32[]{:S(2)}) copy-start(bf16[512,512]{1,0:T(8,128)(2,1)S(1)} %collective-permute-done.2.own_other) | copy-start | bytes 1572868
  62.3 3.8 %copy-start.8 = (bf16[512,512]{1,0:T(8,128)(2,1)}, bf16[512,512]{1,0:T(8,128)(2,1)S(1)}, u32[]{:S(2)}) copy-start(bf16[512,512]{1,0:T(8,128)(2,1)S(1)} %collective-permute-done.1.prev_other) | copy-start | bytes 1572868
  66.1 1.0 copy-start.3
  138.2 32.8 %copy-start.5 = (bf16[512,512]{1,0:T(8,128)(2,1)S(1)}, bf16[512,512]{1,0:T(8,128)(2,1)}, u32[]{:S(2)}) copy-start(bf16[512,512]{1,0:T(8,128)(2,1)} %get-tuple-element.19) | copy-start | bytes 1572868
  154.0 47.2 %all-to-all-start.5 = ((bf16[8,128,512]{2,1,0:T(8,128)(2,1)}), bf16[8,128,512]{2,1,0:T(8,128)(2,1)S(1)}, u32[]{:S(2)}, u32[]{:S(2)}) async-start(bf16[8,128,512]{2,1,0:T(8,128)(2,1)} %broadcast_in_dim.31), calls=%async_computation.5 | async-start | bytes 2097152 | tf_op jit(solution)/shard_map/all_to_all | solution.py:37
  160.7 15.6 %collective-permute-start.5 = (bf16[512,512]{1,0:T(8,128)(2,1)S(1)}, bf16[512,512]{1,0:T(8,128)(2,1)S(1)}, u32[]{:S(2)}, u32[]{:S(2)}) collective-permute-start(bf16[512,512]{1,0:T(8,128)(2,1)S(1)} %get-tuple-element.15), channel_id=1, source_target_pairs={{2,0},{3,1},{4,2},{5,3},{6,4},{7,5},{8,6},{9,7},{10,8},{11,9},{12,... | collective-permute-start | bytes 1572872 | tf_op jit(solution)/shard_map/ppermute | solution.py:29
  162.7 19.2 %collective-permute-start.6 = (bf16[512,512]{1,0:T(8,128)(2,1)S(1)}, bf16[512,512]{1,0:T(8,128)(2,1)S(1)}, u32[]{:S(2)}, u32[]{:S(2)}) collective-permute-start(bf16[512,512]{1,0:T(8,128)(2,1)S(1)} %get-tuple-element.16), channel_id=1, source_target_pairs={{2,1},{3,0},{4,3},{5,2},{6,5},{7,4},{8,7},{9,6},{10,9},{11,8},{12,... | collective-permute-start | bytes 1572872 | tf_op jit(solution)/shard_map/ppermute | solution.py:29
  164.6 29.7 %collective-permute-start.7 = (bf16[512,512]{1,0:T(8,128)(2,1)S(1)}, bf16[512,512]{1,0:T(8,128)(2,1)S(1)}, u32[]{:S(2)}, u32[]{:S(2)}) collective-permute-start(bf16[512,512]{1,0:T(8,128)(2,1)S(1)} %get-tuple-element.17), channel_id=1, source_target_pairs={{0,1},{1,0},{2,3},{3,2},{4,5},{5,4},{6,7},{7,6},{8,9},{9,8},{10,11... | collective-permute-start | bytes 1572872 | tf_op jit(solution)/shard_map/ppermute | solution.py:29
  165.4 32.6 %collective-permute-start.8 = (bf16[512,512]{1,0:T(8,128)(2,1)}, bf16[512,512]{1,0:T(8,128)(2,1)S(1)}, u32[]{:S(2)}, u32[]{:S(2)}) collective-permute-start(bf16[512,512]{1,0:T(8,128)(2,1)} %get-tuple-element.18), channel_id=1, source_target_pairs={{0,2},{1,3},{2,4},{3,5},{4,6},{5,7},{6,8},{7,9},{8,10},{9,11},{10,... | collective-permute-start | bytes 1572872 | tf_op jit(solution)/shard_map/ppermute | solution.py:29
  171.0 27.0 %collective-permute-start.9 = (bf16[512,512]{1,0:T(8,128)(2,1)S(1)}, bf16[512,512]{1,0:T(8,128)(2,1)S(1)}, u32[]{:S(2)}, u32[]{:S(2)}) collective-permute-start(bf16[512,512]{1,0:T(8,128)(2,1)S(1)} %copy-done.5), channel_id=1, source_target_pairs={{0,3},{1,2},{2,5},{3,4},{4,7},{5,6},{6,9},{7,8},{8,11},{9,10},{10,... | collective-permute-start | bytes 1572872 | tf_op jit(solution)/shard_map/ppermute | solution.py:29

commit v2 on v1

v2 whole, which is shorter than its diff:
```python
import functools

import jax
import jax.numpy as jnp
from jax import lax
from jax.experimental import pallas as pl
from jax.experimental.pallas import tpu as pltpu
from jax.sharding import Mesh
from jax.sharding import PartitionSpec as P

BF = jnp.bfloat16
F32 = jnp.float32
BLK = 128
AXES = ("x", "z", "yh", "core", "yl")
EXTENT = (4, 8, 2, 2, 2)
WIDE = ("z", "yh", "yl")
N_WIDE, N_X = 32, 4
DEVICES = 256


def to_core(value):
    return lax.ppermute(value, AXES, [(d, d ^ 2) for d in range(DEVICES)])


def to_side(value):
    return lax.ppermute(value, AXES, [(d, d ^ 1) for d in range(DEVICES)])


def to_off(value):
    pairs = []
    for d in range(DEVICES):
        region = d // 2
        other = region + (1 if region % 2 else -1)
        if 0 <= other < DEVICES // 2:
            pairs.append((d, 2 * other + (1 - d % 2)))
    return lax.ppermute(value, AXES, pairs)


def spread(value, axes, count):
    copies = jnp.broadcast_to(value[None], (count,) + value.shape)
    return lax.all_to_all(copies, axes, 0, 0, tiled=True).reshape(-1, value.shape[-1])


def to_x(value, flip):
    return lax.ppermute(value, "x", [(x, x ^ flip) for x in range(N_X)])


def collect_x(parts):
    total = parts[0].astype(F32)
    for j in range(1, N_X):
        total = total + to_x(parts[j], j).astype(F32)
    return total.astype(BF)


def hub_of(position):
    low = position & 7
    core = (position >> 7) & 1
    mid = (position >> 3) & 15
    high = position >> 8
    return low | (core << 3) | (mid << 4) | (high << 8)


def dot(a, b, ca=1, cb=0):
    return lax.dot_general(a, b, (((ca,), (cb,)), ((), ())), preferred_element_type=F32)


def prepare(order_col, order_row, core, x_ref, features, self_weight, pick, place, own_pre):
    for r in range(2):
        for x in range(N_X):
            here = pl.ds(x * BLK, BLK)
            ids = hub_of(lax.broadcasted_iota(jnp.int32, (BLK, BLK), 1) + (2 * x + (core[0] ^ r)) * BLK)
            there = (2 * (x_ref[0] ^ x) + (core[0] ^ r)) * BLK
            back = hub_of(lax.broadcasted_iota(jnp.int32, (BLK, BLK), 0) + there)
            for j in range(8):
                rows = pl.ds(j * BLK, BLK)
                pick[r, rows, here] = (order_col[rows, :] == ids).astype(F32).astype(BF)
                place[r, here, rows] = (back == order_row[:, rows]).astype(F32).astype(BF)
    for b in range(4):
        rows = pl.ds(b * BLK, BLK)
        own_pre[rows, :] = dot(features[rows, :], self_weight[...])


LOW = (16, 0, 8, 24)


def slot(dest, source, live, flip, m, cat):
    k = 4 * m + cat
    block = source[0, k] - LOW[cat]
    if cat < 3:
        block = block ^ flip
    mask = jnp.where(k < live, 1.0, 0.0).astype(BF)
    return k, dest[0, k], pl.ds(pl.multiple_of(block * BLK, BLK), BLK), mask


def put(r, j, keep, send, value):
    if r == 0:
        keep[j][...] = value.astype(BF)
    else:
        send[pl.ds(j * BLK, BLK), :] = value.astype(BF)


def ahead(
    dest, source, count, side, core_ref, x_ref,
    features, own_other, on_same, on_other, off_same_low, off_same_high, off_other,
    hubs_hbm, hubs_there_hbm, pick_hbm, own_pre_hbm, tiles_hbm, neigh_weight_hbm, cotangent_hbm,
    embedding, slope, *rest,
):
    keep, send = rest[:N_X], rest[N_X]
    table, sums, left, hubs, hubs_there, pick, own_pre, tiles, neigh_weight, cotangent, sems = rest[N_X + 1:]
    live = count[0]
    flip = 4 * side[0]
    core = core_ref[0]
    def load(n, source_ref, target):
        copy = pltpu.make_async_copy(source_ref, target, sems.at[n])
        copy.start()
        return copy

    first = [
        load(n, *refs)
        for n, refs in enumerate(((hubs_hbm, hubs), (hubs_there_hbm, hubs_there), (pick_hbm, pick)))
    ]
    second = [load(3, tiles_hbm, tiles)]
    for n, (ref, cat, block) in enumerate((
        (on_same, core, 0), (on_other, core, 4), (off_same_low, 1 - core, 0), (off_same_high, 1 - core, 2),
        (off_other, 1 - core, 4), (features, 2, 0), (own_other, 2, 4),
    )):
        second.append(load(4 + n, ref, table.at[cat, pl.ds(block * BLK, ref.shape[0])]))
    third = [
        load(11 + n, *refs)
        for n, refs in enumerate(((own_pre_hbm, own_pre), (neigh_weight_hbm, neigh_weight), (cotangent_hbm, cotangent)))
    ]
    sums[...] = jnp.zeros_like(sums)
    for copy in first:
        copy.wait()
    for j in range(8):
        rows = pl.ds(j * BLK, BLK)
        table[3, rows, :] = (dot(pick[0, rows, :], hubs[...]) + dot(pick[1, rows, :], hubs_there[...])).astype(BF)
    for copy in second:
        copy.wait()

    def forward(m, carry):
        for cat in range(4):
            k, d, rows, mask = slot(dest, source, live, flip, m, cat)
            sums[cat, d] += dot(tiles[k] * mask, table[cat, rows, :])
        return carry

    lax.fori_loop(0, (live + 3) // 4, forward, 0)
    for copy in third:
        copy.wait()

    for b in range(4):
        rows = pl.ds(b * BLK, BLK)
        near = (sums[0, b] + sums[1, b] + sums[2, b] + sums[3, b]).astype(BF)
        left[0, rows, :] = table[2, rows, :]
        left[1, rows, :] = near
        pre = own_pre[rows, :] + dot(near, neigh_weight[...])
        sig = jax.nn.sigmoid(pre)
        embedding[rows, :] = (pre * sig).astype(BF)
        slope[rows, :] = (cotangent[rows, :].astype(F32) * (sig * (1.0 + pre * (1.0 - sig)))).astype(BF)
    for r in range(2):
        for j in range(N_X):
            x = x_ref[0] ^ j
            first = (2 * (x & 1) + (core ^ r)) * BLK
            columns = pl.ds(pl.multiple_of(first, BLK), BLK)
            put(r, j, keep, send, dot(left[x >> 1, :, columns], slope[...], 0, 0))


def behind(
    dest, source, count, side, core_ref,
    slope, place, tiles, self_weight, neigh_weight,
    own_grad, g_own_other, g_on_same, g_on_other, g_off_same, g_off_other, *rest,
):
    keep, send, (grads, back, hub_grads) = rest[:N_X], rest[N_X], rest[N_X + 1:]
    live = count[0]
    flip = 4 * side[0]
    core = core_ref[0]
    grads[...] = jnp.zeros_like(grads)
    for b in range(4):
        rows = pl.ds(b * BLK, BLK)
        back[rows, :] = dot(slope[rows, :], neigh_weight[...], 1, 1).astype(BF)
        own_grad[rows, :] = dot(slope[rows, :], self_weight[...], 1, 1)

    def backward(m, carry):
        for cat in range(4):
            k, d, rows, mask = slot(dest, source, live, flip, m, cat)
            there = pl.ds(pl.multiple_of(d * BLK, BLK), BLK)
            grads[cat, rows, :] += dot(tiles[k] * mask, back[there, :], 0, 0)
        return carry

    lax.fori_loop(0, (live + 3) // 4, backward, 0)
    half, rest = pl.ds(0, 4 * BLK), pl.ds(4 * BLK, 4 * BLK)
    g_on_same[...] = grads[core, half, :].astype(BF)
    g_on_other[...] = grads[core, rest, :].astype(BF)
    g_off_same[...] = grads[1 - core, half, :].astype(BF)
    g_off_other[...] = grads[1 - core, rest, :].astype(BF)
    g_own_other[...] = grads[2, rest, :].astype(BF)
    own_grad[...] += grads[2, half, :]
    hub_grads[...] = grads[3].astype(BF)
    for r in range(2):
        for j in range(N_X):
            put(r, j, keep, send, dot(place[r, pl.ds(j * BLK, BLK), :], hub_grads[...]))


def join_cores(parts):
    theirs = to_core(parts[-1])
    return [plus(mine, theirs[j * BLK:(j + 1) * BLK]) for j, mine in enumerate(parts[:-1])]


def plus(a, b):
    return (a.astype(F32) + b.astype(F32)).astype(BF)


def local(
    features,
    hub_features,
    hub_order,
    tile_values,
    tile_dest,
    tile_source,
    tile_count,
    self_weight,
    neighbour_weight,
    cotangent,
):
    rows, width = features.shape
    smem = pl.BlockSpec(memory_space=pltpu.SMEM)
    vmem = pl.BlockSpec(memory_space=pltpu.VMEM)
    hbm = pl.BlockSpec(memory_space=pl.ANY)
    shape = jax.ShapeDtypeStruct
    wide = shape((rows, width), BF)
    part = shape((BLK, width), BF)
    params = pltpu.CompilerParams(vmem_limit_bytes=56 * 1024 * 1024)
    side = lax.axis_index("yl").astype(jnp.int32).reshape(1)
    core = lax.axis_index("core").astype(jnp.int32).reshape(1)
    x = lax.axis_index("x").astype(jnp.int32).reshape(1)
    where = (tile_dest, tile_source, tile_count, side, core)
    barrier = lax.optimization_barrier

    own_other = to_side(features)
    off_other = to_off(features)
    on_same = to_core(features)
    hubs = spread(hub_features, WIDE, N_WIDE)
    pick, place, own_pre = pl.pallas_call(
        prepare,
        in_specs=[vmem, vmem, smem, smem, vmem, vmem],
        out_specs=[vmem] * 3,
        out_shape=[
            shape((2, 8 * BLK, 4 * BLK), BF),
            shape((2, 4 * BLK, 8 * BLK), BF),
            shape((rows, width), F32),
        ],
        compiler_params=params,
        cost_estimate=pl.CostEstimate(flops=3 * 10**8, bytes_accessed=6 * 10**6, transcendentals=0),
        name="prepare",
    )(hub_order.reshape(-1, 1), hub_order.reshape(1, -1), core, x, features, self_weight)
    own_other, off_other, on_same, hubs, pick, place, own_pre = barrier(
        (own_other, off_other, on_same, hubs, pick, place, own_pre)
    )
    off_same_low = to_side(off_other[:rows // 2])
    off_same_high = to_off(own_other[rows // 2:])
    on_other = to_core(own_other)
    hubs = spread(hubs, ("x",), N_X)
    hubs, off_same_low, off_same_high, on_other = barrier((hubs, off_same_low, off_same_high, on_other))
    hubs_there = to_core(hubs)

    embedding, slope, *w = pl.pallas_call(
        ahead,
        in_specs=[smem] * 6 + [hbm] * 14,
        out_specs=[vmem] * (3 + N_X),
        out_shape=[wide, wide] + [part] * N_X + [wide],
        scratch_shapes=[
            pltpu.VMEM((4, 8 * BLK, width), BF),
            pltpu.VMEM((4, 4, BLK, width), F32),
            pltpu.VMEM((2, rows, width), BF),
            pltpu.VMEM((4 * BLK, width), BF),
            pltpu.VMEM((4 * BLK, width), BF),
            pltpu.VMEM((2, 8 * BLK, 4 * BLK), BF),
            pltpu.VMEM((rows, width), F32),
            pltpu.VMEM(tile_values.shape, BF),
            pltpu.VMEM((width, width), BF),
            pltpu.VMEM((rows, width), BF),
            pltpu.SemaphoreType.DMA((14,)),
        ],
        compiler_params=params,
        cost_estimate=pl.CostEstimate(flops=2 * 10**9, bytes_accessed=10 * 10**6, transcendentals=0),
        name="ahead",
    )(
        *where, x,
        features, own_other, on_same, on_other, off_same_low, off_same_high, off_other,
        hubs, hubs_there, pick, own_pre, tile_values, neighbour_weight, cotangent,
    )
    w = join_cores(w)
    w, slope = barrier((w, slope))

    own_grad, g_own_other, g_on_same, g_on_other, g_off_same, g_off_other, *h = pl.pallas_call(
        behind,
        in_specs=[smem] * 5 + [vmem] * 5,
        out_specs=[vmem] * (7 + N_X),
        out_shape=[shape((rows, width), F32)] + [wide] * 5 + [part] * N_X + [wide],
        scratch_shapes=[
            pltpu.VMEM((4, 8 * BLK, width), F32),
            pltpu.VMEM((rows, width), BF),
            pltpu.VMEM((8 * BLK, width), BF),
        ],
        compiler_params=params,
        cost_estimate=pl.CostEstimate(flops=2 * 10**9, bytes_accessed=10 * 10**6, transcendentals=0),
        name="behind",
    )(*where, slope, place, tile_values, self_weight, neighbour_weight)

    w = collect_x(w)
    g = (g_own_other, g_on_same, g_on_other, g_off_same, g_off_other)
    w, h, g = barrier((w, h, g))
    g_own_other, g_on_same, g_on_other, g_off_same, g_off_other = g
    w, h = barrier((w, join_cores(h)))

    w = lax.all_to_all(w.reshape(N_WIDE, 4, width), WIDE, 0, 0, tiled=True).astype(F32).sum(0).astype(BF)
    h = collect_x(h)
    r_on_other = to_core(g_on_other)
    r_off_same = to_side(g_off_same)
    r_on_same = to_core(g_on_same)
    s_side = plus(g_own_other, r_on_other)
    s_off = plus(g_off_other, r_off_same)

    w, h, s_side, s_off, r_on_same = barrier((w, h, s_side, s_off, r_on_same))
    r_side = to_side(s_side)
    r_off = to_off(s_off)
    both = jnp.concatenate([jnp.broadcast_to(w[None], (N_WIDE, 4, width)), h.reshape(N_WIDE, 4, width)], 1)
    both = lax.all_to_all(both, WIDE, 0, 0, tiled=True)
    w = both[:, :4].reshape(BLK, width)
    hub_gradient = both[:, 4:].astype(F32).sum(0)
    w = spread(w, ("x",), N_X)
    w, r_side, r_off = barrier((w, r_side, r_off))
    there = to_core(w)
    feature_gradient = own_grad + r_on_same.astype(F32) + r_side.astype(F32) + r_off.astype(F32)
    first = core[0] == 0
    pair = (N_X, 1, BLK, width)
    low, high = jnp.where(first, w, there).reshape(pair), jnp.where(first, there, w).reshape(pair)
    weights = jnp.concatenate([low, high], 1).reshape(2, width, width).astype(F32)
    return embedding, feature_gradient, hub_gradient, weights[0], weights[1]


def solution(mesh):
    fine = Mesh(mesh.devices.reshape(EXTENT), AXES)
    split = P(AXES)
    in_specs = (split, split, P(), split, split, split, split, P(), P(), split)
    out_specs = (split, split, split, P(), P())
    return jax.shard_map(local, mesh=fine, in_specs=in_specs, out_specs=out_specs, check_vma=False)
```

time: 205 us -> 146 us (0.71)
  blocking collectives: 92.5 us -> 0 us
  starting transfers between devices: 37.8 us -> 77 us
  waiting for transfers between devices: 46.7 us -> 27.1 us
  Pallas kernels: 12.3 us -> 21.8 us
  other arithmetic: 4.8 us -> 8.8 us
    all_to_all x4 -> x0, blocking collectives: 92.5 us -> none  [the longest x2 56.6 us: collect(): return lax.all_to_all(value, axes, 0, 0, tiled=True).astype(F32).sum(0)]
    ppermute x10 -> x21, waiting for transfers between devices: 46.7 us -> 18.6 us  [the longest x3 11.1 us: to_off(): return lax.ppermute(value, AXES, pairs)]
    ppermute x10 -> x21, starting transfers between devices: 24.8 us -> 49.2 us  [the longest x6 19.2 us: to_x(): return lax.ppermute(value, 'x', [(x, x ^ flip) for x in range(N_X)])]
    all_to_all x0 -> x2, starting transfers between devices: none -> 10.8 us  [the longest x1 6.23 us: local(): both = lax.all_to_all(both, WIDE, 0, 0, tiled=True)]
    pallas_call x1 -> x3, Pallas kernels: 12.3 us -> 21.8 us  [the longest x1 9.16 us: local(): pl.pallas_call(behind, in_specs=[smem] * 5 + [vmem] * 5, out_specs=[vmem]...]
    convert_element_type x0 -> x7, other arithmetic: none -> 4.68 us  [the longest x4 3.43 us: plus(): return (a.astype(F32) + b.astype(F32)).astype(BF)]
    all_to_all x2 -> x3, waiting for transfers between devices: 0.01 us -> 4.4 us  [spread(): lax.all_to_all(copies, axes, 0, 0, tiled=True).reshape(-1, value.shape[-1])]
    all_to_all x0 -> x2, waiting for transfers between devices: none -> 4.09 us  [the longest x1 2.34 us: local(): both = lax.all_to_all(both, WIDE, 0, 0, tiled=True)]
  transfers between devices with their start and end apart: 12 -> 26, of which waited for: 8 -> 11; matrix products, arithmetic and copies ran while one was open for 2% -> 8% of each run, Pallas kernels for 0% -> 10%
where the time goes in v2:
time: 146 us; the launch traced here: 145 us
  starting transfers between devices  77 us (53%)
  waiting for transfers between devices  27.1 us (19%)
  Pallas kernels  21.8 us (15%)
  other arithmetic  8.8 us (6%)
  local copies, waits for them, and re-layouts  8.71 us (6%)
  between operations  1.64 us (1%)
    ppermute x6, starting transfers between devices, to_x(): return lax.ppermute(value, 'x', [(x, x ^ flip) for x in range(N_X)])  19.2 us
    all_to_all x3, starting transfers between devices, spread(): lax.all_to_all(copies, axes, 0, 0, tiled=True).reshape(-1, value.shape[-1])  17 us
    ppermute x3, starting transfers between devices, to_off(): return lax.ppermute(value, AXES, pairs)  14.8 us
    ppermute x8, starting transfers between devices, to_core(): return lax.ppermute(value, AXES, [(d, d ^ 2) for d in range(DEVICES)])  11.6 us
    ppermute x3, waiting for transfers between devices, to_off(): return lax.ppermute(value, AXES, pairs)  11.1 us
    pallas_call x1, Pallas kernels, local(): pl.pallas_call(behind, in_specs=[smem] * 5 + [vmem] * 5, out_specs=[vmem]...  9.16 us
    pallas_call x1, Pallas kernels, local(): pl.pallas_call(ahead, in_specs=[smem] * 6 + [hbm] * 14, out_specs=[vmem]...  7.64 us
    all_to_all x1, starting transfers between devices, local(): both = lax.all_to_all(both, WIDE, 0, 0, tiled=True)  6.23 us
  transfers between devices with their start and end apart: 26, of which 11 were waited for; matrix products, arithmetic and copies ran while one was open for 8% of the time, Pallas kernels for 10%

profile of v2, /device:TPU:1, one launch (start us, length us, event | category | flops | bytes accessed | tf_op | source)
XLA Modules:
  0.0 145.1 jit_solution(9057955095748238574)
XLA Ops:
  0.6 2.2 %collective-permute-start = (bf16[512,512]{1,0:T(8,128)(2,1)}, bf16[512,512]{1,0:T(8,128)(2,1)S(1)}, u32[]{:S(2)}, u32[]{:S(2)}) collective-permute-start(bf16[512,512]{1,0:T(8,128)(2,1)} %features.3), channel_id=1, source_target_pairs={{0,1},{1,0},{2,3},{3,2},{4,5},{5,4},{6,7},{7,6},{8,9},{9,8},{10,11... | collective-permute-start | bytes 1572872 | tf_op jit(solution)/shard_map/ppermute | solution.py:26
  2.8 4.6 %collective-permute-start.1 = (bf16[512,512]{1,0:T(8,128)(2,1)}, bf16[512,512]{1,0:T(8,128)(2,1)S(1)}, u32[]{:S(2)}, u32[]{:S(2)}) collective-permute-start(bf16[512,512]{1,0:T(8,128)(2,1)} %features.3), channel_id=1, source_target_pairs={{2,5},{3,4},{4,3},{5,2},{6,9},{7,8},{8,7},{9,6},{10,13},{11,12},{1... | collective-permute-start | bytes 1572872 | tf_op jit(solution)/shard_map/ppermute | solution.py:36
  9.0 9.5 %all-to-all-start = ((bf16[32,4,512]{2,1,0:T(4,128)(2,1)}), bf16[32,4,512]{2,1,0:T(4,128)(2,1)S(1)}, u32[]{:S(2)}, u32[]{:S(2)}) async-start(bf16[32,4,512]{2,1,0:T(4,128)(2,1)} %broadcast_in_dim.10), calls=%async_computation | async-start | bytes 262144 | tf_op jit(solution)/shard_map/all_to_all | solution.py:41
  18.5 1.7 %copy.15.order_col = s32[1024,1]{1,0:T(8,128)} copy(s32[1024,1]{0,1:T(1,128)} %bitcast.19) | data formatting | bytes 8192 | tf_op jit(solution)/shard_map/reshape | solution.py:255
  20.2 5.0 %prepare.1 = (bf16[2,1024,512]{2,1,0:T(8,128)(2,1)}, bf16[2,512,1024]{2,1,0:T(8,128)(2,1)}, f32[512,512]{1,0:T(8,128)}) custom-call(s32[1024,1]{1,0:T(8,128)} %copy.15.order_col, s32[1,1024]{1,0:T(1,128)} %bitcast.20, s32[1]{0:T(128)} %bitcast.1.core.core_ref, s32[1]{0:T(128)} %bitcast.2.x_ref, bf16[512,512]{1,0:T(8,128)(2,1)} %features.3, ...), custom_call_target="tpu_custom_call" | custom-call | flops 300000000 | bytes 6000000 | tf_op jit(solution)/shard_map/prepare/pallas_call | solution.py:243
  25.2 2.7 %all-to-all-done = bf16[32,4,512]{2,1,0:T(4,128)(2,1)S(1)} async-done(((bf16[32,4,512]{2,1,0:T(4,128)(2,1)}), bf16[32,4,512]{2,1,0:T(4,128)(2,1)S(1)}, u32[]{:S(2)}, u32[]{:S(2)}) %all-to-all-start) | async-done | bytes 131104 | tf_op jit(solution)/shard_map/all_to_all | solution.py:41
  28.0 2.2 %collective-permute-start.5 = (bf16[512,512]{1,0:T(8,128)(2,1)S(1)}, bf16[512,512]{1,0:T(8,128)(2,1)S(1)}, u32[]{:S(2)}, u32[]{:S(2)}) collective-permute-start(bf16[512,512]{1,0:T(8,128)(2,1)S(1)} %collective-permute-done.own_other), channel_id=1, source_target_pairs={{0,2},{1,3},{2,0},{3,1},{4,6},{5,7},{6,4},{7,5},{8,10},{9,11},{10,... | collective-permute-start | bytes 1572872 | tf_op jit(solution)/shard_map/ppermute | solution.py:22
  31.0 4.0 %all-to-all-start.1 = ((bf16[4,128,512]{2,1,0:T(8,128)(2,1)}), bf16[4,128,512]{2,1,0:T(8,128)(2,1)S(1)}, u32[]{:S(2)}, u32[]{:S(2)}) async-start(bf16[4,128,512]{2,1,0:T(8,128)(2,1)} %broadcast_in_dim.11), calls=%async_computation.1 | async-start | bytes 1048576 | tf_op jit(solution)/shard_map/all_to_all | solution.py:41
  35.0 3.3 %collective-permute-start.4 = (bf16[256,512]{1,0:T(8,128)(2,1)S(1)}, bf16[256,512]{1,0:T(8,128)(2,1)S(1)}, u32[]{:S(2)}, u32[]{:S(2)}) collective-permute-start(bf16[256,512]{1,0:T(8,128)(2,1)S(1)} %slice.45), channel_id=1, source_target_pairs={{2,5},{3,4},{4,3},{5,2},{6,9},{7,8},{8,7},{9,6},{10,13},{11,12},{1... | collective-permute-start | bytes 786440 | tf_op jit(solution)/shard_map/ppermute | solution.py:36
  38.4 6.0 %collective-permute-done.4.off_same_high = bf16[256,512]{1,0:T(8,128)(2,1)S(1)} collective-permute-done((bf16[256,512]{1,0:T(8,128)(2,1)S(1)}, bf16[256,512]{1,0:T(8,128)(2,1)S(1)}, u32[]{:S(2)}, u32[]{:S(2)}) %collective-permute-start.4) | collective-permute-done | bytes 262176 | tf_op jit(solution)/shard_map/ppermute | solution.py:36
  48.4 7.6 %ahead.1 = (bf16[512,512]{1,0:T(8,128)(2,1)}, bf16[512,512]{1,0:T(8,128)(2,1)}, bf16[128,512]{1,0:T(8,128)(2,1)}, bf16[128,512]{1,0:T(8,128)(2,1)}, bf16[128,512...) custom-call(s32[1,64]{1,0:T(1,128)} %dest.3, s32[1,64]{1,0:T(1,128)} %source.3, ...), custom_call_target="tpu_custom_call" | custom-call | flops 2000000000 | bytes 10000000 | tf_op jit(solution)/shard_map/ahead/pallas_call | solution.py:266
  56.1 1.4 collective-permute-start.7
  57.5 1.7 %collective-permute-done.7 = bf16[512,512]{1,0:T(8,128)(2,1)S(1)} collective-permute-done((bf16[512,512]{1,0:T(8,128)(2,1)}, bf16[512,512]{1,0:T(8,128)(2,1)S(1)}, u32[]{:S(2)}, u32[]{:S(2)}) %collective-permute-start.7) | collective-permute-done | bytes 524320 | tf_op jit(solution)/shard_map/ppermute | solution.py:22
  60.5 7.6 %collective-permute-start.10 = (bf16[128,512]{1,0:T(8,128)(2,1)S(1)}, bf16[128,512]{1,0:T(8,128)(2,1)S(1)}, u32[]{:S(2)}, u32[]{:S(2)}) collective-permute-start(bf16[128,512]{1,0:T(8,128)(2,1)S(1)} %get-tuple-element.92), channel_id=1, source_target_pairs={{0,192},{64,128},{128,64},{192,0},{1,193},{65,129},{129,65},{193,1... | collective-permute-start | bytes 393224 | tf_op jit(solution)/shard_map/ppermute | solution.py:45
  69.3 9.2 %behind.1 = (f32[512,512]{1,0:T(8,128)}, bf16[512,512]{1,0:T(8,128)(2,1)}, bf16[512,512]{1,0:T(8,128)(2,1)}, bf16[512,512]{1,0:T(8,128)(2,1)}, bf16[512,512]{1,0...) custom-call(s32[1,64]{1,0:T(1,128)} %dest.3, ...), custom_call_target="tpu_custom_call" | custom-call | flops 2000000000 | bytes 10000000 | tf_op jit(solution)/shard_map/behind/pallas_call | solution.py:295
  78.6 2.3 %collective-permute-start.11 = (bf16[512,512]{1,0:T(8,128)(2,1)}, bf16[512,512]{1,0:T(8,128)(2,1)S(1)}, u32[]{:S(2)}, u32[]{:S(2)}) collective-permute-start(bf16[512,512]{1,0:T(8,128)(2,1)} %get-tuple-element.105), channel_id=1, source_target_pairs={{0,2},{1,3},{2,0},{3,1},{4,6},{5,7},{6,4},{7,5},{8,10},{9,11},{10,... | collective-permute-start | bytes 1572872 | tf_op jit(solution)/shard_map/ppermute | solution.py:22
  82.7 1.9 %add_convert_fusion.3 = (bf16[128,512]{1,0:T(8,128)(2,1)S(1)}, bf16[128,512]{1,0:T(8,128)(2,1)}, bf16[128,512]{1,0:T(8,128)(2,1)}, bf16[128,512]{1,0:T(8,128)(2,1)S(1)}) fusion(bf16[128,512]{1,0:T(8,128)(2,1)} %get-tuple-element.108, bf16[512,512]{1,0:T(8,128)(2,1)S(1)} %collective-permute-done.11, bf16[128,512]{1,0:T(8,128)(2,1)} %get-tuple-element.107, ...), kind=kLoop, calls=%fused_computation.9 | loop fusion | flops 1048576 | bytes 1572864 | tf_op jit(solution)/shard_map/convert_element_type | solution.py:210
  84.6 2.3 %collective-permute-start.12 = (bf16[128,512]{1,0:T(8,128)(2,1)}, bf16[128,512]{1,0:T(8,128)(2,1)}, u32[]{:S(2)}, u32[]{:S(2)}) collective-permute-start(bf16[128,512]{1,0:T(8,128)(2,1)} %get-tuple-element.111), channel_id=1, source_target_pairs={{0,64},{64,0},{128,192},{192,128},{1,65},{65,1},{129,193},{193,129... | collective-permute-start | bytes 393224 | tf_op jit(solution)/shard_map/ppermute | solution.py:45
  86.9 4.4 %collective-permute-start.13 = (bf16[128,512]{1,0:T(8,128)(2,1)}, bf16[128,512]{1,0:T(8,128)(2,1)}, u32[]{:S(2)}, u32[]{:S(2)}) collective-permute-start(bf16[128,512]{1,0:T(8,128)(2,1)} %get-tuple-element.112), channel_id=1, source_target_pairs={{0,128},{64,192},{128,0},{192,64},{1,129},{65,193},{129,1},{193,65... | collective-permute-start | bytes 393224 | tf_op jit(solution)/shard_map/ppermute | solution.py:45
  92.0 4.6 %all-to-all-start.2 = ((bf16[32,4,512]{2,1,0:T(4,128)(2,1)}), bf16[32,4,512]{2,1,0:T(4,128)(2,1)S(1)}, u32[]{:S(2)}, u32[]{:S(2)}) async-start(bf16[32,4,512]{2,1,0:T(4,128)(2,1)} %reshape.63), calls=%async_computation.2 | async-start | bytes 262144 | tf_op jit(solution)/shard_map/all_to_all | solution.py:316
  96.6 3.6 %collective-permute-start.14 = (bf16[128,512]{1,0:T(8,128)(2,1)S(1)}, bf16[128,512]{1,0:T(8,128)(2,1)S(1)}, u32[]{:S(2)}, u32[]{:S(2)}) collective-permute-start(bf16[128,512]{1,0:T(8,128)(2,1)S(1)} %get-tuple-element.113), channel_id=1, source_target_pairs={{0,192},{64,128},{128,64},{192,0},{1,193},{65,129},{129,65},{193,1... | collective-permute-start | bytes 393224 | tf_op jit(solution)/shard_map/ppermute | solution.py:45
  100.6 2.6 %collective-permute-done.14 = bf16[128,512]{1,0:T(8,128)(2,1)S(1)} collective-permute-done((bf16[128,512]{1,0:T(8,128)(2,1)S(1)}, bf16[128,512]{1,0:T(8,128)(2,1)S(1)}, u32[]{:S(2)}, u32[]{:S(2)}) %collective-permute-start.14) | collective-permute-done | bytes 131104 | tf_op jit(solution)/shard_map/ppermute | solution.py:45
  104.2 1.8 %all-to-all-done.2 = bf16[32,4,512]{2,1,0:T(4,128)(2,1)S(1)} async-done(((bf16[32,4,512]{2,1,0:T(4,128)(2,1)}), bf16[32,4,512]{2,1,0:T(4,128)(2,1)S(1)}, u32[]{:S(2)}, u32[]{:S(2)}) %all-to-all-start.2) | async-done | bytes 131104 | tf_op jit(solution)/shard_map/all_to_all | solution.py:316
  106.9 6.2 %all-to-all-start.3 = ((bf16[32,8,512]{2,1,0:T(8,128)(2,1)}), bf16[32,8,512]{2,1,0:T(8,128)(2,1)S(1)}, u32[]{:S(2)}, u32[]{:S(2)}) async-start(bf16[32,8,512]{2,1,0:T(8,128)(2,1)} %pad_maximum_fusion), calls=%async_computation.3 | async-start | bytes 524288 | tf_op jit(solution)/shard_map/all_to_all | solution.py:328
  114.5 6.9 %collective-permute-start.19 = (bf16[512,512]{1,0:T(8,128)(2,1)S(1)}, bf16[512,512]{1,0:T(8,128)(2,1)}, u32[]{:S(2)}, u32[]{:S(2)}) collective-permute-start(bf16[512,512]{1,0:T(8,128)(2,1)S(1)} %add_convert_fusion), channel_id=1, source_target_pairs={{2,5},{3,4},{4,3},{5,2},{6,9},{7,8},{8,7},{9,6},{10,13},{11,12},{1... | collective-permute-start | bytes 1572872 | tf_op jit(solution)/shard_map/ppermute | solution.py:36
  121.4 2.3 %all-to-all-done.3 = bf16[32,8,512]{2,1,0:T(8,128)(2,1)S(1)} async-done(((bf16[32,8,512]{2,1,0:T(8,128)(2,1)}), bf16[32,8,512]{2,1,0:T(8,128)(2,1)S(1)}, u32[]{:S(2)}, u32[]{:S(2)}) %all-to-all-start.3) | async-done | bytes 262176 | tf_op jit(solution)/shard_map/all_to_all | solution.py:328
  124.6 3.5 %all-to-all-start.4 = ((bf16[4,128,512]{2,1,0:T(8,128)(2,1)}), bf16[4,128,512]{2,1,0:T(8,128)(2,1)S(1)}, u32[]{:S(2)}, u32[]{:S(2)}) async-start(bf16[4,128,512]{2,1,0:T(8,128)(2,1)} %broadcast_in_dim.14), calls=%async_computation.4 | async-start | bytes 1048576 | tf_op jit(solution)/shard_map/all_to_all | solution.py:41
  128.1 5.1 %collective-permute-done.19 = bf16[512,512]{1,0:T(8,128)(2,1)} collective-permute-done((bf16[512,512]{1,0:T(8,128)(2,1)S(1)}, bf16[512,512]{1,0:T(8,128)(2,1)}, u32[]{:S(2)}, u32[]{:S(2)}) %collective-permute-start.19) | collective-permute-done | bytes 524320 | tf_op jit(solution)/shard_map/ppermute | solution.py:36
  133.3 1.7 %all-to-all-done.4 = bf16[4,128,512]{2,1,0:T(8,128)(2,1)S(1)} async-done(((bf16[4,128,512]{2,1,0:T(8,128)(2,1)}), bf16[4,128,512]{2,1,0:T(8,128)(2,1)S(1)}, u32[]{:S(2)}, u32[]{:S(2)}) %all-to-all-start.4) | async-done | bytes 524320 | tf_op jit(solution)/shard_map/all_to_all | solution.py:41
  135.0 5.1 %collective-permute-start.20 = (bf16[512,512]{1,0:T(8,128)(2,1)S(1)}, bf16[512,512]{1,0:T(8,128)(2,1)S(1)}, u32[]{:S(2)}, u32[]{:S(2)}) collective-permute-start(bf16[512,512]{1,0:T(8,128)(2,1)S(1)} %bitcast.13), channel_id=1, source_target_pairs={{0,2},{1,3},{2,0},{3,1},{4,6},{5,7},{6,4},{7,5},{8,10},{9,11},{10,... | collective-permute-start | bytes 1572872 | tf_op jit(solution)/shard_map/ppermute | solution.py:22
  140.8 2.4 %convert_add_fusion = f32[512,512]{1,0:T(8,128)} fusion(bf16[512,512]{1,0:T(8,128)(2,1)} %collective-permute-done.19, bf16[512,512]{1,0:T(8,128)(2,1)} %collective-permute-done.18, f32[512,512]{1,0:T(8,128)S(1)} %copy-done.3, bf16[512,512]{1,0:T(8,128)(2,1)S(1)} %collective-permute-done.17), kind=kLoop, calls=%fused_computation.1 | loop fusion | flops 1572864 | bytes 3670016 | tf_op jit(solution)/shard_map/add | solution.py:334
  143.5 1.6 %fusion = (f32[2,2,128,512]{3,2,1,0:T(8,128)}, f32[2,2,128,512]{3,2,1,0:T(8,128)}) fusion(f32[4,2,128,512]{3,2,1,0:T(8,128)S(1)} %maximum_convert_fusion), kind=kLoop, calls=%fused_computation.18 | loop fusion | bytes 4194304 | tf_op jit(solution)/shard_map/slice | solution.py:339
  (70 shorter events, 16.3 us)
Async XLA Ops:
  0.6 27.3 %collective-permute-start = (bf16[512,512]{1,0:T(8,128)(2,1)}, bf16[512,512]{1,0:T(8,128)(2,1)S(1)}, u32[]{:S(2)}, u32[]{:S(2)}) collective-permute-start(bf16[512,512]{1,0:T(8,128)(2,1)} %features.3), channel_id=1, source_target_pairs={{0,1},{1,0},{2,3},{3,2},{4,5},{5,4},{6,7},{7,6},{8,9},{9,8},{10,11... | collective-permute-start | bytes 1572872 | tf_op jit(solution)/shard_map/ppermute | solution.py:26
  2.8 25.1 %collective-permute-start.1 = (bf16[512,512]{1,0:T(8,128)(2,1)}, bf16[512,512]{1,0:T(8,128)(2,1)S(1)}, u32[]{:S(2)}, u32[]{:S(2)}) collective-permute-start(bf16[512,512]{1,0:T(8,128)(2,1)} %features.3), channel_id=1, source_target_pairs={{2,5},{3,4},{4,3},{5,2},{6,9},{7,8},{8,7},{9,6},{10,13},{11,12},{1... | collective-permute-start | bytes 1572872 | tf_op jit(solution)/shard_map/ppermute | solution.py:36
  7.5 20.4 %collective-permute-start.2 = (bf16[512,512]{1,0:T(8,128)(2,1)}, bf16[512,512]{1,0:T(8,128)(2,1)S(1)}, u32[]{:S(2)}, u32[]{:S(2)}) collective-permute-start(bf16[512,512]{1,0:T(8,128)(2,1)} %features.3), channel_id=1, source_target_pairs={{0,2},{1,3},{2,0},{3,1},{4,6},{5,7},{6,4},{7,5},{8,10},{9,11},{10,... | collective-permute-start | bytes 1572872 | tf_op jit(solution)/shard_map/ppermute | solution.py:22
  9.0 18.9 %all-to-all-start = ((bf16[32,4,512]{2,1,0:T(4,128)(2,1)}), bf16[32,4,512]{2,1,0:T(4,128)(2,1)S(1)}, u32[]{:S(2)}, u32[]{:S(2)}) async-start(bf16[32,4,512]{2,1,0:T(4,128)(2,1)} %broadcast_in_dim.10), calls=%async_computation | async-start | bytes 262144 | tf_op jit(solution)/shard_map/all_to_all | solution.py:41
  27.9 19.7 %copy-start.1 = (bf16[512,512]{1,0:T(8,128)(2,1)}, bf16[512,512]{1,0:T(8,128)(2,1)S(1)}, u32[]{:S(2)}) copy-start(bf16[512,512]{1,0:T(8,128)(2,1)S(1)} %collective-permute-done.own_other) | copy-start | bytes 1572868
  27.9 19.7 %copy-start.2 = (bf16[512,512]{1,0:T(8,128)(2,1)}, bf16[512,512]{1,0:T(8,128)(2,1)S(1)}, u32[]{:S(2)}) copy-start(bf16[512,512]{1,0:T(8,128)(2,1)S(1)} %collective-permute-done.1.off_other) | copy-start | bytes 1572868
  27.9 19.7 %copy-start.4 = (bf16[512,512]{1,0:T(8,128)(2,1)}, bf16[512,512]{1,0:T(8,128)(2,1)S(1)}, u32[]{:S(2)}) copy-start(bf16[512,512]{1,0:T(8,128)(2,1)S(1)} %collective-permute-done.2.on_same) | copy-start | bytes 1572868
  28.0 17.1 %collective-permute-start.5 = (bf16[512,512]{1,0:T(8,128)(2,1)S(1)}, bf16[512,512]{1,0:T(8,128)(2,1)S(1)}, u32[]{:S(2)}, u32[]{:S(2)}) collective-permute-start(bf16[512,512]{1,0:T(8,128)(2,1)S(1)} %collective-permute-done.own_other), channel_id=1, source_target_pairs={{0,2},{1,3},{2,0},{3,1},{4,6},{5,7},{6,4},{7,5},{8,10},{9,11},{10,... | collective-permute-start | bytes 1572872 | tf_op jit(solution)/shard_map/ppermute | solution.py:22
  31.0 14.1 %all-to-all-start.1 = ((bf16[4,128,512]{2,1,0:T(8,128)(2,1)}), bf16[4,128,512]{2,1,0:T(8,128)(2,1)S(1)}, u32[]{:S(2)}, u32[]{:S(2)}) async-start(bf16[4,128,512]{2,1,0:T(8,128)(2,1)} %broadcast_in_dim.11), calls=%async_computation.1 | async-start | bytes 1048576 | tf_op jit(solution)/shard_map/all_to_all | solution.py:41
  35.0 9.4 %collective-permute-start.4 = (bf16[256,512]{1,0:T(8,128)(2,1)S(1)}, bf16[256,512]{1,0:T(8,128)(2,1)S(1)}, u32[]{:S(2)}, u32[]{:S(2)}) collective-permute-start(bf16[256,512]{1,0:T(8,128)(2,1)S(1)} %slice.45), channel_id=1, source_target_pairs={{2,5},{3,4},{4,3},{5,2},{6,9},{7,8},{8,7},{9,6},{10,13},{11,12},{1... | collective-permute-start | bytes 786440 | tf_op jit(solution)/shard_map/ppermute | solution.py:36
  38.3 6.7 %collective-permute-start.3 = (bf16[256,512]{1,0:T(8,128)(2,1)S(1)}, bf16[256,512]{1,0:T(8,128)(2,1)S(1)}, u32[]{:S(2)}, u32[]{:S(2)}) collective-permute-start(bf16[256,512]{1,0:T(8,128)(2,1)S(1)} %slice.44), channel_id=1, source_target_pairs={{0,1},{1,0},{2,3},{3,2},{4,5},{5,4},{6,7},{7,6},{8,9},{9,8},{10,11... | collective-permute-start | bytes 786440 | tf_op jit(solution)/shard_map/ppermute | solution.py:26
  45.7 1.9 %collective-permute-start.6 = (bf16[512,512]{1,0:T(8,128)(2,1)S(1)}, bf16[512,512]{1,0:T(8,128)(2,1)S(1)}, u32[]{:S(2)}, u32[]{:S(2)}) collective-permute-start(bf16[512,512]{1,0:T(8,128)(2,1)S(1)} %bitcast.11), channel_id=1, source_target_pairs={{0,2},{1,3},{2,0},{3,1},{4,6},{5,7},{6,4},{7,5},{8,10},{9,11},{10,... | collective-permute-start | bytes 1572872 | tf_op jit(solution)/shard_map/ppermute | solution.py:22
  56.1 3.1 %collective-permute-start.7 = (bf16[512,512]{1,0:T(8,128)(2,1)}, bf16[512,512]{1,0:T(8,128)(2,1)S(1)}, u32[]{:S(2)}, u32[]{:S(2)}) collective-permute-start(bf16[512,512]{1,0:T(8,128)(2,1)} %get-tuple-element.81), channel_id=1, source_target_pairs={{0,2},{1,3},{2,0},{3,1},{4,6},{5,7},{6,4},{7,5},{8,10},{9,11},{10,... | collective-permute-start | bytes 1572872 | tf_op jit(solution)/shard_map/ppermute | solution.py:22
  60.5 18.1 %collective-permute-start.10 = (bf16[128,512]{1,0:T(8,128)(2,1)S(1)}, bf16[128,512]{1,0:T(8,128)(2,1)S(1)}, u32[]{:S(2)}, u32[]{:S(2)}) collective-permute-start(bf16[128,512]{1,0:T(8,128)(2,1)S(1)} %get-tuple-element.92), channel_id=1, source_target_pairs={{0,192},{64,128},{128,64},{192,0},{1,193},{65,129},{129,65},{193,1... | collective-permute-start | bytes 393224 | tf_op jit(solution)/shard_map/ppermute | solution.py:45
  68.0 10.5 %collective-permute-start.8 = (bf16[128,512]{1,0:T(8,128)(2,1)S(1)}, bf16[128,512]{1,0:T(8,128)(2,1)S(1)}, u32[]{:S(2)}, u32[]{:S(2)}) collective-permute-start(bf16[128,512]{1,0:T(8,128)(2,1)S(1)} %get-tuple-element.90), channel_id=1, source_target_pairs={{0,64},{64,0},{128,192},{192,128},{1,65},{65,1},{129,193},{193,129... | collective-permute-start | bytes 393224 | tf_op jit(solution)/shard_map/ppermute | solution.py:45
  68.1 10.5 %collective-permute-start.9 = (bf16[128,512]{1,0:T(8,128)(2,1)S(1)}, bf16[128,512]{1,0:T(8,128)(2,1)S(1)}, u32[]{:S(2)}, u32[]{:S(2)}) collective-permute-start(bf16[128,512]{1,0:T(8,128)(2,1)S(1)} %get-tuple-element.91), channel_id=1, source_target_pairs={{0,128},{64,192},{128,0},{192,64},{1,129},{65,193},{129,1},{193,65... | collective-permute-start | bytes 393224 | tf_op jit(solution)/shard_map/ppermute | solution.py:45
  78.5 21.8 %copy-start.6 = (bf16[512,512]{1,0:T(8,128)(2,1)S(1)}, bf16[512,512]{1,0:T(8,128)(2,1)}, u32[]{:S(2)}) copy-start(bf16[512,512]{1,0:T(8,128)(2,1)} %get-tuple-element.116) | copy-start | bytes 1572868
  78.5 21.9 %copy-start.5 = (bf16[512,512]{1,0:T(8,128)(2,1)S(1)}, bf16[512,512]{1,0:T(8,128)(2,1)}, u32[]{:S(2)}) copy-start(bf16[512,512]{1,0:T(8,128)(2,1)} %get-tuple-element.114) | copy-start | bytes 1572868
  78.6 4.1 %collective-permute-start.11 = (bf16[512,512]{1,0:T(8,128)(2,1)}, bf16[512,512]{1,0:T(8,128)(2,1)S(1)}, u32[]{:S(2)}, u32[]{:S(2)}) collective-permute-start(bf16[512,512]{1,0:T(8,128)(2,1)} %get-tuple-element.105), channel_id=1, source_target_pairs={{0,2},{1,3},{2,0},{3,1},{4,6},{5,7},{6,4},{7,5},{8,10},{9,11},{10,... | collective-permute-start | bytes 1572872 | tf_op jit(solution)/shard_map/ppermute | solution.py:22
  81.0 15.6 %collective-permute-start.16 = (bf16[512,512]{1,0:T(8,128)(2,1)}, bf16[512,512]{1,0:T(8,128)(2,1)S(1)}, u32[]{:S(2)}, u32[]{:S(2)}) collective-permute-start(bf16[512,512]{1,0:T(8,128)(2,1)} %get-tuple-element.117), channel_id=1, source_target_pairs={{0,1},{1,0},{2,3},{3,2},{4,5},{5,4},{6,7},{7,6},{8,9},{9,8},{10,11... | collective-permute-start | bytes 1572872 | tf_op jit(solution)/shard_map/ppermute | solution.py:26
  81.0 19.4 %collective-permute-start.15 = (bf16[512,512]{1,0:T(8,128)(2,1)}, bf16[512,512]{1,0:T(8,128)(2,1)S(1)}, u32[]{:S(2)}, u32[]{:S(2)}) collective-permute-start(bf16[512,512]{1,0:T(8,128)(2,1)} %get-tuple-element.115), channel_id=1, source_target_pairs={{0,2},{1,3},{2,0},{3,1},{4,6},{5,7},{6,4},{7,5},{8,10},{9,11},{10,... | collective-permute-start | bytes 1572872 | tf_op jit(solution)/shard_map/ppermute | solution.py:22
  81.2 24.9 %collective-permute-start.17 = (bf16[512,512]{1,0:T(8,128)(2,1)}, bf16[512,512]{1,0:T(8,128)(2,1)S(1)}, u32[]{:S(2)}, u32[]{:S(2)}) collective-permute-start(bf16[512,512]{1,0:T(8,128)(2,1)} %get-tuple-element.118), channel_id=1, source_target_pairs={{0,2},{1,3},{2,0},{3,1},{4,6},{5,7},{6,4},{7,5},{8,10},{9,11},{10,... | collective-permute-start | bytes 1572872 | tf_op jit(solution)/shard_map/ppermute | solution.py:22
  84.6 15.9 %collective-permute-start.12 = (bf16[128,512]{1,0:T(8,128)(2,1)}, bf16[128,512]{1,0:T(8,128)(2,1)}, u32[]{:S(2)}, u32[]{:S(2)}) collective-permute-start(bf16[128,512]{1,0:T(8,128)(2,1)} %get-tuple-element.111), channel_id=1, source_target_pairs={{0,64},{64,0},{128,192},{192,128},{1,65},{65,1},{129,193},{193,129... | collective-permute-start | bytes 393224 | tf_op jit(solution)/shard_map/ppermute | solution.py:45
  86.9 13.6 %collective-permute-start.13 = (bf16[128,512]{1,0:T(8,128)(2,1)}, bf16[128,512]{1,0:T(8,128)(2,1)}, u32[]{:S(2)}, u32[]{:S(2)}) collective-permute-start(bf16[128,512]{1,0:T(8,128)(2,1)} %get-tuple-element.112), channel_id=1, source_target_pairs={{0,128},{64,192},{128,0},{192,64},{1,129},{65,193},{129,1},{193,65... | collective-permute-start | bytes 393224 | tf_op jit(solution)/shard_map/ppermute | solution.py:45
  92.0 13.9 %all-to-all-start.2 = ((bf16[32,4,512]{2,1,0:T(4,128)(2,1)}), bf16[32,4,512]{2,1,0:T(4,128)(2,1)S(1)}, u32[]{:S(2)}, u32[]{:S(2)}) async-start(bf16[32,4,512]{2,1,0:T(4,128)(2,1)} %reshape.63), calls=%async_computation.2 | async-start | bytes 262144 | tf_op jit(solution)/shard_map/all_to_all | solution.py:316
  96.6 6.5 %collective-permute-start.14 = (bf16[128,512]{1,0:T(8,128)(2,1)S(1)}, bf16[128,512]{1,0:T(8,128)(2,1)S(1)}, u32[]{:S(2)}, u32[]{:S(2)}) collective-permute-start(bf16[128,512]{1,0:T(8,128)(2,1)S(1)} %get-tuple-element.113), channel_id=1, source_target_pairs={{0,192},{64,128},{128,64},{192,0},{1,193},{65,129},{129,65},{193,1... | collective-permute-start | bytes 393224 | tf_op jit(solution)/shard_map/ppermute | solution.py:45
  104.2 36.7 %copy-start.3 = (f32[512,512]{1,0:T(8,128)S(1)}, f32[512,512]{1,0:T(8,128)}, u32[]{:S(2)}) copy-start(f32[512,512]{1,0:T(8,128)} %get-tuple-element.88) | copy-start | bytes 3145732
  106.9 16.8 %all-to-all-start.3 = ((bf16[32,8,512]{2,1,0:T(8,128)(2,1)}), bf16[32,8,512]{2,1,0:T(8,128)(2,1)S(1)}, u32[]{:S(2)}, u32[]{:S(2)}) async-start(bf16[32,8,512]{2,1,0:T(8,128)(2,1)} %pad_maximum_fusion), calls=%async_computation.3 | async-start | bytes 524288 | tf_op jit(solution)/shard_map/all_to_all | solution.py:328
  113.2 14.9 %collective-permute-start.18 = (bf16[512,512]{1,0:T(8,128)(2,1)S(1)}, bf16[512,512]{1,0:T(8,128)(2,1)}, u32[]{:S(2)}, u32[]{:S(2)}) collective-permute-start(bf16[512,512]{1,0:T(8,128)(2,1)S(1)} %add_convert_fusion.1), channel_id=1, source_target_pairs={{0,1},{1,0},{2,3},{3,2},{4,5},{5,4},{6,7},{7,6},{8,9},{9,8},{10,11... | collective-permute-start | bytes 1572872 | tf_op jit(solution)/shard_map/ppermute | solution.py:26
  114.5 18.8 %collective-permute-start.19 = (bf16[512,512]{1,0:T(8,128)(2,1)S(1)}, bf16[512,512]{1,0:T(8,128)(2,1)}, u32[]{:S(2)}, u32[]{:S(2)}) collective-permute-start(bf16[512,512]{1,0:T(8,128)(2,1)S(1)} %add_convert_fusion), channel_id=1, source_target_pairs={{2,5},{3,4},{4,3},{5,2},{6,9},{7,8},{8,7},{9,6},{10,13},{11,12},{1... | collective-permute-start | bytes 1572872 | tf_op jit(solution)/shard_map/ppermute | solution.py:36
  124.6 10.4 %all-to-all-start.4 = ((bf16[4,128,512]{2,1,0:T(8,128)(2,1)}), bf16[4,128,512]{2,1,0:T(8,128)(2,1)S(1)}, u32[]{:S(2)}, u32[]{:S(2)}) async-start(bf16[4,128,512]{2,1,0:T(8,128)(2,1)} %broadcast_in_dim.14), calls=%async_computation.4 | async-start | bytes 1048576 | tf_op jit(solution)/shard_map/all_to_all | solution.py:41
  135.0 8.3 %collective-permute-start.20 = (bf16[512,512]{1,0:T(8,128)(2,1)S(1)}, bf16[512,512]{1,0:T(8,128)(2,1)S(1)}, u32[]{:S(2)}, u32[]{:S(2)}) collective-permute-start(bf16[512,512]{1,0:T(8,128)(2,1)S(1)} %bitcast.13), channel_id=1, source_target_pairs={{0,2},{1,3},{2,0},{3,1},{4,6},{5,7},{6,4},{7,5},{8,10},{9,11},{10,... | collective-permute-start | bytes 1572872 | tf_op jit(solution)/shard_map/ppermute | solution.py:22
  (5 other events, 9.3 us)

commit v3 on v2

v3 whole, which is shorter than its diff:
```python
import functools

import jax
import jax.numpy as jnp
from jax import lax
from jax.experimental import pallas as pl
from jax.experimental.pallas import tpu as pltpu
from jax.sharding import Mesh
from jax.sharding import PartitionSpec as P

BF = jnp.bfloat16
F32 = jnp.float32
BLK = 128
AXES = ("x", "z", "yh", "core", "yl")
EXTENT = (4, 8, 2, 2, 2)
WIDE = ("z", "yh", "yl")
N_WIDE, N_X = 32, 4
DEVICES = 256


def to_core(value):
    return lax.ppermute(value, AXES, [(d, d ^ 2) for d in range(DEVICES)])


def to_side(value):
    return lax.ppermute(value, AXES, [(d, d ^ 1) for d in range(DEVICES)])


def to_off(value):
    pairs = []
    for d in range(DEVICES):
        region = d // 2
        other = region + (1 if region % 2 else -1)
        if 0 <= other < DEVICES // 2:
            pairs.append((d, 2 * other + (1 - d % 2)))
    return lax.ppermute(value, AXES, pairs)


def spread(value, axes, count):
    copies = jnp.broadcast_to(value[None], (count,) + value.shape)
    return lax.all_to_all(copies, axes, 0, 0, tiled=True).reshape(-1, value.shape[-1])


def to_x(value, flip):
    return lax.ppermute(value, "x", [(x, x ^ flip) for x in range(N_X)])


def collect_x(parts):
    total = parts[0].astype(F32)
    for j in range(1, N_X):
        total = total + to_x(parts[j], j).astype(F32)
    return total.astype(BF)


def hub_of(position):
    low = position & 7
    core = (position >> 7) & 1
    mid = (position >> 3) & 15
    high = position >> 8
    return low | (core << 3) | (mid << 4) | (high << 8)


def dot(a, b, ca=1, cb=0):
    return lax.dot_general(a, b, (((ca,), (cb,)), ((), ())), preferred_element_type=F32)


def prepare(
    dest, source, count, side, core_ref, order_col, features_hbm, self_weight_hbm, tiles_hbm,
    near, own_pre,
    cells, hub_cells, pick, features, self_weight, tiles, sems,
):
    copies = [
        pltpu.make_async_copy(*refs, sems.at[n])
        for n, refs in enumerate(((tiles_hbm, tiles), (features_hbm, features), (self_weight_hbm, self_weight)))
    ]
    for copy in copies:
        copy.start()
    live, flip, core = count[0], 4 * side[0], core_ref[0]
    for r in range(2):
        for x in range(N_X):
            ids = hub_of(lax.broadcasted_iota(jnp.int32, (BLK, BLK), 1) + (2 * x + (core ^ r)) * BLK)
            for j in range(8):
                rows = pl.ds(j * BLK, BLK)
                pick[r, rows, pl.ds(x * BLK, BLK)] = (order_col[rows, :] == ids).astype(F32).astype(BF)
    cells[...] = jnp.zeros_like(cells)
    for copy in copies:
        copy.wait()
    low = (16, 0, 8, 24)
    base = (2 + 2 * core, 4 - 2 * core, 0, 6)

    def add(m, carry):
        for cat in range(4):
            k = 4 * m + cat
            block = source[0, k] - low[cat]
            if cat < 3:
                block = block ^ flip
            rows = pl.ds(pl.multiple_of(dest[0, k] * BLK, BLK), BLK)
            cells[base[cat] + (block >> 2), block & 3, rows, :] += jnp.where(k < live, tiles[k].astype(F32), 0.0)
        return carry

    lax.fori_loop(0, (live + 3) // 4, add, 0)
    for p in range(8):
        for j in range(4):
            cell = cells[p, j].astype(BF)
            if p < 6:
                near[p, :, pl.ds(j * BLK, BLK)] = cell
            else:
                hub_cells[:, pl.ds(((p - 6) * 4 + j) * BLK, BLK)] = cell
    for r in range(2):
        near[6 + r] = dot(hub_cells[...], pick[r]).astype(BF)
    own_pre[...] = dot(features[...], self_weight[...])


def put(r, j, keep, send, value):
    if r == 0:
        keep[j][...] = value.astype(BF)
    else:
        send[pl.ds(j * BLK, BLK), :] = value.astype(BF)


def ahead(
    core_ref, x_ref, near_hbm,
    features, own_other, on_same, on_other, off_same_low, off_same_high, off_other, hubs, hubs_there,
    own_pre_hbm, neigh_weight_hbm, cotangent_hbm,
    embedding, slope, *rest,
):
    keep, send = rest[:N_X], rest[N_X]
    near, table, sums, left, own_pre, neigh_weight, cotangent, sems = rest[N_X + 1:]
    core = core_ref[0]
    half = 2 * BLK

    def load(n, source_ref, target):
        copy = pltpu.make_async_copy(source_ref, target, sems.at[n])
        copy.start()
        return copy

    waits = []
    n = 0
    for p, refs in enumerate((
        (features,), (own_other,), (on_same,), (on_other,), (off_same_low, off_same_high), (off_other,),
        (hubs,), (hubs_there,),
    )):
        waits.append([load(n, near_hbm.at[p], near.at[p])])
        n += 1
        for i, ref in enumerate(refs):
            waits[-1].append(load(n, ref, table.at[p, pl.ds(i * half, ref.shape[0])]))
            n += 1
    last = [
        load(n + i, *refs)
        for i, refs in enumerate(((own_pre_hbm, own_pre), (neigh_weight_hbm, neigh_weight), (cotangent_hbm, cotangent)))
    ]
    for p in range(8):
        for copy in waits[p]:
            copy.wait()
        value = dot(near[p], table[p])
        sums[...] = value if p == 0 else sums[...] + value
    for copy in last:
        copy.wait()
    left[0] = table[0]
    for b in range(4):
        rows = pl.ds(b * BLK, BLK)
        aggregate = sums[rows, :].astype(BF)
        left[1, rows, :] = aggregate
        pre = own_pre[rows, :] + dot(aggregate, neigh_weight[...])
        sig = jax.nn.sigmoid(pre)
        embedding[rows, :] = (pre * sig).astype(BF)
        slope[rows, :] = (cotangent[rows, :].astype(F32) * (sig * (1.0 + pre * (1.0 - sig)))).astype(BF)
    for r in range(2):
        for j in range(N_X):
            x = x_ref[0] ^ j
            first = (2 * (x & 1) + (core ^ r)) * BLK
            columns = pl.ds(pl.multiple_of(first, BLK), BLK)
            put(r, j, keep, send, dot(left[x >> 1, :, columns], slope[...], 0, 0))


def behind(
    x_ref, near_hbm, slope_hbm, self_weight_hbm, neigh_weight_hbm,
    own_grad, g_own_other, g_on_same, g_on_other, g_off_same, g_off_other, *rest,
):
    keep, send = rest[:N_X], rest[N_X]
    near, back, slope, self_weight, neigh_weight, sems = rest[N_X + 1:]
    first = [
        pltpu.make_async_copy(*refs, sems.at[n])
        for n, refs in enumerate((
            (slope_hbm, slope), (neigh_weight_hbm, neigh_weight), (self_weight_hbm, self_weight),
        ))
    ]
    order = (6, 7, 1, 2, 3, 4, 5, 0)
    second = [pltpu.make_async_copy(near_hbm.at[p], near.at[p], sems.at[3 + p]) for p in range(8)]
    for copy in first + [second[p] for p in order]:
        copy.start()
    for copy in first:
        copy.wait()
    back[...] = dot(slope[...], neigh_weight[...], 1, 1).astype(BF)
    outs = (None, g_own_other, g_on_same, g_on_other, g_off_same, g_off_other)
    for p in order:
        second[p].wait()
        if p >= 6:
            for j in range(N_X):
                columns = pl.ds(pl.multiple_of((x_ref[0] ^ j) * BLK, BLK), BLK)
                put(p - 6, j, keep, send, dot(near[p, :, columns], back[...], 0, 0))
        elif p > 0:
            outs[p][...] = dot(near[p], back[...], 0, 0).astype(BF)
        else:
            own_grad[...] = dot(near[p], back[...], 0, 0) + dot(slope[...], self_weight[...], 1, 1)


def join_cores(parts):
    theirs = to_core(parts[-1])
    return [plus(mine, theirs[j * BLK:(j + 1) * BLK]) for j, mine in enumerate(parts[:-1])]


def plus(a, b):
    return (a.astype(F32) + b.astype(F32)).astype(BF)


def local(
    features,
    hub_features,
    hub_order,
    tile_values,
    tile_dest,
    tile_source,
    tile_count,
    self_weight,
    neighbour_weight,
    cotangent,
):
    rows, width = features.shape
    smem = pl.BlockSpec(memory_space=pltpu.SMEM)
    vmem = pl.BlockSpec(memory_space=pltpu.VMEM)
    hbm = pl.BlockSpec(memory_space=pl.ANY)
    shape = jax.ShapeDtypeStruct
    wide = shape((rows, width), BF)
    part = shape((BLK, width), BF)
    params = pltpu.CompilerParams(vmem_limit_bytes=56 * 1024 * 1024)
    side = lax.axis_index("yl").astype(jnp.int32).reshape(1)
    core = lax.axis_index("core").astype(jnp.int32).reshape(1)
    x = lax.axis_index("x").astype(jnp.int32).reshape(1)
    barrier = lax.optimization_barrier

    own_other = to_side(features)
    off_other = to_off(features)
    on_same = to_core(features)
    hubs = spread(hub_features, WIDE, N_WIDE)
    pieces = shape((8, rows, width), BF)
    near, own_pre = pl.pallas_call(
        prepare,
        in_specs=[smem] * 5 + [vmem] + [hbm] * 3,
        out_specs=[vmem] * 2,
        out_shape=[pieces, shape((rows, width), F32)],
        scratch_shapes=[
            pltpu.VMEM((8, 4, rows, BLK), F32),
            pltpu.VMEM((rows, 8 * BLK), BF),
            pltpu.VMEM((2, 8 * BLK, 4 * BLK), BF),
            pltpu.VMEM((rows, width), BF),
            pltpu.VMEM((width, width), BF),
            pltpu.VMEM(tile_values.shape, BF),
            pltpu.SemaphoreType.DMA((3,)),
        ],
        compiler_params=params,
        cost_estimate=pl.CostEstimate(flops=13 * 10**8, bytes_accessed=9 * 10**6, transcendentals=0),
        name="prepare",
    )(tile_dest, tile_source, tile_count, side, core, hub_order.reshape(-1, 1), features, self_weight, tile_values)
    own_other, off_other, on_same, hubs, near, own_pre = barrier((own_other, off_other, on_same, hubs, near, own_pre))
    off_same_low = to_side(off_other[:rows // 2])
    off_same_high = to_off(own_other[rows // 2:])
    on_other = to_core(own_other)
    hubs = spread(hubs, ("x",), N_X)
    hubs, off_same_low, off_same_high, on_other = barrier((hubs, off_same_low, off_same_high, on_other))
    hubs_there = to_core(hubs)

    embedding, slope, *w = pl.pallas_call(
        ahead,
        in_specs=[smem] * 2 + [hbm] * 13,
        out_specs=[vmem] * (3 + N_X),
        out_shape=[wide, wide] + [part] * N_X + [wide],
        scratch_shapes=[
            pltpu.VMEM((8, rows, width), BF),
            pltpu.VMEM((8, rows, width), BF),
            pltpu.VMEM((rows, width), F32),
            pltpu.VMEM((2, rows, width), BF),
            pltpu.VMEM((rows, width), F32),
            pltpu.VMEM((width, width), BF),
            pltpu.VMEM((rows, width), BF),
            pltpu.SemaphoreType.DMA((20,)),
        ],
        compiler_params=params,
        cost_estimate=pl.CostEstimate(flops=3 * 10**9, bytes_accessed=12 * 10**6, transcendentals=0),
        name="ahead",
    )(
        core, x, near,
        features, own_other, on_same, on_other, off_same_low, off_same_high, off_other, hubs, hubs_there,
        own_pre, neighbour_weight, cotangent,
    )
    w = join_cores(w)
    w, slope = barrier((w, slope))

    own_grad, g_own_other, g_on_same, g_on_other, g_off_same, g_off_other, *h = pl.pallas_call(
        behind,
        in_specs=[smem] + [hbm] * 4,
        out_specs=[vmem] * (7 + N_X),
        out_shape=[shape((rows, width), F32)] + [wide] * 5 + [part] * N_X + [wide],
        scratch_shapes=[
            pltpu.VMEM((8, rows, width), BF),
            pltpu.VMEM((rows, width), BF),
            pltpu.VMEM((rows, width), BF),
            pltpu.VMEM((width, width), BF),
            pltpu.VMEM((width, width), BF),
            pltpu.SemaphoreType.DMA((11,)),
        ],
        compiler_params=params,
        cost_estimate=pl.CostEstimate(flops=3 * 10**9, bytes_accessed=10 * 10**6, transcendentals=0),
        name="behind",
    )(x, near, slope, self_weight, neighbour_weight)

    w = collect_x(w)
    g = (g_own_other, g_on_same, g_on_other, g_off_same, g_off_other)
    w, h, g = barrier((w, h, g))
    g_own_other, g_on_same, g_on_other, g_off_same, g_off_other = g
    w, h = barrier((w, join_cores(h)))

    w = lax.all_to_all(w.reshape(N_WIDE, 4, width), WIDE, 0, 0, tiled=True).astype(F32).sum(0).astype(BF)
    h = collect_x(h)
    r_on_other = to_core(g_on_other)
    r_off_same = to_side(g_off_same)
    r_on_same = to_core(g_on_same)
    s_side = plus(g_own_other, r_on_other)
    s_off = plus(g_off_other, r_off_same)

    w, h, s_side, s_off, r_on_same = barrier((w, h, s_side, s_off, r_on_same))
    r_side = to_side(s_side)
    r_off = to_off(s_off)
    both = jnp.concatenate([jnp.broadcast_to(w[None], (N_WIDE, 4, width)), h.reshape(N_WIDE, 4, width)], 1)
    both = lax.all_to_all(both, WIDE, 0, 0, tiled=True)
    w = both[:, :4].reshape(BLK, width)
    hub_gradient = both[:, 4:].astype(F32).sum(0)
    w = spread(w, ("x",), N_X)
    w, r_side, r_off = barrier((w, r_side, r_off))
    there = to_core(w)
    feature_gradient = own_grad + r_on_same.astype(F32) + r_side.astype(F32) + r_off.astype(F32)
    first = core[0] == 0
    pair = (N_X, 1, BLK, width)
    low, high = jnp.where(first, w, there).reshape(pair), jnp.where(first, there, w).reshape(pair)
    weights = jnp.concatenate([low, high], 1).reshape(2, width, width).astype(F32)
    return embedding, feature_gradient, hub_gradient, weights[0], weights[1]


def solution(mesh):
    fine = Mesh(mesh.devices.reshape(EXTENT), AXES)
    split = P(AXES)
    in_specs = (split, split, P(), split, split, split, split, P(), P(), split)
    out_specs = (split, split, split, P(), P())
    return jax.shard_map(local, mesh=fine, in_specs=in_specs, out_specs=out_specs, check_vma=False)
```

time: 146 us -> 139 us (0.952)
  starting transfers between devices: 77 us -> 70 us
    ppermute x6, starting transfers between devices: 19.2 us -> 10.7 us  [to_x(): return lax.ppermute(value, 'x', [(x, x ^ flip) for x in range(N_X)])]
    all_to_all x1, starting transfers between devices: 4.56 us -> 8.15 us  [local(): lax.all_to_all(w.reshape(N_WIDE, 4, width), WIDE, 0, 0, tiled=True)]
    ppermute x8, starting transfers between devices: 11.6 us -> 8.83 us  [to_core(): return lax.ppermute(value, AXES, [(d, d ^ 2) for d in range(DEVICES)])]
    all_to_all x3, waiting for transfers between devices: 4.4 us -> 1.75 us  [spread(): lax.all_to_all(copies, axes, 0, 0, tiled=True).reshape(-1, value.shape[-1])]
    ppermute x6, waiting for transfers between devices: 2.58 us -> 4.99 us  [to_x(): return lax.ppermute(value, 'x', [(x, x ^ flip) for x in range(N_X)])]
  transfers between devices with their start and end apart: 26 -> 26, of which waited for: 11 -> 10; matrix products, arithmetic and copies ran while one was open for 8% -> 9% of each run, Pallas kernels for 10% -> 11%
where the time goes in v3:
time: 139 us; the launch traced here: 138 us
  starting transfers between devices  70 us (50%)
  waiting for transfers between devices  28.2 us (20%)
  Pallas kernels  21.1 us (15%)
  other arithmetic  8.8 us (6%)
  local copies, waits for them, and re-layouts  8.76 us (6%)
  between operations  1.67 us (1%)
    all_to_all x3, starting transfers between devices, spread(): lax.all_to_all(copies, axes, 0, 0, tiled=True).reshape(-1, value.shape[-1])  17 us
    ppermute x3, starting transfers between devices, to_off(): return lax.ppermute(value, AXES, pairs)  15.3 us
    ppermute x3, waiting for transfers between devices, to_off(): return lax.ppermute(value, AXES, pairs)  11.1 us
    ppermute x6, starting transfers between devices, to_x(): return lax.ppermute(value, 'x', [(x, x ^ flip) for x in range(N_X)])  10.7 us
    ppermute x8, starting transfers between devices, to_core(): return lax.ppermute(value, AXES, [(d, d ^ 2) for d in range(DEVICES)])  8.83 us
    all_to_all x1, starting transfers between devices, local(): lax.all_to_all(w.reshape(N_WIDE, 4, width), WIDE, 0, 0, tiled=True)  8.15 us
    pallas_call x1, Pallas kernels, local(): pl.pallas_call(behind, in_specs=[smem] + [hbm] * 4, out_specs=[vmem] * (7...  7.37 us
    pallas_call x1, Pallas kernels, local(): pl.pallas_call(prepare, in_specs=[smem] * 5 + [vmem] + [hbm] * 3, out_spe...  7.34 us
  transfers between devices with their start and end apart: 26, of which 10 were waited for; matrix products, arithmetic and copies ran while one was open for 9% of the time, Pallas kernels for 11%

profile of v3, /device:TPU:1, one launch (start us, length us, event | category | flops | bytes accessed | tf_op | source)
XLA Modules:
  0.0 138.4 jit_solution(1009821359920687660)
XLA Ops:
  0.6 2.2 %collective-permute-start = (bf16[512,512]{1,0:T(8,128)(2,1)}, bf16[512,512]{1,0:T(8,128)(2,1)S(1)}, u32[]{:S(2)}, u32[]{:S(2)}) collective-permute-start(bf16[512,512]{1,0:T(8,128)(2,1)} %features.1), channel_id=1, source_target_pairs={{0,1},{1,0},{2,3},{3,2},{4,5},{5,4},{6,7},{7,6},{8,9},{9,8},{10,11... | collective-permute-start | bytes 1572872 | tf_op jit(solution)/shard_map/ppermute | solution.py:26
  2.8 4.6 %collective-permute-start.1 = (bf16[512,512]{1,0:T(8,128)(2,1)}, bf16[512,512]{1,0:T(8,128)(2,1)S(1)}, u32[]{:S(2)}, u32[]{:S(2)}) collective-permute-start(bf16[512,512]{1,0:T(8,128)(2,1)} %features.1), channel_id=1, source_target_pairs={{2,5},{3,4},{4,3},{5,2},{6,9},{7,8},{8,7},{9,6},{10,13},{11,12},{1... | collective-permute-start | bytes 1572872 | tf_op jit(solution)/shard_map/ppermute | solution.py:36
  7.6 1.4 broadcast_in_dim.10
  9.0 9.5 %all-to-all-start = ((bf16[32,4,512]{2,1,0:T(4,128)(2,1)}), bf16[32,4,512]{2,1,0:T(4,128)(2,1)S(1)}, u32[]{:S(2)}, u32[]{:S(2)}) async-start(bf16[32,4,512]{2,1,0:T(4,128)(2,1)} %broadcast_in_dim.10), calls=%async_computation | async-start | bytes 262144 | tf_op jit(solution)/shard_map/all_to_all | solution.py:41
  18.5 1.7 %copy.15.order_col = s32[1024,1]{1,0:T(8,128)} copy(s32[1024,1]{0,1:T(1,128)} %bitcast.18) | data formatting | bytes 8192 | tf_op jit(solution)/shard_map/reshape | solution.py:264
  20.9 7.3 %prepare.1 = (bf16[8,512,512]{2,1,0:T(8,128)(2,1)}, f32[512,512]{1,0:T(8,128)}) custom-call(s32[1,64]{1,0:T(1,128)} %dest.1, s32[1,64]{1,0:T(1,128)} %source.1, s32[1]{0:T(128)S(6)} %copy.16.count, s32[1]{0:T(128)} %bitcast.2.side, s32[1]{0:T(128)} %bitcast.core_ref, s32[1024,1]{1,0:T(8,128)} %copy.15.order_col, bf16[512,512]{1,0:T(8,128)(2,1)} %features.1, ...), custom_call_target="tpu_custom_call" | custom-call | flops 1300000000 | bytes 9000000 | tf_op jit(solution)/shard_map/prepare/pallas_call | solution.py:247
  28.3 1.8 %collective-permute-start.5 = (bf16[512,512]{1,0:T(8,128)(2,1)S(1)}, bf16[512,512]{1,0:T(8,128)(2,1)S(1)}, u32[]{:S(2)}, u32[]{:S(2)}) collective-permute-start(bf16[512,512]{1,0:T(8,128)(2,1)S(1)} %collective-permute-done.own_other), channel_id=1, source_target_pairs={{0,2},{1,3},{2,0},{3,1},{4,6},{5,7},{6,4},{7,5},{8,10},{9,11},{10,... | collective-permute-start | bytes 1572872 | tf_op jit(solution)/shard_map/ppermute | solution.py:22
  31.0 4.0 %all-to-all-start.1 = ((bf16[4,128,512]{2,1,0:T(8,128)(2,1)}), bf16[4,128,512]{2,1,0:T(8,128)(2,1)S(1)}, u32[]{:S(2)}, u32[]{:S(2)}) async-start(bf16[4,128,512]{2,1,0:T(8,128)(2,1)} %broadcast_in_dim.11), calls=%async_computation.1 | async-start | bytes 1048576 | tf_op jit(solution)/shard_map/all_to_all | solution.py:41
  35.0 3.8 %collective-permute-start.4 = (bf16[256,512]{1,0:T(8,128)(2,1)S(1)}, bf16[256,512]{1,0:T(8,128)(2,1)S(1)}, u32[]{:S(2)}, u32[]{:S(2)}) collective-permute-start(bf16[256,512]{1,0:T(8,128)(2,1)S(1)} %slice.45), channel_id=1, source_target_pairs={{2,5},{3,4},{4,3},{5,2},{6,9},{7,8},{8,7},{9,6},{10,13},{11,12},{1... | collective-permute-start | bytes 786440 | tf_op jit(solution)/shard_map/ppermute | solution.py:36
  39.0 5.9 %collective-permute-done.4.off_same_high = bf16[256,512]{1,0:T(8,128)(2,1)S(1)} collective-permute-done((bf16[256,512]{1,0:T(8,128)(2,1)S(1)}, bf16[256,512]{1,0:T(8,128)(2,1)S(1)}, u32[]{:S(2)}, u32[]{:S(2)}) %collective-permute-start.4) | collective-permute-done | bytes 262176 | tf_op jit(solution)/shard_map/ppermute | solution.py:36
  45.8 1.9 %collective-permute-done.6.hubs_there = bf16[512,512]{1,0:T(8,128)(2,1)S(1)} collective-permute-done((bf16[512,512]{1,0:T(8,128)(2,1)S(1)}, bf16[512,512]{1,0:T(8,128)(2,1)S(1)}, u32[]{:S(2)}, u32[]{:S(2)}) %collective-permute-start.6) | collective-permute-done | bytes 524320 | tf_op jit(solution)/shard_map/ppermute | solution.py:22
  48.5 6.4 %ahead.1 = (bf16[512,512]{1,0:T(8,128)(2,1)}, bf16[512,512]{1,0:T(8,128)(2,1)}, bf16[128,512]{1,0:T(8,128)(2,1)}, bf16[128,512]{1,0:T(8,128)(2,1)}, bf16[128,512...) custom-call(s32[1]{0:T(128)} %bitcast.core_ref, s32[1]{0:T(128)} %bitcast.1.x_ref, ...), custom_call_target="tpu_custom_call" | custom-call | flops 3000000000 | bytes 12000000 | tf_op jit(solution)/shard_map/ahead/pallas_call | solution.py:273
  55.1 2.0 %collective-permute-done.7 = bf16[512,512]{1,0:T(8,128)(2,1)S(1)} collective-permute-done((bf16[512,512]{1,0:T(8,128)(2,1)}, bf16[512,512]{1,0:T(8,128)(2,1)S(1)}, u32[]{:S(2)}, u32[]{:S(2)}) %collective-permute-start.7) | collective-permute-done | bytes 524320 | tf_op jit(solution)/shard_map/ppermute | solution.py:22
  57.1 1.2 add_convert_fusion.8
  58.3 5.3 %collective-permute-start.10 = (bf16[128,512]{1,0:T(8,128)(2,1)S(1)}, bf16[128,512]{1,0:T(8,128)(2,1)S(1)}, u32[]{:S(2)}, u32[]{:S(2)}) collective-permute-start(bf16[128,512]{1,0:T(8,128)(2,1)S(1)} %get-tuple-element.88), channel_id=1, source_target_pairs={{0,192},{64,128},{128,64},{192,0},{1,193},{65,129},{129,65},{193,1... | collective-permute-start | bytes 393224 | tf_op jit(solution)/shard_map/ppermute | solution.py:45
  63.5 1.3 collective-permute-start.9
  64.8 7.4 %behind.1 = (f32[512,512]{1,0:T(8,128)}, bf16[512,512]{1,0:T(8,128)(2,1)}, bf16[512,512]{1,0:T(8,128)(2,1)}, bf16[512,512]{1,0:T(8,128)(2,1)}, bf16[512,512]{1,0...) custom-call(s32[1]{0:T(128)} %bitcast.1.x_ref, ...), custom_call_target="tpu_custom_call" | custom-call | flops 3000000000 | bytes 10000000 | tf_op jit(solution)/shard_map/behind/pallas_call | solution.py:299
  75.2 1.9 %add_convert_fusion.3 = (bf16[128,512]{1,0:T(8,128)(2,1)S(1)}, bf16[128,512]{1,0:T(8,128)(2,1)}, bf16[128,512]{1,0:T(8,128)(2,1)}, bf16[128,512]{1,0:T(8,128)(2,1)S(1)}) fusion(bf16[128,512]{1,0:T(8,128)(2,1)} %get-tuple-element.104, bf16[512,512]{1,0:T(8,128)(2,1)S(1)} %collective-permute-done.11, bf16[128,512]{1,0:T(8,128)(2,1)} %get-tuple-element.103, ...), kind=kLoop, calls=%fused_computation.9 | loop fusion | flops 1048576 | bytes 1572864 | tf_op jit(solution)/shard_map/convert_element_type | solution.py:214
  77.5 3.6 %collective-permute-start.13 = (bf16[128,512]{1,0:T(8,128)(2,1)}, bf16[128,512]{1,0:T(8,128)(2,1)}, u32[]{:S(2)}, u32[]{:S(2)}) collective-permute-start(bf16[128,512]{1,0:T(8,128)(2,1)} %get-tuple-element.108), channel_id=1, source_target_pairs={{0,128},{64,192},{128,0},{192,64},{1,129},{65,193},{129,1},{193,65... | collective-permute-start | bytes 393224 | tf_op jit(solution)/shard_map/ppermute | solution.py:45
  81.8 8.2 %all-to-all-start.2 = ((bf16[32,4,512]{2,1,0:T(4,128)(2,1)}), bf16[32,4,512]{2,1,0:T(4,128)(2,1)S(1)}, u32[]{:S(2)}, u32[]{:S(2)}) async-start(bf16[32,4,512]{2,1,0:T(4,128)(2,1)} %reshape.59), calls=%async_computation.2 | async-start | bytes 262144 | tf_op jit(solution)/shard_map/all_to_all | solution.py:323
  90.4 5.0 %collective-permute-done.14 = bf16[128,512]{1,0:T(8,128)(2,1)S(1)} collective-permute-done((bf16[128,512]{1,0:T(8,128)(2,1)S(1)}, bf16[128,512]{1,0:T(8,128)(2,1)S(1)}, u32[]{:S(2)}, u32[]{:S(2)}) %collective-permute-start.14) | collective-permute-done | bytes 131104 | tf_op jit(solution)/shard_map/ppermute | solution.py:45
  96.5 2.9 %all-to-all-done.2 = bf16[32,4,512]{2,1,0:T(4,128)(2,1)S(1)} async-done(((bf16[32,4,512]{2,1,0:T(4,128)(2,1)}), bf16[32,4,512]{2,1,0:T(4,128)(2,1)S(1)}, u32[]{:S(2)}, u32[]{:S(2)}) %all-to-all-start.2) | async-done | bytes 131104 | tf_op jit(solution)/shard_map/all_to_all | solution.py:323
  100.3 6.2 %all-to-all-start.3 = ((bf16[32,8,512]{2,1,0:T(8,128)(2,1)}), bf16[32,8,512]{2,1,0:T(8,128)(2,1)S(1)}, u32[]{:S(2)}, u32[]{:S(2)}) async-start(bf16[32,8,512]{2,1,0:T(8,128)(2,1)} %pad_maximum_fusion), calls=%async_computation.3 | async-start | bytes 524288 | tf_op jit(solution)/shard_map/all_to_all | solution.py:335
  106.6 1.3 collective-permute-start.18
  107.9 6.9 %collective-permute-start.19 = (bf16[512,512]{1,0:T(8,128)(2,1)S(1)}, bf16[512,512]{1,0:T(8,128)(2,1)}, u32[]{:S(2)}, u32[]{:S(2)}) collective-permute-start(bf16[512,512]{1,0:T(8,128)(2,1)S(1)} %add_convert_fusion), channel_id=1, source_target_pairs={{2,5},{3,4},{4,3},{5,2},{6,9},{7,8},{8,7},{9,6},{10,13},{11,12},{1... | collective-permute-start | bytes 1572872 | tf_op jit(solution)/shard_map/ppermute | solution.py:36
  114.8 2.3 %all-to-all-done.3 = bf16[32,8,512]{2,1,0:T(8,128)(2,1)S(1)} async-done(((bf16[32,8,512]{2,1,0:T(8,128)(2,1)}), bf16[32,8,512]{2,1,0:T(8,128)(2,1)S(1)}, u32[]{:S(2)}, u32[]{:S(2)}) %all-to-all-start.3) | async-done | bytes 262176 | tf_op jit(solution)/shard_map/all_to_all | solution.py:335
  118.0 3.5 %all-to-all-start.4 = ((bf16[4,128,512]{2,1,0:T(8,128)(2,1)}), bf16[4,128,512]{2,1,0:T(8,128)(2,1)S(1)}, u32[]{:S(2)}, u32[]{:S(2)}) async-start(bf16[4,128,512]{2,1,0:T(8,128)(2,1)} %broadcast_in_dim.14), calls=%async_computation.4 | async-start | bytes 1048576 | tf_op jit(solution)/shard_map/all_to_all | solution.py:41
  121.5 5.1 %collective-permute-done.19 = bf16[512,512]{1,0:T(8,128)(2,1)} collective-permute-done((bf16[512,512]{1,0:T(8,128)(2,1)S(1)}, bf16[512,512]{1,0:T(8,128)(2,1)}, u32[]{:S(2)}, u32[]{:S(2)}) %collective-permute-start.19) | collective-permute-done | bytes 524320 | tf_op jit(solution)/shard_map/ppermute | solution.py:36
  126.7 1.7 %all-to-all-done.4 = bf16[4,128,512]{2,1,0:T(8,128)(2,1)S(1)} async-done(((bf16[4,128,512]{2,1,0:T(8,128)(2,1)}), bf16[4,128,512]{2,1,0:T(8,128)(2,1)S(1)}, u32[]{:S(2)}, u32[]{:S(2)}) %all-to-all-start.4) | async-done | bytes 524320 | tf_op jit(solution)/shard_map/all_to_all | solution.py:41
  128.4 5.1 %collective-permute-start.20 = (bf16[512,512]{1,0:T(8,128)(2,1)S(1)}, bf16[512,512]{1,0:T(8,128)(2,1)S(1)}, u32[]{:S(2)}, u32[]{:S(2)}) collective-permute-start(bf16[512,512]{1,0:T(8,128)(2,1)S(1)} %bitcast.10), channel_id=1, source_target_pairs={{0,2},{1,3},{2,0},{3,1},{4,6},{5,7},{6,4},{7,5},{8,10},{9,11},{10,... | collective-permute-start | bytes 1572872 | tf_op jit(solution)/shard_map/ppermute | solution.py:22
  134.2 2.4 %convert_add_fusion = f32[512,512]{1,0:T(8,128)} fusion(bf16[512,512]{1,0:T(8,128)(2,1)} %collective-permute-done.19, bf16[512,512]{1,0:T(8,128)(2,1)} %collective-permute-done.18, f32[512,512]{1,0:T(8,128)S(1)} %copy-done, bf16[512,512]{1,0:T(8,128)(2,1)S(1)} %collective-permute-done.17), kind=kLoop, calls=%fused_computation.1 | loop fusion | flops 1572864 | bytes 3670016 | tf_op jit(solution)/shard_map/add | solution.py:341
  136.9 1.6 %fusion = (f32[2,2,128,512]{3,2,1,0:T(8,128)}, f32[2,2,128,512]{3,2,1,0:T(8,128)}) fusion(f32[4,2,128,512]{3,2,1,0:T(8,128)S(1)} %maximum_convert_fusion), kind=kLoop, calls=%fused_computation.18 | loop fusion | bytes 4194304 | tf_op jit(solution)/shard_map/slice | solution.py:346
  (70 shorter events, 11.3 us)
Async XLA Ops:
  0.6 27.6 %collective-permute-start = (bf16[512,512]{1,0:T(8,128)(2,1)}, bf16[512,512]{1,0:T(8,128)(2,1)S(1)}, u32[]{:S(2)}, u32[]{:S(2)}) collective-permute-start(bf16[512,512]{1,0:T(8,128)(2,1)} %features.1), channel_id=1, source_target_pairs={{0,1},{1,0},{2,3},{3,2},{4,5},{5,4},{6,7},{7,6},{8,9},{9,8},{10,11... | collective-permute-start | bytes 1572872 | tf_op jit(solution)/shard_map/ppermute | solution.py:26
  2.8 25.5 %collective-permute-start.1 = (bf16[512,512]{1,0:T(8,128)(2,1)}, bf16[512,512]{1,0:T(8,128)(2,1)S(1)}, u32[]{:S(2)}, u32[]{:S(2)}) collective-permute-start(bf16[512,512]{1,0:T(8,128)(2,1)} %features.1), channel_id=1, source_target_pairs={{2,5},{3,4},{4,3},{5,2},{6,9},{7,8},{8,7},{9,6},{10,13},{11,12},{1... | collective-permute-start | bytes 1572872 | tf_op jit(solution)/shard_map/ppermute | solution.py:36
  7.5 20.8 %collective-permute-start.2 = (bf16[512,512]{1,0:T(8,128)(2,1)}, bf16[512,512]{1,0:T(8,128)(2,1)S(1)}, u32[]{:S(2)}, u32[]{:S(2)}) collective-permute-start(bf16[512,512]{1,0:T(8,128)(2,1)} %features.1), channel_id=1, source_target_pairs={{0,2},{1,3},{2,0},{3,1},{4,6},{5,7},{6,4},{7,5},{8,10},{9,11},{10,... | collective-permute-start | bytes 1572872 | tf_op jit(solution)/shard_map/ppermute | solution.py:22
  9.0 19.3 %all-to-all-start = ((bf16[32,4,512]{2,1,0:T(4,128)(2,1)}), bf16[32,4,512]{2,1,0:T(4,128)(2,1)S(1)}, u32[]{:S(2)}, u32[]{:S(2)}) async-start(bf16[32,4,512]{2,1,0:T(4,128)(2,1)} %broadcast_in_dim.10), calls=%async_computation | async-start | bytes 262144 | tf_op jit(solution)/shard_map/all_to_all | solution.py:41
  28.3 19.4 %copy-start.4 = (bf16[512,512]{1,0:T(8,128)(2,1)}, bf16[512,512]{1,0:T(8,128)(2,1)S(1)}, u32[]{:S(2)}) copy-start(bf16[512,512]{1,0:T(8,128)(2,1)S(1)} %collective-permute-done.own_other) | copy-start | bytes 1572868
  28.3 19.4 %copy-start.5 = (bf16[512,512]{1,0:T(8,128)(2,1)}, bf16[512,512]{1,0:T(8,128)(2,1)S(1)}, u32[]{:S(2)}) copy-start(bf16[512,512]{1,0:T(8,128)(2,1)S(1)} %collective-permute-done.1.off_other) | copy-start | bytes 1572868
  28.3 19.4 %copy-start.6 = (bf16[512,512]{1,0:T(8,128)(2,1)}, bf16[512,512]{1,0:T(8,128)(2,1)S(1)}, u32[]{:S(2)}) copy-start(bf16[512,512]{1,0:T(8,128)(2,1)S(1)} %collective-permute-done.2.on_same) | copy-start | bytes 1572868
  28.3 16.7 %collective-permute-start.5 = (bf16[512,512]{1,0:T(8,128)(2,1)S(1)}, bf16[512,512]{1,0:T(8,128)(2,1)S(1)}, u32[]{:S(2)}, u32[]{:S(2)}) collective-permute-start(bf16[512,512]{1,0:T(8,128)(2,1)S(1)} %collective-permute-done.own_other), channel_id=1, source_target_pairs={{0,2},{1,3},{2,0},{3,1},{4,6},{5,7},{6,4},{7,5},{8,10},{9,11},{10,... | collective-permute-start | bytes 1572872 | tf_op jit(solution)/shard_map/ppermute | solution.py:22
  31.0 14.1 %all-to-all-start.1 = ((bf16[4,128,512]{2,1,0:T(8,128)(2,1)}), bf16[4,128,512]{2,1,0:T(8,128)(2,1)S(1)}, u32[]{:S(2)}, u32[]{:S(2)}) async-start(bf16[4,128,512]{2,1,0:T(8,128)(2,1)} %broadcast_in_dim.11), calls=%async_computation.1 | async-start | bytes 1048576 | tf_op jit(solution)/shard_map/all_to_all | solution.py:41
  35.0 9.9 %collective-permute-start.4 = (bf16[256,512]{1,0:T(8,128)(2,1)S(1)}, bf16[256,512]{1,0:T(8,128)(2,1)S(1)}, u32[]{:S(2)}, u32[]{:S(2)}) collective-permute-start(bf16[256,512]{1,0:T(8,128)(2,1)S(1)} %slice.45), channel_id=1, source_target_pairs={{2,5},{3,4},{4,3},{5,2},{6,9},{7,8},{8,7},{9,6},{10,13},{11,12},{1... | collective-permute-start | bytes 786440 | tf_op jit(solution)/shard_map/ppermute | solution.py:36
  38.8 6.2 %collective-permute-start.3 = (bf16[256,512]{1,0:T(8,128)(2,1)S(1)}, bf16[256,512]{1,0:T(8,128)(2,1)S(1)}, u32[]{:S(2)}, u32[]{:S(2)}) collective-permute-start(bf16[256,512]{1,0:T(8,128)(2,1)S(1)} %slice.44), channel_id=1, source_target_pairs={{0,1},{1,0},{2,3},{3,2},{4,5},{5,4},{6,7},{7,6},{8,9},{9,8},{10,11... | collective-permute-start | bytes 786440 | tf_op jit(solution)/shard_map/ppermute | solution.py:26
  45.8 1.9 %collective-permute-start.6 = (bf16[512,512]{1,0:T(8,128)(2,1)S(1)}, bf16[512,512]{1,0:T(8,128)(2,1)S(1)}, u32[]{:S(2)}, u32[]{:S(2)}) collective-permute-start(bf16[512,512]{1,0:T(8,128)(2,1)S(1)} %bitcast.16), channel_id=1, source_target_pairs={{0,2},{1,3},{2,0},{3,1},{4,6},{5,7},{6,4},{7,5},{8,10},{9,11},{10,... | collective-permute-start | bytes 1572872 | tf_op jit(solution)/shard_map/ppermute | solution.py:22
  54.8 2.2 %collective-permute-start.7 = (bf16[512,512]{1,0:T(8,128)(2,1)}, bf16[512,512]{1,0:T(8,128)(2,1)S(1)}, u32[]{:S(2)}, u32[]{:S(2)}) collective-permute-start(bf16[512,512]{1,0:T(8,128)(2,1)} %get-tuple-element.78), channel_id=1, source_target_pairs={{0,2},{1,3},{2,0},{3,1},{4,6},{5,7},{6,4},{7,5},{8,10},{9,11},{10,... | collective-permute-start | bytes 1572872 | tf_op jit(solution)/shard_map/ppermute | solution.py:22
  58.3 13.9 %collective-permute-start.10 = (bf16[128,512]{1,0:T(8,128)(2,1)S(1)}, bf16[128,512]{1,0:T(8,128)(2,1)S(1)}, u32[]{:S(2)}, u32[]{:S(2)}) collective-permute-start(bf16[128,512]{1,0:T(8,128)(2,1)S(1)} %get-tuple-element.88), channel_id=1, source_target_pairs={{0,192},{64,128},{128,64},{192,0},{1,193},{65,129},{129,65},{193,1... | collective-permute-start | bytes 393224 | tf_op jit(solution)/shard_map/ppermute | solution.py:45
  63.5 8.7 %collective-permute-start.8 = (bf16[128,512]{1,0:T(8,128)(2,1)S(1)}, bf16[128,512]{1,0:T(8,128)(2,1)S(1)}, u32[]{:S(2)}, u32[]{:S(2)}) collective-permute-start(bf16[128,512]{1,0:T(8,128)(2,1)S(1)} %get-tuple-element.86), channel_id=1, source_target_pairs={{0,64},{64,0},{128,192},{192,128},{1,65},{65,1},{129,193},{193,129... | collective-permute-start | bytes 393224 | tf_op jit(solution)/shard_map/ppermute | solution.py:45
  63.5 8.7 %collective-permute-start.9 = (bf16[128,512]{1,0:T(8,128)(2,1)S(1)}, bf16[128,512]{1,0:T(8,128)(2,1)S(1)}, u32[]{:S(2)}, u32[]{:S(2)}) collective-permute-start(bf16[128,512]{1,0:T(8,128)(2,1)S(1)} %get-tuple-element.87), channel_id=1, source_target_pairs={{0,128},{64,192},{128,0},{192,64},{1,129},{65,193},{129,1},{193,65... | collective-permute-start | bytes 393224 | tf_op jit(solution)/shard_map/ppermute | solution.py:45
  72.2 17.9 %copy-start.2 = (bf16[512,512]{1,0:T(8,128)(2,1)S(1)}, bf16[512,512]{1,0:T(8,128)(2,1)}, u32[]{:S(2)}) copy-start(bf16[512,512]{1,0:T(8,128)(2,1)} %get-tuple-element.112) | copy-start | bytes 1572868
  72.2 18.0 %copy-start.1 = (bf16[512,512]{1,0:T(8,128)(2,1)S(1)}, bf16[512,512]{1,0:T(8,128)(2,1)}, u32[]{:S(2)}) copy-start(bf16[512,512]{1,0:T(8,128)(2,1)} %get-tuple-element.110) | copy-start | bytes 1572868
  72.3 2.8 %collective-permute-start.11 = (bf16[512,512]{1,0:T(8,128)(2,1)}, bf16[512,512]{1,0:T(8,128)(2,1)S(1)}, u32[]{:S(2)}, u32[]{:S(2)}) collective-permute-start(bf16[512,512]{1,0:T(8,128)(2,1)} %get-tuple-element.101), channel_id=1, source_target_pairs={{0,2},{1,3},{2,0},{3,1},{4,6},{5,7},{6,4},{7,5},{8,10},{9,11},{10,... | collective-permute-start | bytes 1572872 | tf_op jit(solution)/shard_map/ppermute | solution.py:22
  73.4 16.6 %collective-permute-start.16 = (bf16[512,512]{1,0:T(8,128)(2,1)}, bf16[512,512]{1,0:T(8,128)(2,1)S(1)}, u32[]{:S(2)}, u32[]{:S(2)}) collective-permute-start(bf16[512,512]{1,0:T(8,128)(2,1)} %get-tuple-element.113), channel_id=1, source_target_pairs={{0,1},{1,0},{2,3},{3,2},{4,5},{5,4},{6,7},{7,6},{8,9},{9,8},{10,11... | collective-permute-start | bytes 1572872 | tf_op jit(solution)/shard_map/ppermute | solution.py:26
  73.5 16.8 %collective-permute-start.15 = (bf16[512,512]{1,0:T(8,128)(2,1)}, bf16[512,512]{1,0:T(8,128)(2,1)S(1)}, u32[]{:S(2)}, u32[]{:S(2)}) collective-permute-start(bf16[512,512]{1,0:T(8,128)(2,1)} %get-tuple-element.111), channel_id=1, source_target_pairs={{0,2},{1,3},{2,0},{3,1},{4,6},{5,7},{6,4},{7,5},{8,10},{9,11},{10,... | collective-permute-start | bytes 1572872 | tf_op jit(solution)/shard_map/ppermute | solution.py:22
  73.8 25.6 %collective-permute-start.17 = (bf16[512,512]{1,0:T(8,128)(2,1)}, bf16[512,512]{1,0:T(8,128)(2,1)S(1)}, u32[]{:S(2)}, u32[]{:S(2)}) collective-permute-start(bf16[512,512]{1,0:T(8,128)(2,1)} %get-tuple-element.114), channel_id=1, source_target_pairs={{0,2},{1,3},{2,0},{3,1},{4,6},{5,7},{6,4},{7,5},{8,10},{9,11},{10,... | collective-permute-start | bytes 1572872 | tf_op jit(solution)/shard_map/ppermute | solution.py:22
  77.1 13.3 %collective-permute-start.12 = (bf16[128,512]{1,0:T(8,128)(2,1)}, bf16[128,512]{1,0:T(8,128)(2,1)}, u32[]{:S(2)}, u32[]{:S(2)}) collective-permute-start(bf16[128,512]{1,0:T(8,128)(2,1)} %get-tuple-element.107), channel_id=1, source_target_pairs={{0,64},{64,0},{128,192},{192,128},{1,65},{65,1},{129,193},{193,129... | collective-permute-start | bytes 393224 | tf_op jit(solution)/shard_map/ppermute | solution.py:45
  77.5 12.9 %collective-permute-start.13 = (bf16[128,512]{1,0:T(8,128)(2,1)}, bf16[128,512]{1,0:T(8,128)(2,1)}, u32[]{:S(2)}, u32[]{:S(2)}) collective-permute-start(bf16[128,512]{1,0:T(8,128)(2,1)} %get-tuple-element.108), channel_id=1, source_target_pairs={{0,128},{64,192},{128,0},{192,64},{1,129},{65,193},{129,1},{193,65... | collective-permute-start | bytes 393224 | tf_op jit(solution)/shard_map/ppermute | solution.py:45
  81.8 17.5 %all-to-all-start.2 = ((bf16[32,4,512]{2,1,0:T(4,128)(2,1)}), bf16[32,4,512]{2,1,0:T(4,128)(2,1)S(1)}, u32[]{:S(2)}, u32[]{:S(2)}) async-start(bf16[32,4,512]{2,1,0:T(4,128)(2,1)} %reshape.59), calls=%async_computation.2 | async-start | bytes 262144 | tf_op jit(solution)/shard_map/all_to_all | solution.py:323
  90.0 5.4 %collective-permute-start.14 = (bf16[128,512]{1,0:T(8,128)(2,1)S(1)}, bf16[128,512]{1,0:T(8,128)(2,1)S(1)}, u32[]{:S(2)}, u32[]{:S(2)}) collective-permute-start(bf16[128,512]{1,0:T(8,128)(2,1)S(1)} %get-tuple-element.109), channel_id=1, source_target_pairs={{0,192},{64,128},{128,64},{192,0},{1,193},{65,129},{129,65},{193,1... | collective-permute-start | bytes 393224 | tf_op jit(solution)/shard_map/ppermute | solution.py:45
  96.4 37.8 %copy-start = (f32[512,512]{1,0:T(8,128)S(1)}, f32[512,512]{1,0:T(8,128)}, u32[]{:S(2)}) copy-start(f32[512,512]{1,0:T(8,128)} %get-tuple-element.84) | copy-start | bytes 3145732
  100.3 16.8 %all-to-all-start.3 = ((bf16[32,8,512]{2,1,0:T(8,128)(2,1)}), bf16[32,8,512]{2,1,0:T(8,128)(2,1)S(1)}, u32[]{:S(2)}, u32[]{:S(2)}) async-start(bf16[32,8,512]{2,1,0:T(8,128)(2,1)} %pad_maximum_fusion), calls=%async_computation.3 | async-start | bytes 524288 | tf_op jit(solution)/shard_map/all_to_all | solution.py:335
  106.6 14.9 %collective-permute-start.18 = (bf16[512,512]{1,0:T(8,128)(2,1)S(1)}, bf16[512,512]{1,0:T(8,128)(2,1)}, u32[]{:S(2)}, u32[]{:S(2)}) collective-permute-start(bf16[512,512]{1,0:T(8,128)(2,1)S(1)} %add_convert_fusion.1), channel_id=1, source_target_pairs={{0,1},{1,0},{2,3},{3,2},{4,5},{5,4},{6,7},{7,6},{8,9},{9,8},{10,11... | collective-permute-start | bytes 1572872 | tf_op jit(solution)/shard_map/ppermute | solution.py:26
  107.9 18.8 %collective-permute-start.19 = (bf16[512,512]{1,0:T(8,128)(2,1)S(1)}, bf16[512,512]{1,0:T(8,128)(2,1)}, u32[]{:S(2)}, u32[]{:S(2)}) collective-permute-start(bf16[512,512]{1,0:T(8,128)(2,1)S(1)} %add_convert_fusion), channel_id=1, source_target_pairs={{2,5},{3,4},{4,3},{5,2},{6,9},{7,8},{8,7},{9,6},{10,13},{11,12},{1... | collective-permute-start | bytes 1572872 | tf_op jit(solution)/shard_map/ppermute | solution.py:36
  118.0 10.4 %all-to-all-start.4 = ((bf16[4,128,512]{2,1,0:T(8,128)(2,1)}), bf16[4,128,512]{2,1,0:T(8,128)(2,1)S(1)}, u32[]{:S(2)}, u32[]{:S(2)}) async-start(bf16[4,128,512]{2,1,0:T(8,128)(2,1)} %broadcast_in_dim.14), calls=%async_computation.4 | async-start | bytes 1048576 | tf_op jit(solution)/shard_map/all_to_all | solution.py:41
  128.4 8.3 %collective-permute-start.20 = (bf16[512,512]{1,0:T(8,128)(2,1)S(1)}, bf16[512,512]{1,0:T(8,128)(2,1)S(1)}, u32[]{:S(2)}, u32[]{:S(2)}) collective-permute-start(bf16[512,512]{1,0:T(8,128)(2,1)S(1)} %bitcast.10), channel_id=1, source_target_pairs={{0,2},{1,3},{2,0},{3,1},{4,6},{5,7},{6,4},{7,5},{8,10},{9,11},{10,... | collective-permute-start | bytes 1572872 | tf_op jit(solution)/shard_map/ppermute | solution.py:22
  (5 other events, 9.0 us)

commit v4 on v3

--- a/solution.py
+++ b/solution.py
@@ -111,21 +111,14 @@
     own_pre[...] = dot(features[...], self_weight[...])
 
 
-def put(r, j, keep, send, value):
-    if r == 0:
-        keep[j][...] = value.astype(BF)
-    else:
-        send[pl.ds(j * BLK, BLK), :] = value.astype(BF)
-
-
 def ahead(
     core_ref, x_ref, near_hbm,
     features, own_other, on_same, on_other, off_same_low, off_same_high, off_other, hubs, hubs_there,
     own_pre_hbm, neigh_weight_hbm, cotangent_hbm,
-    embedding, slope, *rest,
+    embedding, slope, back, send, *rest,
 ):
-    keep, send = rest[:N_X], rest[N_X]
-    near, table, sums, left, own_pre, neigh_weight, cotangent, sems = rest[N_X + 1:]
+    keep, keep_hub = rest[:N_X], rest[N_X:2 * N_X]
+    near, table, sums, left, own_pre, neigh_weight, cotangent, sems = rest[2 * N_X:]
     core = core_ref[0]
     half = 2 * BLK
 
@@ -165,49 +158,42 @@
         sig = jax.nn.sigmoid(pre)
         embedding[rows, :] = (pre * sig).astype(BF)
         slope[rows, :] = (cotangent[rows, :].astype(F32) * (sig * (1.0 + pre * (1.0 - sig)))).astype(BF)
+    back[...] = dot(slope[...], neigh_weight[...], 1, 1).astype(BF)
     for r in range(2):
         for j in range(N_X):
             x = x_ref[0] ^ j
             first = (2 * (x & 1) + (core ^ r)) * BLK
             columns = pl.ds(pl.multiple_of(first, BLK), BLK)
-            put(r, j, keep, send, dot(left[x >> 1, :, columns], slope[...], 0, 0))
+            value = dot(left[x >> 1, :, columns], slope[...], 0, 0).astype(BF)
+            columns = pl.ds(pl.multiple_of(x * BLK, BLK), BLK)
+            hub_value = dot(near[6 + r, :, columns], back[...], 0, 0).astype(BF)
+            if r == 0:
+                keep[j][...] = value
+                keep_hub[j][...] = hub_value
+            else:
+                send[pl.ds(j * BLK, BLK), :] = value
+                send[pl.ds((N_X + j) * BLK, BLK), :] = hub_value
 
 
 def behind(
-    x_ref, near_hbm, slope_hbm, self_weight_hbm, neigh_weight_hbm,
-    own_grad, g_own_other, g_on_same, g_on_other, g_off_same, g_off_other, *rest,
+    near_hbm, back_hbm, slope_hbm, self_weight_hbm,
+    own_grad, g_own_other, g_on_same, g_on_other, g_off_same, g_off_other,
+    near, back, slope, self_weight, sems,
 ):
-    keep, send = rest[:N_X], rest[N_X]
-    near, back, slope, self_weight, neigh_weight, sems = rest[N_X + 1:]
-    first = [
-        pltpu.make_async_copy(*refs, sems.at[n])
-        for n, refs in enumerate((
-            (slope_hbm, slope), (neigh_weight_hbm, neigh_weight), (self_weight_hbm, self_weight),
-        ))
-    ]
-    order = (6, 7, 1, 2, 3, 4, 5, 0)
-    second = [pltpu.make_async_copy(near_hbm.at[p], near.at[p], sems.at[3 + p]) for p in range(8)]
-    for copy in first + [second[p] for p in order]:
+    order = (1, 2, 3, 4, 5, 0)
+    moves = [(back_hbm, back)] + [(near_hbm.at[p], near.at[p]) for p in order]
+    moves += [(slope_hbm, slope), (self_weight_hbm, self_weight)]
+    copies = [pltpu.make_async_copy(*refs, sems.at[n]) for n, refs in enumerate(moves)]
+    for copy in copies:
         copy.start()
-    for copy in first:
+    copies[0].wait()
+    outs = (None, g_own_other, g_on_same, g_on_other, g_off_same, g_off_other)
+    for n, p in enumerate(order[:-1]):
+        copies[1 + n].wait()
+        outs[p][...] = dot(near[p], back[...], 0, 0).astype(BF)
+    for copy in copies[6:]:
         copy.wait()
-    back[...] = dot(slope[...], neigh_weight[...], 1, 1).astype(BF)
-    outs = (None, g_own_other, g_on_same, g_on_other, g_off_same, g_off_other)
-    for p in order:
-        second[p].wait()
-        if p >= 6:
-            for j in range(N_X):
-                columns = pl.ds(pl.multiple_of((x_ref[0] ^ j) * BLK, BLK), BLK)
-                put(p - 6, j, keep, send, dot(near[p, :, columns], back[...], 0, 0))
-        elif p > 0:
-            outs[p][...] = dot(near[p], back[...], 0, 0).astype(BF)
-        else:
-            own_grad[...] = dot(near[p], back[...], 0, 0) + dot(slope[...], self_weight[...], 1, 1)
-
-
-def join_cores(parts):
-    theirs = to_core(parts[-1])
-    return [plus(mine, theirs[j * BLK:(j + 1) * BLK]) for j, mine in enumerate(parts[:-1])]
+    own_grad[...] = dot(near[0], back[...], 0, 0) + dot(slope[...], self_weight[...], 1, 1)
 
 
 def plus(a, b):
@@ -270,11 +256,11 @@
     hubs, off_same_low, off_same_high, on_other = barrier((hubs, off_same_low, off_same_high, on_other))
     hubs_there = to_core(hubs)
 
-    embedding, slope, *w = pl.pallas_call(
+    embedding, slope, back, send, *kept = pl.pallas_call(
         ahead,
         in_specs=[smem] * 2 + [hbm] * 13,
-        out_specs=[vmem] * (3 + N_X),
-        out_shape=[wide, wide] + [part] * N_X + [wide],
+        out_specs=[vmem] * (4 + 2 * N_X),
+        out_shape=[wide] * 3 + [shape((2 * rows, width), BF)] + [part] * (2 * N_X),
         scratch_shapes=[
             pltpu.VMEM((8, rows, width), BF),
             pltpu.VMEM((8, rows, width), BF),
@@ -286,49 +272,48 @@
             pltpu.SemaphoreType.DMA((20,)),
         ],
         compiler_params=params,
-        cost_estimate=pl.CostEstimate(flops=3 * 10**9, bytes_accessed=12 * 10**6, transcendentals=0),
+        cost_estimate=pl.CostEstimate(flops=4 * 10**9, bytes_accessed=12 * 10**6, transcendentals=0),
         name="ahead",
     )(
         core, x, near,
         features, own_other, on_same, on_other, off_same_low, off_same_high, off_other, hubs, hubs_there,
         own_pre, neighbour_weight, cotangent,
     )
-    w = join_cores(w)
-    w, slope = barrier((w, slope))
-
-    own_grad, g_own_other, g_on_same, g_on_other, g_off_same, g_off_other, *h = pl.pallas_call(
+    theirs = to_core(send)
+    kept = [plus(mine, theirs[j * BLK:(j + 1) * BLK]) for j, mine in enumerate(kept)]
+    w, h = kept[:N_X], kept[N_X:]
+    w, h, slope, back = barrier((w, h, slope, back))
+
+    own_grad, g_own_other, g_on_same, g_on_other, g_off_same, g_off_other = pl.pallas_call(
         behind,
-        in_specs=[smem] + [hbm] * 4,
-        out_specs=[vmem] * (7 + N_X),
-        out_shape=[shape((rows, width), F32)] + [wide] * 5 + [part] * N_X + [wide],
+        in_specs=[hbm] * 4,
+        out_specs=[vmem] * 6,
+        out_shape=[shape((rows, width), F32)] + [wide] * 5,
         scratch_shapes=[
             pltpu.VMEM((8, rows, width), BF),
             pltpu.VMEM((rows, width), BF),
             pltpu.VMEM((rows, width), BF),
             pltpu.VMEM((width, width), BF),
-            pltpu.VMEM((width, width), BF),
-            pltpu.SemaphoreType.DMA((11,)),
+            pltpu.SemaphoreType.DMA((9,)),
         ],
         compiler_params=params,
-        cost_estimate=pl.CostEstimate(flops=3 * 10**9, bytes_accessed=10 * 10**6, transcendentals=0),
+        cost_estimate=pl.CostEstimate(flops=2 * 10**9, bytes_accessed=8 * 10**6, transcendentals=0),
         name="behind",
-    )(x, near, slope, self_weight, neighbour_weight)
+    )(near, back, slope, self_weight)
 
     w = collect_x(w)
     g = (g_own_other, g_on_same, g_on_other, g_off_same, g_off_other)
     w, h, g = barrier((w, h, g))
     g_own_other, g_on_same, g_on_other, g_off_same, g_off_other = g
-    w, h = barrier((w, join_cores(h)))
-
     w = lax.all_to_all(w.reshape(N_WIDE, 4, width), WIDE, 0, 0, tiled=True).astype(F32).sum(0).astype(BF)
     h = collect_x(h)
     r_on_other = to_core(g_on_other)
     r_off_same = to_side(g_off_same)
     r_on_same = to_core(g_on_same)
+
+    w, h, r_on_other, r_off_same, r_on_same = barrier((w, h, r_on_other, r_off_same, r_on_same))
     s_side = plus(g_own_other, r_on_other)
     s_off = plus(g_off_other, r_off_same)
-
-    w, h, s_side, s_off, r_on_same = barrier((w, h, s_side, s_off, r_on_same))
     r_side = to_side(s_side)
     r_off = to_off(s_off)
     both = jnp.concatenate([jnp.broadcast_to(w[None], (N_WIDE, 4, width)), h.reshape(N_WIDE, 4, width)], 1)
@@ -339,10 +324,11 @@
     w, r_side, r_off = barrier((w, r_side, r_off))
     there = to_core(w)
     feature_gradient = own_grad + r_on_same.astype(F32) + r_side.astype(F32) + r_off.astype(F32)
-    first = core[0] == 0
-    pair = (N_X, 1, BLK, width)
-    low, high = jnp.where(first, w, there).reshape(pair), jnp.where(first, there, w).reshape(pair)
-    weights = jnp.concatenate([low, high], 1).reshape(2, width, width).astype(F32)
+    mine = lax.broadcasted_iota(jnp.int32, (1, 2, 1, 1), 1) == core[0]
+    w, there = w.reshape(N_X, 1, BLK, width), there.reshape(N_X, 1, BLK, width)
+    weights = [
+        jnp.where(mine, w[i:i + 2], there[i:i + 2]).astype(F32).reshape(width, width) for i in (0, 2)
+    ]
     return embedding, feature_gradient, hub_gradient, weights[0], weights[1]
 
 

time: 139 us -> 138 us (level)
  starting transfers between devices: 70 us -> 71.4 us
    all_to_all x1, waiting for transfers between devices: 2.87 us -> 9.24 us  [local(): lax.all_to_all(w.reshape(N_WIDE, 4, width), WIDE, 0, 0, tiled=True)]
    ppermute x6, waiting for transfers between devices: 4.99 us -> 1.93 us  [to_x(): return lax.ppermute(value, 'x', [(x, x ^ flip) for x in range(N_X)])]
    all_to_all x1, starting transfers between devices: 6.23 us -> 3.87 us  [local(): both = lax.all_to_all(both, WIDE, 0, 0, tiled=True)]
    all_to_all x1, waiting for transfers between devices: 2.34 us -> 0.01 us  [local(): both = lax.all_to_all(both, WIDE, 0, 0, tiled=True)]
    ppermute x6, starting transfers between devices: 10.7 us -> 12.9 us  [to_x(): return lax.ppermute(value, 'x', [(x, x ^ flip) for x in range(N_X)])]
    pallas_call x1, Pallas kernels: 7.37 us -> 5.46 us  [local(): pl.pallas_call(behind, in_specs=[hbm] * 4, out_specs=[vmem] * 6, out_shap...]
    all_to_all x3, waiting for transfers between devices: 1.75 us -> 0.18 us  [spread(): lax.all_to_all(copies, axes, 0, 0, tiled=True).reshape(-1, value.shape[-1])]
    slice x1 -> x2, local copies, waits for them, and re-layouts: 1.56 us -> 0.07 us  [the longest x1 0.03 us: local(): w[i:i + 2]]
  transfers between devices with their start and end apart: 26 -> 25, of which waited for: 10 -> 10; matrix products, arithmetic and copies ran while one was open for 9% -> 8% of each run, Pallas kernels for 11% -> 9%
where the time goes in v4:
time: 138 us; the launch traced here: 137 us
  starting transfers between devices  71.4 us (52%)
  waiting for transfers between devices  27.8 us (20%)
  Pallas kernels  20 us (14%)
  other arithmetic  9.03 us (7%)
  local copies, waits for them, and re-layouts  7.4 us (5%)
  between operations  1.62 us (1%)
    all_to_all x3, starting transfers between devices, spread(): lax.all_to_all(copies, axes, 0, 0, tiled=True).reshape(-1, value.shape[-1])  17 us
    ppermute x3, starting transfers between devices, to_off(): return lax.ppermute(value, AXES, pairs)  16.2 us
    ppermute x6, starting transfers between devices, to_x(): return lax.ppermute(value, 'x', [(x, x ^ flip) for x in range(N_X)])  12.9 us
    ppermute x3, waiting for transfers between devices, to_off(): return lax.ppermute(value, AXES, pairs)  10.6 us
    ppermute x7, starting transfers between devices, to_core(): return lax.ppermute(value, AXES, [(d, d ^ 2) for d in range(DEVICES)])  9.53 us
    all_to_all x1, waiting for transfers between devices, local(): lax.all_to_all(w.reshape(N_WIDE, 4, width), WIDE, 0, 0, tiled=True)  9.24 us
    all_to_all x1, starting transfers between devices, local(): lax.all_to_all(w.reshape(N_WIDE, 4, width), WIDE, 0, 0, tiled=True)  8.8 us
    pallas_call x1, Pallas kernels, local(): pl.pallas_call(ahead, in_specs=[smem] * 2 + [hbm] * 13, out_specs=[vmem]...  7.45 us
  transfers between devices with their start and end apart: 25, of which 10 were waited for; matrix products, arithmetic and copies ran while one was open for 8% of the time, Pallas kernels for 9%

profile of v4, /device:TPU:1, one launch (start us, length us, event | category | flops | bytes accessed | tf_op | source)
XLA Modules:
  0.0 137.3 jit_solution(4950262322478755500)
XLA Ops:
  0.6 2.2 %collective-permute-start = (bf16[512,512]{1,0:T(8,128)(2,1)}, bf16[512,512]{1,0:T(8,128)(2,1)S(1)}, u32[]{:S(2)}, u32[]{:S(2)}) collective-permute-start(bf16[512,512]{1,0:T(8,128)(2,1)} %features.1), channel_id=1, source_target_pairs={{0,1},{1,0},{2,3},{3,2},{4,5},{5,4},{6,7},{7,6},{8,9},{9,8},{10,11... | collective-permute-start | bytes 1572872 | tf_op jit(solution)/shard_map/ppermute | solution.py:26
  2.8 4.6 %collective-permute-start.1 = (bf16[512,512]{1,0:T(8,128)(2,1)}, bf16[512,512]{1,0:T(8,128)(2,1)S(1)}, u32[]{:S(2)}, u32[]{:S(2)}) collective-permute-start(bf16[512,512]{1,0:T(8,128)(2,1)} %features.1), channel_id=1, source_target_pairs={{2,5},{3,4},{4,3},{5,2},{6,9},{7,8},{8,7},{9,6},{10,13},{11,12},{1... | collective-permute-start | bytes 1572872 | tf_op jit(solution)/shard_map/ppermute | solution.py:36
  7.6 1.4 %broadcast_in_dim.82 = bf16[32,4,512]{2,1,0:T(4,128)(2,1)} broadcast(bf16[4,512]{1,0:T(4,128)(2,1)} %param.11), dimensions={1,2} | broadcast | bytes 135168 | tf_op jit(solution)/shard_map/broadcast_in_dim | solution.py:40
  9.0 9.5 %all-to-all-start = ((bf16[32,4,512]{2,1,0:T(4,128)(2,1)}), bf16[32,4,512]{2,1,0:T(4,128)(2,1)S(1)}, u32[]{:S(2)}, u32[]{:S(2)}) async-start(bf16[32,4,512]{2,1,0:T(4,128)(2,1)} %broadcast_in_dim.82), calls=%async_computation | async-start | bytes 262144 | tf_op jit(solution)/shard_map/all_to_all | solution.py:41
  18.5 1.7 %copy.15.order_col = s32[1024,1]{1,0:T(8,128)} copy(s32[1024,1]{0,1:T(1,128)} %bitcast.30) | data formatting | bytes 8192 | tf_op jit(solution)/shard_map/reshape | solution.py:250
  20.9 7.1 %prepare.1 = (bf16[8,512,512]{2,1,0:T(8,128)(2,1)}, f32[512,512]{1,0:T(8,128)}) custom-call(s32[1,64]{1,0:T(1,128)} %dest.1, s32[1,64]{1,0:T(1,128)} %source.1, s32[1]{0:T(128)S(6)} %copy.16.count, s32[1]{0:T(128)} %bitcast.2.side, s32[1]{0:T(128)} %bitcast.core_ref, s32[1024,1]{1,0:T(8,128)} %copy.15.order_col, bf16[512,512]{1,0:T(8,128)(2,1)} %features.1, ...), custom_call_target="tpu_custom_call" | custom-call | flops 1300000000 | bytes 9000000 | tf_op jit(solution)/shard_map/prepare/pallas_call | solution.py:233
  28.1 2.0 %collective-permute-start.5 = (bf16[512,512]{1,0:T(8,128)(2,1)S(1)}, bf16[512,512]{1,0:T(8,128)(2,1)S(1)}, u32[]{:S(2)}, u32[]{:S(2)}) collective-permute-start(bf16[512,512]{1,0:T(8,128)(2,1)S(1)} %collective-permute-done.own_other), channel_id=1, source_target_pairs={{0,2},{1,3},{2,0},{3,1},{4,6},{5,7},{6,4},{7,5},{8,10},{9,11},{10,... | collective-permute-start | bytes 1572872 | tf_op jit(solution)/shard_map/ppermute | solution.py:22
  31.0 4.0 %all-to-all-start.1 = ((bf16[4,128,512]{2,1,0:T(8,128)(2,1)}), bf16[4,128,512]{2,1,0:T(8,128)(2,1)S(1)}, u32[]{:S(2)}, u32[]{:S(2)}) async-start(bf16[4,128,512]{2,1,0:T(8,128)(2,1)} %broadcast_in_dim.83), calls=%async_computation.1 | async-start | bytes 1048576 | tf_op jit(solution)/shard_map/all_to_all | solution.py:41
  35.0 3.9 %collective-permute-start.4 = (bf16[256,512]{1,0:T(8,128)(2,1)S(1)}, bf16[256,512]{1,0:T(8,128)(2,1)S(1)}, u32[]{:S(2)}, u32[]{:S(2)}) collective-permute-start(bf16[256,512]{1,0:T(8,128)(2,1)S(1)} %slice.53), channel_id=1, source_target_pairs={{2,5},{3,4},{4,3},{5,2},{6,9},{7,8},{8,7},{9,6},{10,13},{11,12},{1... | collective-permute-start | bytes 786440 | tf_op jit(solution)/shard_map/ppermute | solution.py:36
  39.4 5.6 %collective-permute-done.4.off_same_high = bf16[256,512]{1,0:T(8,128)(2,1)S(1)} collective-permute-done((bf16[256,512]{1,0:T(8,128)(2,1)S(1)}, bf16[256,512]{1,0:T(8,128)(2,1)S(1)}, u32[]{:S(2)}, u32[]{:S(2)}) %collective-permute-start.4) | collective-permute-done | bytes 262176 | tf_op jit(solution)/shard_map/ppermute | solution.py:36
  45.8 1.9 %collective-permute-done.6.hubs_there = bf16[512,512]{1,0:T(8,128)(2,1)S(1)} collective-permute-done((bf16[512,512]{1,0:T(8,128)(2,1)S(1)}, bf16[512,512]{1,0:T(8,128)(2,1)S(1)}, u32[]{:S(2)}, u32[]{:S(2)}) %collective-permute-start.6) | collective-permute-done | bytes 524320 | tf_op jit(solution)/shard_map/ppermute | solution.py:22
  48.5 7.4 %ahead.1 = (bf16[512,512]{1,0:T(8,128)(2,1)}, bf16[512,512]{1,0:T(8,128)(2,1)}, bf16[512,512]{1,0:T(8,128)(2,1)}, bf16[1024,512]{1,0:T(8,128)(2,1)}, bf16[128,51...) custom-call(s32[1]{0:T(128)} %bitcast.core_ref, ...), custom_call_target="tpu_custom_call" | custom-call | flops 4000000000 | bytes 12000000 | tf_op jit(solution)/shard_map/ahead/pallas_call | solution.py:259
  56.2 2.7 %collective-permute-done.7 = bf16[1024,512]{1,0:T(8,128)(2,1)S(1)} collective-permute-done((bf16[1024,512]{1,0:T(8,128)(2,1)}, bf16[1024,512]{1,0:T(8,128)(2,1)S(1)}, u32[]{:S(2)}, u32[]{:S(2)}) %collective-permute-start.7) | collective-permute-done | bytes 1048608 | tf_op jit(solution)/shard_map/ppermute | solution.py:22
  59.0 1.6 %add_convert_fusion.4 = (bf16[128,512]{1,0:T(8,128)(2,1)S(1)}, bf16[128,512]{1,0:T(8,128)(2,1)S(1)}, bf16[128,512]{1,0:T(8,128)(2,1)S(1)}, bf16[128,512]{1,0:T(8...) fusion(bf16[128,512]{1,0:T(8,128)(2,1)} %get-tuple-element.84, ...), kind=kLoop, calls=%fused_computation.11 | loop fusion | flops 2097152 | bytes 3145728 | tf_op jit(solution)/shard_map/convert_element_type | solution.py:200
  60.5 5.4 %collective-permute-start.10 = (bf16[128,512]{1,0:T(8,128)(2,1)S(1)}, bf16[128,512]{1,0:T(8,128)(2,1)S(1)}, u32[]{:S(2)}, u32[]{:S(2)}) collective-permute-start(bf16[128,512]{1,0:T(8,128)(2,1)S(1)} %get-tuple-element.93), channel_id=1, source_target_pairs={{0,192},{64,128},{128,64},{192,0},{1,193},{65,129},{129,65},{193,1... | collective-permute-start | bytes 393224 | tf_op jit(solution)/shard_map/ppermute | solution.py:45
  66.0 1.5 %collective-permute-start.9 = (bf16[128,512]{1,0:T(8,128)(2,1)S(1)}, bf16[128,512]{1,0:T(8,128)(2,1)S(1)}, u32[]{:S(2)}, u32[]{:S(2)}) collective-permute-start(bf16[128,512]{1,0:T(8,128)(2,1)S(1)} %get-tuple-element.92), channel_id=1, source_target_pairs={{0,128},{64,192},{128,0},{192,64},{1,129},{65,193},{129,1},{193,65... | collective-permute-start | bytes 393224 | tf_op jit(solution)/shard_map/ppermute | solution.py:45
  67.4 5.5 %behind.1 = (f32[512,512]{1,0:T(8,128)}, bf16[512,512]{1,0:T(8,128)(2,1)}, bf16[512,512]{1,0:T(8,128)(2,1)}, bf16[512,512]{1,0:T(8,128)(2,1)}, bf16[512,512]{1,0:T(8,128)(2,1)}, /*index=5*/bf16[512,512]{1,0:T(8,128)(2,1)}) custom-call(bf16[8,512,512]{2,1,0:T(8,128)(2,1)} %get-tuple-element.65.near_hbm, bf16[512,512]{1,0:T(8,128)(2,1)} %get-tuple-element.87.back_hbm, ...), custom_call_target="tpu_custom_call" | custom-call | flops 2000000000 | bytes 8000000 | tf_op jit(solution)/shard_map/behind/pallas_call | solution.py:287
  73.6 1.3 collective-permute-start.14
  75.8 3.4 %collective-permute-start.12 = (bf16[128,512]{1,0:T(8,128)(2,1)S(1)}, bf16[128,512]{1,0:T(8,128)(2,1)S(1)}, u32[]{:S(2)}, u32[]{:S(2)}) collective-permute-start(bf16[128,512]{1,0:T(8,128)(2,1)S(1)} %get-tuple-element.106), channel_id=1, source_target_pairs={{0,128},{64,192},{128,0},{192,64},{1,129},{65,193},{129,1},{193,65... | collective-permute-start | bytes 393224 | tf_op jit(solution)/shard_map/ppermute | solution.py:45
  79.2 1.4 collective-permute-done.11
  80.5 2.4 %collective-permute-start.13 = (bf16[128,512]{1,0:T(8,128)(2,1)S(1)}, bf16[128,512]{1,0:T(8,128)(2,1)S(1)}, u32[]{:S(2)}, u32[]{:S(2)}) collective-permute-start(bf16[128,512]{1,0:T(8,128)(2,1)S(1)} %get-tuple-element.107), channel_id=1, source_target_pairs={{0,192},{64,128},{128,64},{192,0},{1,193},{65,129},{129,65},{193,1... | collective-permute-start | bytes 393224 | tf_op jit(solution)/shard_map/ppermute | solution.py:45
  83.6 8.8 %all-to-all-start.2 = ((bf16[32,4,512]{2,1,0:T(4,128)(2,1)}), bf16[32,4,512]{2,1,0:T(4,128)(2,1)S(1)}, u32[]{:S(2)}, u32[]{:S(2)}) async-start(bf16[32,4,512]{2,1,0:T(4,128)(2,1)} %reshape.70), calls=%async_computation.2 | async-start | bytes 262144 | tf_op jit(solution)/shard_map/all_to_all | solution.py:308
  92.5 9.2 %all-to-all-done.2 = bf16[32,4,512]{2,1,0:T(4,128)(2,1)S(1)} async-done(((bf16[32,4,512]{2,1,0:T(4,128)(2,1)}), bf16[32,4,512]{2,1,0:T(4,128)(2,1)S(1)}, u32[]{:S(2)}, u32[]{:S(2)}) %all-to-all-start.2) | async-done | bytes 131104 | tf_op jit(solution)/shard_map/all_to_all | solution.py:308
  102.8 3.9 %all-to-all-start.3 = ((bf16[32,8,512]{2,1,0:T(8,128)(2,1)}), bf16[32,8,512]{2,1,0:T(8,128)(2,1)S(1)}, u32[]{:S(2)}, u32[]{:S(2)}) async-start(bf16[32,8,512]{2,1,0:T(8,128)(2,1)} %pad_maximum_fusion), calls=%async_computation.3 | async-start | bytes 524288 | tf_op jit(solution)/shard_map/all_to_all | solution.py:320
  106.7 2.0 %add_convert_fusion = bf16[512,512]{1,0:T(8,128)(2,1)} fusion(bf16[512,512]{1,0:T(8,128)(2,1)S(1)} %collective-permute-done.15, bf16[512,512]{1,0:T(8,128)(2,1)} %get-tuple-element.116), kind=kLoop, calls=%fused_computation.1 | loop fusion | flops 1048576 | bytes 1572864 | tf_op jit(solution)/shard_map/convert_element_type | solution.py:200
  108.6 7.7 %collective-permute-start.18 = (bf16[512,512]{1,0:T(8,128)(2,1)}, bf16[512,512]{1,0:T(8,128)(2,1)S(1)}, u32[]{:S(2)}, u32[]{:S(2)}) collective-permute-start(bf16[512,512]{1,0:T(8,128)(2,1)} %add_convert_fusion), channel_id=1, source_target_pairs={{2,5},{3,4},{4,3},{5,2},{6,9},{7,8},{8,7},{9,6},{10,13},{11,12},{1... | collective-permute-start | bytes 1572872 | tf_op jit(solution)/shard_map/ppermute | solution.py:36
  116.4 0.9 add_convert_fusion.1
  118.2 3.5 %all-to-all-start.4 = ((bf16[4,128,512]{2,1,0:T(8,128)(2,1)}), bf16[4,128,512]{2,1,0:T(8,128)(2,1)S(1)}, u32[]{:S(2)}, u32[]{:S(2)}) async-start(bf16[4,128,512]{2,1,0:T(8,128)(2,1)} %broadcast_in_dim.86), calls=%async_computation.4 | async-start | bytes 1048576 | tf_op jit(solution)/shard_map/all_to_all | solution.py:41
  122.5 5.1 %collective-permute-done.18 = bf16[512,512]{1,0:T(8,128)(2,1)S(1)} collective-permute-done((bf16[512,512]{1,0:T(8,128)(2,1)}, bf16[512,512]{1,0:T(8,128)(2,1)S(1)}, u32[]{:S(2)}, u32[]{:S(2)}) %collective-permute-start.18) | collective-permute-done | bytes 524320 | tf_op jit(solution)/shard_map/ppermute | solution.py:36
  128.6 5.6 %collective-permute-start.19 = (bf16[512,512]{1,0:T(8,128)(2,1)S(1)}, bf16[512,512]{1,0:T(8,128)(2,1)S(1)}, u32[]{:S(2)}, u32[]{:S(2)}) collective-permute-start(bf16[512,512]{1,0:T(8,128)(2,1)S(1)} %bitcast.22), channel_id=1, source_target_pairs={{0,2},{1,3},{2,0},{3,1},{4,6},{5,7},{6,4},{7,5},{8,10},{9,11},{10,... | collective-permute-start | bytes 1572872 | tf_op jit(solution)/shard_map/ppermute | solution.py:22
  134.2 1.2 convert_add_fusion
  135.7 1.5 %fusion = (f32[512,512]{1,0:T(8,128)}, f32[512,512]{1,0:T(8,128)}) fusion(pred[512]{0:T(512)(128)(4,1)S(1)} %broadcast_in_dim.88, bf16[2,128,512]{2,1,0:T(8,128)(2,1)S(1)} %bitcast.26, bf16[2,128,512]{2,1,0:T(8,128)(2,1)S(1)} %bitcast.24, bf16[2,128,512]{2,1,0:T(8,128)(2,1)S(1)} %bitcast.27, bf16[2,128,512]{2,1,0:T(8,128)(2,1)S(1)} %bitcast.25), kind=kLoop, calls=%fused_computation.4 | loop fusion | flops 1048576 | bytes 3146240 | tf_op jit(solution)/shard_map/convert_element_type | solution.py:330
  (68 shorter events, 9.7 us)
Async XLA Ops:
  0.6 27.4 %collective-permute-start = (bf16[512,512]{1,0:T(8,128)(2,1)}, bf16[512,512]{1,0:T(8,128)(2,1)S(1)}, u32[]{:S(2)}, u32[]{:S(2)}) collective-permute-start(bf16[512,512]{1,0:T(8,128)(2,1)} %features.1), channel_id=1, source_target_pairs={{0,1},{1,0},{2,3},{3,2},{4,5},{5,4},{6,7},{7,6},{8,9},{9,8},{10,11... | collective-permute-start | bytes 1572872 | tf_op jit(solution)/shard_map/ppermute | solution.py:26
  2.8 25.2 %collective-permute-start.1 = (bf16[512,512]{1,0:T(8,128)(2,1)}, bf16[512,512]{1,0:T(8,128)(2,1)S(1)}, u32[]{:S(2)}, u32[]{:S(2)}) collective-permute-start(bf16[512,512]{1,0:T(8,128)(2,1)} %features.1), channel_id=1, source_target_pairs={{2,5},{3,4},{4,3},{5,2},{6,9},{7,8},{8,7},{9,6},{10,13},{11,12},{1... | collective-permute-start | bytes 1572872 | tf_op jit(solution)/shard_map/ppermute | solution.py:36
  7.5 20.6 %collective-permute-start.2 = (bf16[512,512]{1,0:T(8,128)(2,1)}, bf16[512,512]{1,0:T(8,128)(2,1)S(1)}, u32[]{:S(2)}, u32[]{:S(2)}) collective-permute-start(bf16[512,512]{1,0:T(8,128)(2,1)} %features.1), channel_id=1, source_target_pairs={{0,2},{1,3},{2,0},{3,1},{4,6},{5,7},{6,4},{7,5},{8,10},{9,11},{10,... | collective-permute-start | bytes 1572872 | tf_op jit(solution)/shard_map/ppermute | solution.py:22
  9.0 19.0 %all-to-all-start = ((bf16[32,4,512]{2,1,0:T(4,128)(2,1)}), bf16[32,4,512]{2,1,0:T(4,128)(2,1)S(1)}, u32[]{:S(2)}, u32[]{:S(2)}) async-start(bf16[32,4,512]{2,1,0:T(4,128)(2,1)} %broadcast_in_dim.82), calls=%async_computation | async-start | bytes 262144 | tf_op jit(solution)/shard_map/all_to_all | solution.py:41
  28.1 19.6 %copy-start.3 = (bf16[512,512]{1,0:T(8,128)(2,1)}, bf16[512,512]{1,0:T(8,128)(2,1)S(1)}, u32[]{:S(2)}) copy-start(bf16[512,512]{1,0:T(8,128)(2,1)S(1)} %collective-permute-done.own_other) | copy-start | bytes 1572868
  28.1 19.6 %copy-start.4 = (bf16[512,512]{1,0:T(8,128)(2,1)}, bf16[512,512]{1,0:T(8,128)(2,1)S(1)}, u32[]{:S(2)}) copy-start(bf16[512,512]{1,0:T(8,128)(2,1)S(1)} %collective-permute-done.1.off_other) | copy-start | bytes 1572868
  28.1 19.6 %copy-start.5 = (bf16[512,512]{1,0:T(8,128)(2,1)}, bf16[512,512]{1,0:T(8,128)(2,1)S(1)}, u32[]{:S(2)}) copy-start(bf16[512,512]{1,0:T(8,128)(2,1)S(1)} %collective-permute-done.2.on_same) | copy-start | bytes 1572868
  28.1 16.9 %collective-permute-start.5 = (bf16[512,512]{1,0:T(8,128)(2,1)S(1)}, bf16[512,512]{1,0:T(8,128)(2,1)S(1)}, u32[]{:S(2)}, u32[]{:S(2)}) collective-permute-start(bf16[512,512]{1,0:T(8,128)(2,1)S(1)} %collective-permute-done.own_other), channel_id=1, source_target_pairs={{0,2},{1,3},{2,0},{3,1},{4,6},{5,7},{6,4},{7,5},{8,10},{9,11},{10,... | collective-permute-start | bytes 1572872 | tf_op jit(solution)/shard_map/ppermute | solution.py:22
  31.0 14.1 %all-to-all-start.1 = ((bf16[4,128,512]{2,1,0:T(8,128)(2,1)}), bf16[4,128,512]{2,1,0:T(8,128)(2,1)S(1)}, u32[]{:S(2)}, u32[]{:S(2)}) async-start(bf16[4,128,512]{2,1,0:T(8,128)(2,1)} %broadcast_in_dim.83), calls=%async_computation.1 | async-start | bytes 1048576 | tf_op jit(solution)/shard_map/all_to_all | solution.py:41
  35.0 10.0 %collective-permute-start.4 = (bf16[256,512]{1,0:T(8,128)(2,1)S(1)}, bf16[256,512]{1,0:T(8,128)(2,1)S(1)}, u32[]{:S(2)}, u32[]{:S(2)}) collective-permute-start(bf16[256,512]{1,0:T(8,128)(2,1)S(1)} %slice.53), channel_id=1, source_target_pairs={{2,5},{3,4},{4,3},{5,2},{6,9},{7,8},{8,7},{9,6},{10,13},{11,12},{1... | collective-permute-start | bytes 786440 | tf_op jit(solution)/shard_map/ppermute | solution.py:36
  38.9 6.1 %collective-permute-start.3 = (bf16[256,512]{1,0:T(8,128)(2,1)S(1)}, bf16[256,512]{1,0:T(8,128)(2,1)S(1)}, u32[]{:S(2)}, u32[]{:S(2)}) collective-permute-start(bf16[256,512]{1,0:T(8,128)(2,1)S(1)} %slice.52), channel_id=1, source_target_pairs={{0,1},{1,0},{2,3},{3,2},{4,5},{5,4},{6,7},{7,6},{8,9},{9,8},{10,11... | collective-permute-start | bytes 786440 | tf_op jit(solution)/shard_map/ppermute | solution.py:26
  45.0 2.7 %copy-start.8 = (bf16[256,512]{1,0:T(8,128)(2,1)}, bf16[256,512]{1,0:T(8,128)(2,1)S(1)}, u32[]{:S(2)}) copy-start(bf16[256,512]{1,0:T(8,128)(2,1)S(1)} %collective-permute-done.4.off_same_high) | copy-start | bytes 786436
  45.0 2.7 %copy-start.2 = (bf16[4,128,512]{2,1,0:T(8,128)(2,1)}, bf16[4,128,512]{2,1,0:T(8,128)(2,1)S(1)}, u32[]{:S(2)}) copy-start(bf16[4,128,512]{2,1,0:T(8,128)(2,1)S(1)} %all-to-all-done.1) | copy-start | bytes 1572868
  45.8 1.9 %collective-permute-start.6 = (bf16[512,512]{1,0:T(8,128)(2,1)S(1)}, bf16[512,512]{1,0:T(8,128)(2,1)S(1)}, u32[]{:S(2)}, u32[]{:S(2)}) collective-permute-start(bf16[512,512]{1,0:T(8,128)(2,1)S(1)} %bitcast.28), channel_id=1, source_target_pairs={{0,2},{1,3},{2,0},{3,1},{4,6},{5,7},{6,4},{7,5},{8,10},{9,11},{10,... | collective-permute-start | bytes 1572872 | tf_op jit(solution)/shard_map/ppermute | solution.py:22
  56.0 3.0 %collective-permute-start.7 = (bf16[1024,512]{1,0:T(8,128)(2,1)}, bf16[1024,512]{1,0:T(8,128)(2,1)S(1)}, u32[]{:S(2)}, u32[]{:S(2)}) collective-permute-start(bf16[1024,512]{1,0:T(8,128)(2,1)} %get-tuple-element.77), channel_id=1, source_target_pairs={{0,2},{1,3},{2,0},{3,1},{4,6},{5,7},{6,4},{7,5},{8,10},{9,11},{10,... | collective-permute-start | bytes 3145736 | tf_op jit(solution)/shard_map/ppermute | solution.py:22
  60.5 12.4 %collective-permute-start.10 = (bf16[128,512]{1,0:T(8,128)(2,1)S(1)}, bf16[128,512]{1,0:T(8,128)(2,1)S(1)}, u32[]{:S(2)}, u32[]{:S(2)}) collective-permute-start(bf16[128,512]{1,0:T(8,128)(2,1)S(1)} %get-tuple-element.93), channel_id=1, source_target_pairs={{0,192},{64,128},{128,64},{192,0},{1,193},{65,129},{129,65},{193,1... | collective-permute-start | bytes 393224 | tf_op jit(solution)/shard_map/ppermute | solution.py:45
  66.0 7.0 %collective-permute-start.8 = (bf16[128,512]{1,0:T(8,128)(2,1)S(1)}, bf16[128,512]{1,0:T(8,128)(2,1)S(1)}, u32[]{:S(2)}, u32[]{:S(2)}) collective-permute-start(bf16[128,512]{1,0:T(8,128)(2,1)S(1)} %get-tuple-element.91), channel_id=1, source_target_pairs={{0,64},{64,0},{128,192},{192,128},{1,65},{65,1},{129,193},{193,129... | collective-permute-start | bytes 393224 | tf_op jit(solution)/shard_map/ppermute | solution.py:45
  66.0 7.5 %collective-permute-start.9 = (bf16[128,512]{1,0:T(8,128)(2,1)S(1)}, bf16[128,512]{1,0:T(8,128)(2,1)S(1)}, u32[]{:S(2)}, u32[]{:S(2)}) collective-permute-start(bf16[128,512]{1,0:T(8,128)(2,1)S(1)} %get-tuple-element.92), channel_id=1, source_target_pairs={{0,128},{64,192},{128,0},{192,64},{1,129},{65,193},{129,1},{193,65... | collective-permute-start | bytes 393224 | tf_op jit(solution)/shard_map/ppermute | solution.py:45
  72.9 43.5 %copy-start.1 = (bf16[512,512]{1,0:T(8,128)(2,1)S(1)}, bf16[512,512]{1,0:T(8,128)(2,1)}, u32[]{:S(2)}) copy-start(bf16[512,512]{1,0:T(8,128)(2,1)} %get-tuple-element.114) | copy-start | bytes 1572868
  73.6 28.3 %collective-permute-start.14 = (bf16[512,512]{1,0:T(8,128)(2,1)}, bf16[512,512]{1,0:T(8,128)(2,1)S(1)}, u32[]{:S(2)}, u32[]{:S(2)}) collective-permute-start(bf16[512,512]{1,0:T(8,128)(2,1)} %get-tuple-element.108), channel_id=1, source_target_pairs={{0,2},{1,3},{2,0},{3,1},{4,6},{5,7},{6,4},{7,5},{8,10},{9,11},{10,... | collective-permute-start | bytes 1572872 | tf_op jit(solution)/shard_map/ppermute | solution.py:22
  74.9 27.0 %collective-permute-start.15 = (bf16[512,512]{1,0:T(8,128)(2,1)}, bf16[512,512]{1,0:T(8,128)(2,1)S(1)}, u32[]{:S(2)}, u32[]{:S(2)}) collective-permute-start(bf16[512,512]{1,0:T(8,128)(2,1)} %get-tuple-element.109), channel_id=1, source_target_pairs={{0,1},{1,0},{2,3},{3,2},{4,5},{5,4},{6,7},{7,6},{8,9},{9,8},{10,11... | collective-permute-start | bytes 1572872 | tf_op jit(solution)/shard_map/ppermute | solution.py:26
  75.2 26.6 %collective-permute-start.16 = (bf16[512,512]{1,0:T(8,128)(2,1)}, bf16[512,512]{1,0:T(8,128)(2,1)S(1)}, u32[]{:S(2)}, u32[]{:S(2)}) collective-permute-start(bf16[512,512]{1,0:T(8,128)(2,1)} %get-tuple-element.110), channel_id=1, source_target_pairs={{0,2},{1,3},{2,0},{3,1},{4,6},{5,7},{6,4},{7,5},{8,10},{9,11},{10,... | collective-permute-start | bytes 1572872 | tf_op jit(solution)/shard_map/ppermute | solution.py:22
  75.6 4.9 %collective-permute-start.11 = (bf16[128,512]{1,0:T(8,128)(2,1)S(1)}, bf16[128,512]{1,0:T(8,128)(2,1)S(1)}, u32[]{:S(2)}, u32[]{:S(2)}) collective-permute-start(bf16[128,512]{1,0:T(8,128)(2,1)S(1)} %get-tuple-element.105), channel_id=1, source_target_pairs={{0,64},{64,0},{128,192},{192,128},{1,65},{65,1},{129,193},{193,129... | collective-permute-start | bytes 393224 | tf_op jit(solution)/shard_map/ppermute | solution.py:45
  75.8 16.7 %collective-permute-start.12 = (bf16[128,512]{1,0:T(8,128)(2,1)S(1)}, bf16[128,512]{1,0:T(8,128)(2,1)S(1)}, u32[]{:S(2)}, u32[]{:S(2)}) collective-permute-start(bf16[128,512]{1,0:T(8,128)(2,1)S(1)} %get-tuple-element.106), channel_id=1, source_target_pairs={{0,128},{64,192},{128,0},{192,64},{1,129},{65,193},{129,1},{193,65... | collective-permute-start | bytes 393224 | tf_op jit(solution)/shard_map/ppermute | solution.py:45
  80.5 11.9 %collective-permute-start.13 = (bf16[128,512]{1,0:T(8,128)(2,1)S(1)}, bf16[128,512]{1,0:T(8,128)(2,1)S(1)}, u32[]{:S(2)}, u32[]{:S(2)}) collective-permute-start(bf16[128,512]{1,0:T(8,128)(2,1)S(1)} %get-tuple-element.107), channel_id=1, source_target_pairs={{0,192},{64,128},{128,64},{192,0},{1,193},{65,129},{129,65},{193,1... | collective-permute-start | bytes 393224 | tf_op jit(solution)/shard_map/ppermute | solution.py:45
  83.6 18.2 %all-to-all-start.2 = ((bf16[32,4,512]{2,1,0:T(4,128)(2,1)}), bf16[32,4,512]{2,1,0:T(4,128)(2,1)S(1)}, u32[]{:S(2)}, u32[]{:S(2)}) async-start(bf16[32,4,512]{2,1,0:T(4,128)(2,1)} %reshape.70), calls=%async_computation.2 | async-start | bytes 262144 | tf_op jit(solution)/shard_map/all_to_all | solution.py:308
  92.5 41.7 %copy-start = (f32[512,512]{1,0:T(8,128)S(1)}, f32[512,512]{1,0:T(8,128)}, u32[]{:S(2)}) copy-start(f32[512,512]{1,0:T(8,128)} %get-tuple-element.89) | copy-start | bytes 3145732
  102.8 14.5 %all-to-all-start.3 = ((bf16[32,8,512]{2,1,0:T(8,128)(2,1)}), bf16[32,8,512]{2,1,0:T(8,128)(2,1)S(1)}, u32[]{:S(2)}, u32[]{:S(2)}) async-start(bf16[32,8,512]{2,1,0:T(8,128)(2,1)} %pad_maximum_fusion), calls=%async_computation.3 | async-start | bytes 524288 | tf_op jit(solution)/shard_map/all_to_all | solution.py:320
  108.6 18.9 %collective-permute-start.18 = (bf16[512,512]{1,0:T(8,128)(2,1)}, bf16[512,512]{1,0:T(8,128)(2,1)S(1)}, u32[]{:S(2)}, u32[]{:S(2)}) collective-permute-start(bf16[512,512]{1,0:T(8,128)(2,1)} %add_convert_fusion), channel_id=1, source_target_pairs={{2,5},{3,4},{4,3},{5,2},{6,9},{7,8},{8,7},{9,6},{10,13},{11,12},{1... | collective-permute-start | bytes 1572872 | tf_op jit(solution)/shard_map/ppermute | solution.py:36
  117.3 11.1 %collective-permute-start.17 = (bf16[512,512]{1,0:T(8,128)(2,1)}, bf16[512,512]{1,0:T(8,128)(2,1)S(1)}, u32[]{:S(2)}, u32[]{:S(2)}) collective-permute-start(bf16[512,512]{1,0:T(8,128)(2,1)} %add_convert_fusion.1), channel_id=1, source_target_pairs={{0,1},{1,0},{2,3},{3,2},{4,5},{5,4},{6,7},{7,6},{8,9},{9,8},{10,11... | collective-permute-start | bytes 1572872 | tf_op jit(solution)/shard_map/ppermute | solution.py:26
  118.2 10.4 %all-to-all-start.4 = ((bf16[4,128,512]{2,1,0:T(8,128)(2,1)}), bf16[4,128,512]{2,1,0:T(8,128)(2,1)S(1)}, u32[]{:S(2)}, u32[]{:S(2)}) async-start(bf16[4,128,512]{2,1,0:T(8,128)(2,1)} %broadcast_in_dim.86), calls=%async_computation.4 | async-start | bytes 1048576 | tf_op jit(solution)/shard_map/all_to_all | solution.py:41
  128.6 7.1 %collective-permute-start.19 = (bf16[512,512]{1,0:T(8,128)(2,1)S(1)}, bf16[512,512]{1,0:T(8,128)(2,1)S(1)}, u32[]{:S(2)}, u32[]{:S(2)}) collective-permute-start(bf16[512,512]{1,0:T(8,128)(2,1)S(1)} %bitcast.22), channel_id=1, source_target_pairs={{0,2},{1,3},{2,0},{3,1},{4,6},{5,7},{6,4},{7,5},{8,10},{9,11},{10,... | collective-permute-start | bytes 1572872 | tf_op jit(solution)/shard_map/ppermute | solution.py:22
  (3 other events, 3.6 us)

commit v5 on v4

--- a/solution.py
+++ b/solution.py
@@ -177,7 +177,7 @@
 
 def behind(
     near_hbm, back_hbm, slope_hbm, self_weight_hbm,
-    own_grad, g_own_other, g_on_same, g_on_other, g_off_same, g_off_other,
+    own_grad, g_own_other, g_on, g_off_same, g_off_other,
     near, back, slope, self_weight, sems,
 ):
     order = (1, 2, 3, 4, 5, 0)
@@ -187,7 +187,8 @@
     for copy in copies:
         copy.start()
     copies[0].wait()
-    outs = (None, g_own_other, g_on_same, g_on_other, g_off_same, g_off_other)
+    rows = near.shape[1]
+    outs = (None, g_own_other, g_on.at[pl.ds(0, rows)], g_on.at[pl.ds(rows, rows)], g_off_same, g_off_other)
     for n, p in enumerate(order[:-1]):
         copies[1 + n].wait()
         outs[p][...] = dot(near[p], back[...], 0, 0).astype(BF)
@@ -284,11 +285,11 @@
     w, h = kept[:N_X], kept[N_X:]
     w, h, slope, back = barrier((w, h, slope, back))
 
-    own_grad, g_own_other, g_on_same, g_on_other, g_off_same, g_off_other = pl.pallas_call(
+    own_grad, g_own_other, g_on, g_off_same, g_off_other = pl.pallas_call(
         behind,
         in_specs=[hbm] * 4,
-        out_specs=[vmem] * 6,
-        out_shape=[shape((rows, width), F32)] + [wide] * 5,
+        out_specs=[vmem] * 5,
+        out_shape=[shape((rows, width), F32), wide, shape((2 * rows, width), BF), wide, wide],
         scratch_shapes=[
             pltpu.VMEM((8, rows, width), BF),
             pltpu.VMEM((rows, width), BF),
@@ -302,17 +303,16 @@
     )(near, back, slope, self_weight)
 
     w = collect_x(w)
-    g = (g_own_other, g_on_same, g_on_other, g_off_same, g_off_other)
+    g = (g_own_other, g_on, g_off_same, g_off_other)
     w, h, g = barrier((w, h, g))
-    g_own_other, g_on_same, g_on_other, g_off_same, g_off_other = g
+    g_own_other, g_on, g_off_same, g_off_other = g
     w = lax.all_to_all(w.reshape(N_WIDE, 4, width), WIDE, 0, 0, tiled=True).astype(F32).sum(0).astype(BF)
     h = collect_x(h)
-    r_on_other = to_core(g_on_other)
+    r_on = to_core(g_on)
     r_off_same = to_side(g_off_same)
-    r_on_same = to_core(g_on_same)
-
-    w, h, r_on_other, r_off_same, r_on_same = barrier((w, h, r_on_other, r_off_same, r_on_same))
-    s_side = plus(g_own_other, r_on_other)
+
+    w, h, r_on, r_off_same = barrier((w, h, r_on, r_off_same))
+    s_side = plus(g_own_other, r_on[rows:])
     s_off = plus(g_off_other, r_off_same)
     r_side = to_side(s_side)
     r_off = to_off(s_off)
@@ -323,7 +323,7 @@
     w = spread(w, ("x",), N_X)
     w, r_side, r_off = barrier((w, r_side, r_off))
     there = to_core(w)
-    feature_gradient = own_grad + r_on_same.astype(F32) + r_side.astype(F32) + r_off.astype(F32)
+    feature_gradient = own_grad + r_on[:rows].astype(F32) + r_side.astype(F32) + r_off.astype(F32)
     mine = lax.broadcasted_iota(jnp.int32, (1, 2, 1, 1), 1) == core[0]
     w, there = w.reshape(N_X, 1, BLK, width), there.reshape(N_X, 1, BLK, width)
     weights = [

time: 138 us -> 135 us (0.978)
  starting transfers between devices: 71.4 us -> 68 us
    ppermute x6, starting transfers between devices: 12.9 us -> 10.7 us  [to_x(): return lax.ppermute(value, 'x', [(x, x ^ flip) for x in range(N_X)])]
    ppermute x7 -> x6, starting transfers between devices: 9.53 us -> 9.04 us  [to_core(): return lax.ppermute(value, AXES, [(d, d ^ 2) for d in range(DEVICES)])]
    ppermute x7 -> x6, waiting for transfers between devices: 4.91 us -> 4.66 us  [to_core(): return lax.ppermute(value, AXES, [(d, d ^ 2) for d in range(DEVICES)])]
  transfers between devices with their start and end apart: 25 -> 24, of which waited for: 10 -> 9; matrix products, arithmetic and copies ran while one was open for 8% -> 9% of each run, Pallas kernels for 9% -> 9%
where the time goes in v5:
time: 135 us; the launch traced here: 134 us
  starting transfers between devices  68 us (50%)
  waiting for transfers between devices  27.2 us (20%)
  Pallas kernels  20 us (15%)
  other arithmetic  10.1 us (7%)
  local copies, waits for them, and re-layouts  7.44 us (6%)
  between operations  1.63 us (1%)
    all_to_all x3, starting transfers between devices, spread(): lax.all_to_all(copies, axes, 0, 0, tiled=True).reshape(-1, value.shape[-1])  17.2 us
    ppermute x3, starting transfers between devices, to_off(): return lax.ppermute(value, AXES, pairs)  16 us
    ppermute x6, starting transfers between devices, to_x(): return lax.ppermute(value, 'x', [(x, x ^ flip) for x in range(N_X)])  10.7 us
    ppermute x3, waiting for transfers between devices, to_off(): return lax.ppermute(value, AXES, pairs)  10.5 us
    all_to_all x1, waiting for transfers between devices, local(): lax.all_to_all(w.reshape(N_WIDE, 4, width), WIDE, 0, 0, tiled=True)  9.23 us
    ppermute x6, starting transfers between devices, to_core(): return lax.ppermute(value, AXES, [(d, d ^ 2) for d in range(DEVICES)])  9.04 us
    all_to_all x1, starting transfers between devices, local(): lax.all_to_all(w.reshape(N_WIDE, 4, width), WIDE, 0, 0, tiled=True)  8.8 us
    pallas_call x1, Pallas kernels, local(): pl.pallas_call(ahead, in_specs=[smem] * 2 + [hbm] * 13, out_specs=[vmem]...  7.44 us
  transfers between devices with their start and end apart: 24, of which 9 were waited for; matrix products, arithmetic and copies ran while one was open for 9% of the time, Pallas kernels for 9%

profile of v5, /device:TPU:1, one launch (start us, length us, event | category | flops | bytes accessed | tf_op | source)
XLA Modules:
  0.0 134.3 jit_solution(11385069860048111126)
XLA Ops:
  0.6 2.2 %collective-permute-start = (bf16[512,512]{1,0:T(8,128)(2,1)}, bf16[512,512]{1,0:T(8,128)(2,1)S(1)}, u32[]{:S(2)}, u32[]{:S(2)}) collective-permute-start(bf16[512,512]{1,0:T(8,128)(2,1)} %features.1), channel_id=1, source_target_pairs={{0,1},{1,0},{2,3},{3,2},{4,5},{5,4},{6,7},{7,6},{8,9},{9,8},{10,11... | collective-permute-start | bytes 1572872 | tf_op jit(solution)/shard_map/ppermute | solution.py:26
  2.8 4.6 %collective-permute-start.1 = (bf16[512,512]{1,0:T(8,128)(2,1)}, bf16[512,512]{1,0:T(8,128)(2,1)S(1)}, u32[]{:S(2)}, u32[]{:S(2)}) collective-permute-start(bf16[512,512]{1,0:T(8,128)(2,1)} %features.1), channel_id=1, source_target_pairs={{2,5},{3,4},{4,3},{5,2},{6,9},{7,8},{8,7},{9,6},{10,13},{11,12},{1... | collective-permute-start | bytes 1572872 | tf_op jit(solution)/shard_map/ppermute | solution.py:36
  7.6 1.4 %broadcast_in_dim.82 = bf16[32,4,512]{2,1,0:T(4,128)(2,1)} broadcast(bf16[4,512]{1,0:T(4,128)(2,1)} %param.11), dimensions={1,2} | broadcast | bytes 135168 | tf_op jit(solution)/shard_map/broadcast_in_dim | solution.py:40
  9.0 9.5 %all-to-all-start = ((bf16[32,4,512]{2,1,0:T(4,128)(2,1)}), bf16[32,4,512]{2,1,0:T(4,128)(2,1)S(1)}, u32[]{:S(2)}, u32[]{:S(2)}) async-start(bf16[32,4,512]{2,1,0:T(4,128)(2,1)} %broadcast_in_dim.82), calls=%async_computation | async-start | bytes 262144 | tf_op jit(solution)/shard_map/all_to_all | solution.py:41
  18.5 1.7 %copy.15.order_col = s32[1024,1]{1,0:T(8,128)} copy(s32[1024,1]{0,1:T(1,128)} %bitcast.30) | data formatting | bytes 8192 | tf_op jit(solution)/shard_map/reshape | solution.py:251
  20.9 7.1 %prepare.1 = (bf16[8,512,512]{2,1,0:T(8,128)(2,1)}, f32[512,512]{1,0:T(8,128)}) custom-call(s32[1,64]{1,0:T(1,128)} %dest.1, s32[1,64]{1,0:T(1,128)} %source.1, s32[1]{0:T(128)S(6)} %copy.16.count, s32[1]{0:T(128)} %bitcast.2.side, s32[1]{0:T(128)} %bitcast.core_ref, s32[1024,1]{1,0:T(8,128)} %copy.15.order_col, bf16[512,512]{1,0:T(8,128)(2,1)} %features.1, ...), custom_call_target="tpu_custom_call" | custom-call | flops 1300000000 | bytes 9000000 | tf_op jit(solution)/shard_map/prepare/pallas_call | solution.py:234
  28.1 2.0 %collective-permute-start.5 = (bf16[512,512]{1,0:T(8,128)(2,1)S(1)}, bf16[512,512]{1,0:T(8,128)(2,1)S(1)}, u32[]{:S(2)}, u32[]{:S(2)}) collective-permute-start(bf16[512,512]{1,0:T(8,128)(2,1)S(1)} %collective-permute-done.own_other), channel_id=1, source_target_pairs={{0,2},{1,3},{2,0},{3,1},{4,6},{5,7},{6,4},{7,5},{8,10},{9,11},{10,... | collective-permute-start | bytes 1572872 | tf_op jit(solution)/shard_map/ppermute | solution.py:22
  31.0 4.0 %all-to-all-start.1 = ((bf16[4,128,512]{2,1,0:T(8,128)(2,1)}), bf16[4,128,512]{2,1,0:T(8,128)(2,1)S(1)}, u32[]{:S(2)}, u32[]{:S(2)}) async-start(bf16[4,128,512]{2,1,0:T(8,128)(2,1)} %broadcast_in_dim.83), calls=%async_computation.1 | async-start | bytes 1048576 | tf_op jit(solution)/shard_map/all_to_all | solution.py:41
  35.0 4.3 %collective-permute-start.4 = (bf16[256,512]{1,0:T(8,128)(2,1)S(1)}, bf16[256,512]{1,0:T(8,128)(2,1)S(1)}, u32[]{:S(2)}, u32[]{:S(2)}) collective-permute-start(bf16[256,512]{1,0:T(8,128)(2,1)S(1)} %slice.59), channel_id=1, source_target_pairs={{2,5},{3,4},{4,3},{5,2},{6,9},{7,8},{8,7},{9,6},{10,13},{11,12},{1... | collective-permute-start | bytes 786440 | tf_op jit(solution)/shard_map/ppermute | solution.py:36
  39.5 6.0 %collective-permute-done.4.off_same_high = bf16[256,512]{1,0:T(8,128)(2,1)S(1)} collective-permute-done((bf16[256,512]{1,0:T(8,128)(2,1)S(1)}, bf16[256,512]{1,0:T(8,128)(2,1)S(1)}, u32[]{:S(2)}, u32[]{:S(2)}) %collective-permute-start.4) | collective-permute-done | bytes 262176 | tf_op jit(solution)/shard_map/ppermute | solution.py:36
  46.2 1.9 %collective-permute-done.6.hubs_there = bf16[512,512]{1,0:T(8,128)(2,1)S(1)} collective-permute-done((bf16[512,512]{1,0:T(8,128)(2,1)S(1)}, bf16[512,512]{1,0:T(8,128)(2,1)S(1)}, u32[]{:S(2)}, u32[]{:S(2)}) %collective-permute-start.6) | collective-permute-done | bytes 524320 | tf_op jit(solution)/shard_map/ppermute | solution.py:22
  49.0 7.4 %ahead.1 = (bf16[512,512]{1,0:T(8,128)(2,1)}, bf16[512,512]{1,0:T(8,128)(2,1)}, bf16[512,512]{1,0:T(8,128)(2,1)}, bf16[1024,512]{1,0:T(8,128)(2,1)}, bf16[128,51...) custom-call(s32[1]{0:T(128)} %bitcast.core_ref, ...), custom_call_target="tpu_custom_call" | custom-call | flops 4000000000 | bytes 12000000 | tf_op jit(solution)/shard_map/ahead/pallas_call | solution.py:260
  56.7 2.7 %collective-permute-done.7 = bf16[1024,512]{1,0:T(8,128)(2,1)S(1)} collective-permute-done((bf16[1024,512]{1,0:T(8,128)(2,1)}, bf16[1024,512]{1,0:T(8,128)(2,1)S(1)}, u32[]{:S(2)}, u32[]{:S(2)}) %collective-permute-start.7) | collective-permute-done | bytes 1048608 | tf_op jit(solution)/shard_map/ppermute | solution.py:22
  59.4 1.6 %add_convert_fusion.4 = (bf16[128,512]{1,0:T(8,128)(2,1)S(1)}, bf16[128,512]{1,0:T(8,128)(2,1)S(1)}, bf16[128,512]{1,0:T(8,128)(2,1)S(1)}, bf16[128,512]{1,0:T(8...) fusion(bf16[128,512]{1,0:T(8,128)(2,1)} %get-tuple-element.81, ...), kind=kLoop, calls=%fused_computation.11 | loop fusion | flops 2097152 | bytes 3145728 | tf_op jit(solution)/shard_map/convert_element_type | solution.py:201
  61.0 5.4 %collective-permute-start.10 = (bf16[128,512]{1,0:T(8,128)(2,1)S(1)}, bf16[128,512]{1,0:T(8,128)(2,1)S(1)}, u32[]{:S(2)}, u32[]{:S(2)}) collective-permute-start(bf16[128,512]{1,0:T(8,128)(2,1)S(1)} %get-tuple-element.90), channel_id=1, source_target_pairs={{0,192},{64,128},{128,64},{192,0},{1,193},{65,129},{129,65},{193,1... | collective-permute-start | bytes 393224 | tf_op jit(solution)/shard_map/ppermute | solution.py:45
  66.4 1.5 %collective-permute-start.9 = (bf16[128,512]{1,0:T(8,128)(2,1)S(1)}, bf16[128,512]{1,0:T(8,128)(2,1)S(1)}, u32[]{:S(2)}, u32[]{:S(2)}) collective-permute-start(bf16[128,512]{1,0:T(8,128)(2,1)S(1)} %get-tuple-element.89), channel_id=1, source_target_pairs={{0,128},{64,192},{128,0},{192,64},{1,129},{65,193},{129,1},{193,65... | collective-permute-start | bytes 393224 | tf_op jit(solution)/shard_map/ppermute | solution.py:45
  67.8 5.5 %behind.1 = (f32[512,512]{1,0:T(8,128)}, bf16[512,512]{1,0:T(8,128)(2,1)}, bf16[1024,512]{1,0:T(8,128)(2,1)}, bf16[512,512]{1,0:T(8,128)(2,1)}, bf16[512,512]{1,0:T(8,128)(2,1)}) custom-call(bf16[8,512,512]{2,1,0:T(8,128)(2,1)} %get-tuple-element.62.near_hbm, bf16[512,512]{1,0:T(8,128)(2,1)} %get-tuple-element.84.back_hbm, ...), custom_call_target="tpu_custom_call" | custom-call | flops 2000000000 | bytes 8000000 | tf_op jit(solution)/shard_map/behind/pallas_call | solution.py:288
  74.0 1.3 collective-permute-start.14
  75.4 3.4 %collective-permute-start.12 = (bf16[128,512]{1,0:T(8,128)(2,1)S(1)}, bf16[128,512]{1,0:T(8,128)(2,1)S(1)}, u32[]{:S(2)}, u32[]{:S(2)}) collective-permute-start(bf16[128,512]{1,0:T(8,128)(2,1)S(1)} %get-tuple-element.102), channel_id=1, source_target_pairs={{0,128},{64,192},{128,0},{192,64},{1,129},{65,193},{129,1},{193,65... | collective-permute-start | bytes 393224 | tf_op jit(solution)/shard_map/ppermute | solution.py:45
  79.8 8.8 %all-to-all-start.2 = ((bf16[32,4,512]{2,1,0:T(4,128)(2,1)}), bf16[32,4,512]{2,1,0:T(4,128)(2,1)S(1)}, u32[]{:S(2)}, u32[]{:S(2)}) async-start(bf16[32,4,512]{2,1,0:T(4,128)(2,1)} %reshape.70), calls=%async_computation.2 | async-start | bytes 262144 | tf_op jit(solution)/shard_map/all_to_all | solution.py:309
  88.7 9.2 %all-to-all-done.2 = bf16[32,4,512]{2,1,0:T(4,128)(2,1)S(1)} async-done(((bf16[32,4,512]{2,1,0:T(4,128)(2,1)}), bf16[32,4,512]{2,1,0:T(4,128)(2,1)S(1)}, u32[]{:S(2)}, u32[]{:S(2)}) %all-to-all-start.2) | async-done | bytes 131104 | tf_op jit(solution)/shard_map/all_to_all | solution.py:309
  99.0 3.9 %all-to-all-start.3 = ((bf16[32,8,512]{2,1,0:T(8,128)(2,1)}), bf16[32,8,512]{2,1,0:T(8,128)(2,1)S(1)}, u32[]{:S(2)}, u32[]{:S(2)}) async-start(bf16[32,8,512]{2,1,0:T(8,128)(2,1)} %pad_maximum_fusion), calls=%async_computation.3 | async-start | bytes 524288 | tf_op jit(solution)/shard_map/all_to_all | solution.py:320
  102.9 2.0 %add_convert_fusion = bf16[512,512]{1,0:T(8,128)(2,1)} fusion(bf16[512,512]{1,0:T(8,128)(2,1)S(1)} %collective-permute-done.15, bf16[512,512]{1,0:T(8,128)(2,1)} %get-tuple-element.110), kind=kLoop, calls=%fused_computation.1 | loop fusion | flops 1048576 | bytes 1572864 | tf_op jit(solution)/shard_map/convert_element_type | solution.py:201
  104.8 7.1 %collective-permute-start.17 = (bf16[512,512]{1,0:T(8,128)(2,1)}, bf16[512,512]{1,0:T(8,128)(2,1)S(1)}, u32[]{:S(2)}, u32[]{:S(2)}) collective-permute-start(bf16[512,512]{1,0:T(8,128)(2,1)} %add_convert_fusion), channel_id=1, source_target_pairs={{2,5},{3,4},{4,3},{5,2},{6,9},{7,8},{8,7},{9,6},{10,13},{11,12},{1... | collective-permute-start | bytes 1572872 | tf_op jit(solution)/shard_map/ppermute | solution.py:36
  111.9 0.9 add_convert_fusion.1
  113.5 0.8 broadcast_in_dim.86
  114.4 3.7 %all-to-all-start.4 = ((bf16[4,128,512]{2,1,0:T(8,128)(2,1)}), bf16[4,128,512]{2,1,0:T(8,128)(2,1)S(1)}, u32[]{:S(2)}, u32[]{:S(2)}) async-start(bf16[4,128,512]{2,1,0:T(8,128)(2,1)} %broadcast_in_dim.86), calls=%async_computation.4 | async-start | bytes 1048576 | tf_op jit(solution)/shard_map/all_to_all | solution.py:41
  118.8 4.5 %collective-permute-done.17 = bf16[512,512]{1,0:T(8,128)(2,1)S(1)} collective-permute-done((bf16[512,512]{1,0:T(8,128)(2,1)}, bf16[512,512]{1,0:T(8,128)(2,1)S(1)}, u32[]{:S(2)}, u32[]{:S(2)}) %collective-permute-start.17) | collective-permute-done | bytes 524320 | tf_op jit(solution)/shard_map/ppermute | solution.py:36
  124.1 0.9 all-to-all-done.4
  125.0 5.4 %collective-permute-start.18 = (bf16[512,512]{1,0:T(8,128)(2,1)S(1)}, bf16[512,512]{1,0:T(8,128)(2,1)S(1)}, u32[]{:S(2)}, u32[]{:S(2)}) collective-permute-start(bf16[512,512]{1,0:T(8,128)(2,1)S(1)} %bitcast.22), channel_id=1, source_target_pairs={{0,2},{1,3},{2,0},{3,1},{4,6},{5,7},{6,4},{7,5},{8,10},{9,11},{10,... | collective-permute-start | bytes 1572872 | tf_op jit(solution)/shard_map/ppermute | solution.py:22
  130.5 2.3 %convert_add_fusion = f32[512,512]{1,0:T(8,128)} fusion(bf16[512,512]{1,0:T(8,128)(2,1)S(1)} %collective-permute-done.17, bf16[512,512]{1,0:T(8,128)(2,1)} %collective-permute-done.16, f32[512,512]{1,0:T(8,128)S(1)} %copy-done, bf16[1024,512]{1,0:T(8,128)(2,1)S(1)} %collective-permute-done.14), kind=kLoop, calls=%fused_computation | loop fusion | flops 1572864 | bytes 3670016 | tf_op jit(solution)/shard_map/add | solution.py:326
  132.8 1.5 %fusion = (f32[512,512]{1,0:T(8,128)}, f32[512,512]{1,0:T(8,128)}) fusion(pred[512]{0:T(512)(128)(4,1)S(1)} %broadcast_in_dim.88, bf16[2,128,512]{2,1,0:T(8,128)(2,1)S(1)} %bitcast.26, bf16[2,128,512]{2,1,0:T(8,128)(2,1)S(1)} %bitcast.24, bf16[2,128,512]{2,1,0:T(8,128)(2,1)S(1)} %bitcast.27, bf16[2,128,512]{2,1,0:T(8,128)(2,1)S(1)} %bitcast.25), kind=kLoop, calls=%fused_computation.4 | loop fusion | flops 1048576 | bytes 3146240 | tf_op jit(solution)/shard_map/convert_element_type | solution.py:330
  (66 shorter events, 8.1 us)
Async XLA Ops:
  0.6 27.4 %collective-permute-start = (bf16[512,512]{1,0:T(8,128)(2,1)}, bf16[512,512]{1,0:T(8,128)(2,1)S(1)}, u32[]{:S(2)}, u32[]{:S(2)}) collective-permute-start(bf16[512,512]{1,0:T(8,128)(2,1)} %features.1), channel_id=1, source_target_pairs={{0,1},{1,0},{2,3},{3,2},{4,5},{5,4},{6,7},{7,6},{8,9},{9,8},{10,11... | collective-permute-start | bytes 1572872 | tf_op jit(solution)/shard_map/ppermute | solution.py:26
  2.8 25.2 %collective-permute-start.1 = (bf16[512,512]{1,0:T(8,128)(2,1)}, bf16[512,512]{1,0:T(8,128)(2,1)S(1)}, u32[]{:S(2)}, u32[]{:S(2)}) collective-permute-start(bf16[512,512]{1,0:T(8,128)(2,1)} %features.1), channel_id=1, source_target_pairs={{2,5},{3,4},{4,3},{5,2},{6,9},{7,8},{8,7},{9,6},{10,13},{11,12},{1... | collective-permute-start | bytes 1572872 | tf_op jit(solution)/shard_map/ppermute | solution.py:36
  7.5 20.6 %collective-permute-start.2 = (bf16[512,512]{1,0:T(8,128)(2,1)}, bf16[512,512]{1,0:T(8,128)(2,1)S(1)}, u32[]{:S(2)}, u32[]{:S(2)}) collective-permute-start(bf16[512,512]{1,0:T(8,128)(2,1)} %features.1), channel_id=1, source_target_pairs={{0,2},{1,3},{2,0},{3,1},{4,6},{5,7},{6,4},{7,5},{8,10},{9,11},{10,... | collective-permute-start | bytes 1572872 | tf_op jit(solution)/shard_map/ppermute | solution.py:22
  9.0 19.0 %all-to-all-start = ((bf16[32,4,512]{2,1,0:T(4,128)(2,1)}), bf16[32,4,512]{2,1,0:T(4,128)(2,1)S(1)}, u32[]{:S(2)}, u32[]{:S(2)}) async-start(bf16[32,4,512]{2,1,0:T(4,128)(2,1)} %broadcast_in_dim.82), calls=%async_computation | async-start | bytes 262144 | tf_op jit(solution)/shard_map/all_to_all | solution.py:41
  28.1 20.1 %copy-start.3 = (bf16[512,512]{1,0:T(8,128)(2,1)}, bf16[512,512]{1,0:T(8,128)(2,1)S(1)}, u32[]{:S(2)}) copy-start(bf16[512,512]{1,0:T(8,128)(2,1)S(1)} %collective-permute-done.own_other) | copy-start | bytes 1572868
  28.1 20.1 %copy-start.4 = (bf16[512,512]{1,0:T(8,128)(2,1)}, bf16[512,512]{1,0:T(8,128)(2,1)S(1)}, u32[]{:S(2)}) copy-start(bf16[512,512]{1,0:T(8,128)(2,1)S(1)} %collective-permute-done.1.off_other) | copy-start | bytes 1572868
  28.1 20.0 %copy-start.5 = (bf16[512,512]{1,0:T(8,128)(2,1)}, bf16[512,512]{1,0:T(8,128)(2,1)S(1)}, u32[]{:S(2)}) copy-start(bf16[512,512]{1,0:T(8,128)(2,1)S(1)} %collective-permute-done.2.on_same) | copy-start | bytes 1572868
  28.1 17.4 %collective-permute-start.5 = (bf16[512,512]{1,0:T(8,128)(2,1)S(1)}, bf16[512,512]{1,0:T(8,128)(2,1)S(1)}, u32[]{:S(2)}, u32[]{:S(2)}) collective-permute-start(bf16[512,512]{1,0:T(8,128)(2,1)S(1)} %collective-permute-done.own_other), channel_id=1, source_target_pairs={{0,2},{1,3},{2,0},{3,1},{4,6},{5,7},{6,4},{7,5},{8,10},{9,11},{10,... | collective-permute-start | bytes 1572872 | tf_op jit(solution)/shard_map/ppermute | solution.py:22
  31.0 14.5 %all-to-all-start.1 = ((bf16[4,128,512]{2,1,0:T(8,128)(2,1)}), bf16[4,128,512]{2,1,0:T(8,128)(2,1)S(1)}, u32[]{:S(2)}, u32[]{:S(2)}) async-start(bf16[4,128,512]{2,1,0:T(8,128)(2,1)} %broadcast_in_dim.83), calls=%async_computation.1 | async-start | bytes 1048576 | tf_op jit(solution)/shard_map/all_to_all | solution.py:41
  35.0 10.4 %collective-permute-start.4 = (bf16[256,512]{1,0:T(8,128)(2,1)S(1)}, bf16[256,512]{1,0:T(8,128)(2,1)S(1)}, u32[]{:S(2)}, u32[]{:S(2)}) collective-permute-start(bf16[256,512]{1,0:T(8,128)(2,1)S(1)} %slice.59), channel_id=1, source_target_pairs={{2,5},{3,4},{4,3},{5,2},{6,9},{7,8},{8,7},{9,6},{10,13},{11,12},{1... | collective-permute-start | bytes 786440 | tf_op jit(solution)/shard_map/ppermute | solution.py:36
  39.4 6.1 %collective-permute-start.3 = (bf16[256,512]{1,0:T(8,128)(2,1)S(1)}, bf16[256,512]{1,0:T(8,128)(2,1)S(1)}, u32[]{:S(2)}, u32[]{:S(2)}) collective-permute-start(bf16[256,512]{1,0:T(8,128)(2,1)S(1)} %slice.58), channel_id=1, source_target_pairs={{0,1},{1,0},{2,3},{3,2},{4,5},{5,4},{6,7},{7,6},{8,9},{9,8},{10,11... | collective-permute-start | bytes 786440 | tf_op jit(solution)/shard_map/ppermute | solution.py:26
  45.4 2.7 %copy-start.8 = (bf16[256,512]{1,0:T(8,128)(2,1)}, bf16[256,512]{1,0:T(8,128)(2,1)S(1)}, u32[]{:S(2)}) copy-start(bf16[256,512]{1,0:T(8,128)(2,1)S(1)} %collective-permute-done.4.off_same_high) | copy-start | bytes 786436
  45.5 2.7 %copy-start.2 = (bf16[4,128,512]{2,1,0:T(8,128)(2,1)}, bf16[4,128,512]{2,1,0:T(8,128)(2,1)S(1)}, u32[]{:S(2)}) copy-start(bf16[4,128,512]{2,1,0:T(8,128)(2,1)S(1)} %all-to-all-done.1) | copy-start | bytes 1572868
  46.2 1.9 %copy-start.6 = (bf16[512,512]{1,0:T(8,128)(2,1)}, bf16[512,512]{1,0:T(8,128)(2,1)S(1)}, u32[]{:S(2)}) copy-start(bf16[512,512]{1,0:T(8,128)(2,1)S(1)} %collective-permute-done.5.on_other) | copy-start | bytes 1572868
  46.2 1.9 %collective-permute-start.6 = (bf16[512,512]{1,0:T(8,128)(2,1)S(1)}, bf16[512,512]{1,0:T(8,128)(2,1)S(1)}, u32[]{:S(2)}, u32[]{:S(2)}) collective-permute-start(bf16[512,512]{1,0:T(8,128)(2,1)S(1)} %bitcast.28), channel_id=1, source_target_pairs={{0,2},{1,3},{2,0},{3,1},{4,6},{5,7},{6,4},{7,5},{8,10},{9,11},{10,... | collective-permute-start | bytes 1572872 | tf_op jit(solution)/shard_map/ppermute | solution.py:22
  56.4 3.0 %collective-permute-start.7 = (bf16[1024,512]{1,0:T(8,128)(2,1)}, bf16[1024,512]{1,0:T(8,128)(2,1)S(1)}, u32[]{:S(2)}, u32[]{:S(2)}) collective-permute-start(bf16[1024,512]{1,0:T(8,128)(2,1)} %get-tuple-element.74), channel_id=1, source_target_pairs={{0,2},{1,3},{2,0},{3,1},{4,6},{5,7},{6,4},{7,5},{8,10},{9,11},{10,... | collective-permute-start | bytes 3145736 | tf_op jit(solution)/shard_map/ppermute | solution.py:22
  61.0 12.3 %collective-permute-start.10 = (bf16[128,512]{1,0:T(8,128)(2,1)S(1)}, bf16[128,512]{1,0:T(8,128)(2,1)S(1)}, u32[]{:S(2)}, u32[]{:S(2)}) collective-permute-start(bf16[128,512]{1,0:T(8,128)(2,1)S(1)} %get-tuple-element.90), channel_id=1, source_target_pairs={{0,192},{64,128},{128,64},{192,0},{1,193},{65,129},{129,65},{193,1... | collective-permute-start | bytes 393224 | tf_op jit(solution)/shard_map/ppermute | solution.py:45
  66.4 7.0 %collective-permute-start.8 = (bf16[128,512]{1,0:T(8,128)(2,1)S(1)}, bf16[128,512]{1,0:T(8,128)(2,1)S(1)}, u32[]{:S(2)}, u32[]{:S(2)}) collective-permute-start(bf16[128,512]{1,0:T(8,128)(2,1)S(1)} %get-tuple-element.88), channel_id=1, source_target_pairs={{0,64},{64,0},{128,192},{192,128},{1,65},{65,1},{129,193},{193,129... | collective-permute-start | bytes 393224 | tf_op jit(solution)/shard_map/ppermute | solution.py:45
  66.4 7.5 %collective-permute-start.9 = (bf16[128,512]{1,0:T(8,128)(2,1)S(1)}, bf16[128,512]{1,0:T(8,128)(2,1)S(1)}, u32[]{:S(2)}, u32[]{:S(2)}) collective-permute-start(bf16[128,512]{1,0:T(8,128)(2,1)S(1)} %get-tuple-element.89), channel_id=1, source_target_pairs={{0,128},{64,192},{128,0},{192,64},{1,129},{65,193},{129,1},{193,65... | collective-permute-start | bytes 393224 | tf_op jit(solution)/shard_map/ppermute | solution.py:45
  73.3 38.6 %copy-start.1 = (bf16[512,512]{1,0:T(8,128)(2,1)S(1)}, bf16[512,512]{1,0:T(8,128)(2,1)}, u32[]{:S(2)}) copy-start(bf16[512,512]{1,0:T(8,128)(2,1)} %get-tuple-element.109) | copy-start | bytes 1572868
  74.0 24.1 %collective-permute-start.14 = (bf16[1024,512]{1,0:T(8,128)(2,1)}, bf16[1024,512]{1,0:T(8,128)(2,1)S(1)}, u32[]{:S(2)}, u32[]{:S(2)}) collective-permute-start(bf16[1024,512]{1,0:T(8,128)(2,1)} %get-tuple-element.104), channel_id=1, source_target_pairs={{0,2},{1,3},{2,0},{3,1},{4,6},{5,7},{6,4},{7,5},{8,10},{9,11},{10,... | collective-permute-start | bytes 3145736 | tf_op jit(solution)/shard_map/ppermute | solution.py:22
  75.2 22.8 %collective-permute-start.15 = (bf16[512,512]{1,0:T(8,128)(2,1)}, bf16[512,512]{1,0:T(8,128)(2,1)S(1)}, u32[]{:S(2)}, u32[]{:S(2)}) collective-permute-start(bf16[512,512]{1,0:T(8,128)(2,1)} %get-tuple-element.105), channel_id=1, source_target_pairs={{0,1},{1,0},{2,3},{3,2},{4,5},{5,4},{6,7},{7,6},{8,9},{9,8},{10,11... | collective-permute-start | bytes 1572872 | tf_op jit(solution)/shard_map/ppermute | solution.py:26
  75.3 13.4 %collective-permute-start.11 = (bf16[128,512]{1,0:T(8,128)(2,1)S(1)}, bf16[128,512]{1,0:T(8,128)(2,1)S(1)}, u32[]{:S(2)}, u32[]{:S(2)}) collective-permute-start(bf16[128,512]{1,0:T(8,128)(2,1)S(1)} %get-tuple-element.101), channel_id=1, source_target_pairs={{0,64},{64,0},{128,192},{192,128},{1,65},{65,1},{129,193},{193,129... | collective-permute-start | bytes 393224 | tf_op jit(solution)/shard_map/ppermute | solution.py:45
  75.4 13.2 %collective-permute-start.12 = (bf16[128,512]{1,0:T(8,128)(2,1)S(1)}, bf16[128,512]{1,0:T(8,128)(2,1)S(1)}, u32[]{:S(2)}, u32[]{:S(2)}) collective-permute-start(bf16[128,512]{1,0:T(8,128)(2,1)S(1)} %get-tuple-element.102), channel_id=1, source_target_pairs={{0,128},{64,192},{128,0},{192,64},{1,129},{65,193},{129,1},{193,65... | collective-permute-start | bytes 393224 | tf_op jit(solution)/shard_map/ppermute | solution.py:45
  78.8 9.8 %collective-permute-start.13 = (bf16[128,512]{1,0:T(8,128)(2,1)S(1)}, bf16[128,512]{1,0:T(8,128)(2,1)S(1)}, u32[]{:S(2)}, u32[]{:S(2)}) collective-permute-start(bf16[128,512]{1,0:T(8,128)(2,1)S(1)} %get-tuple-element.103), channel_id=1, source_target_pairs={{0,192},{64,128},{128,64},{192,0},{1,193},{65,129},{129,65},{193,1... | collective-permute-start | bytes 393224 | tf_op jit(solution)/shard_map/ppermute | solution.py:45
  79.8 18.2 %all-to-all-start.2 = ((bf16[32,4,512]{2,1,0:T(4,128)(2,1)}), bf16[32,4,512]{2,1,0:T(4,128)(2,1)S(1)}, u32[]{:S(2)}, u32[]{:S(2)}) async-start(bf16[32,4,512]{2,1,0:T(4,128)(2,1)} %reshape.70), calls=%async_computation.2 | async-start | bytes 262144 | tf_op jit(solution)/shard_map/all_to_all | solution.py:309
  88.7 41.7 %copy-start = (f32[512,512]{1,0:T(8,128)S(1)}, f32[512,512]{1,0:T(8,128)}, u32[]{:S(2)}) copy-start(f32[512,512]{1,0:T(8,128)} %get-tuple-element.86) | copy-start | bytes 3145732
  99.0 14.5 %all-to-all-start.3 = ((bf16[32,8,512]{2,1,0:T(8,128)(2,1)}), bf16[32,8,512]{2,1,0:T(8,128)(2,1)S(1)}, u32[]{:S(2)}, u32[]{:S(2)}) async-start(bf16[32,8,512]{2,1,0:T(8,128)(2,1)} %pad_maximum_fusion), calls=%async_computation.3 | async-start | bytes 524288 | tf_op jit(solution)/shard_map/all_to_all | solution.py:320
  104.8 18.5 %collective-permute-start.17 = (bf16[512,512]{1,0:T(8,128)(2,1)}, bf16[512,512]{1,0:T(8,128)(2,1)S(1)}, u32[]{:S(2)}, u32[]{:S(2)}) collective-permute-start(bf16[512,512]{1,0:T(8,128)(2,1)} %add_convert_fusion), channel_id=1, source_target_pairs={{2,5},{3,4},{4,3},{5,2},{6,9},{7,8},{8,7},{9,6},{10,13},{11,12},{1... | collective-permute-start | bytes 1572872 | tf_op jit(solution)/shard_map/ppermute | solution.py:36
  112.8 11.2 %collective-permute-start.16 = (bf16[512,512]{1,0:T(8,128)(2,1)}, bf16[512,512]{1,0:T(8,128)(2,1)}, u32[]{:S(2)}, u32[]{:S(2)}) collective-permute-start(bf16[512,512]{1,0:T(8,128)(2,1)} %add_convert_fusion.1), channel_id=1, source_target_pairs={{0,1},{1,0},{2,3},{3,2},{4,5},{5,4},{6,7},{7,6},{8,9},{9,8},{10,11... | collective-permute-start | bytes 1572872 | tf_op jit(solution)/shard_map/ppermute | solution.py:26
  114.4 10.6 %all-to-all-start.4 = ((bf16[4,128,512]{2,1,0:T(8,128)(2,1)}), bf16[4,128,512]{2,1,0:T(8,128)(2,1)S(1)}, u32[]{:S(2)}, u32[]{:S(2)}) async-start(bf16[4,128,512]{2,1,0:T(8,128)(2,1)} %broadcast_in_dim.86), calls=%async_computation.4 | async-start | bytes 1048576 | tf_op jit(solution)/shard_map/all_to_all | solution.py:41
  125.0 7.8 %collective-permute-start.18 = (bf16[512,512]{1,0:T(8,128)(2,1)S(1)}, bf16[512,512]{1,0:T(8,128)(2,1)S(1)}, u32[]{:S(2)}, u32[]{:S(2)}) collective-permute-start(bf16[512,512]{1,0:T(8,128)(2,1)S(1)} %bitcast.22), channel_id=1, source_target_pairs={{0,2},{1,3},{2,0},{3,1},{4,6},{5,7},{6,4},{7,5},{8,10},{9,11},{10,... | collective-permute-start | bytes 1572872 | tf_op jit(solution)/shard_map/ppermute | solution.py:22
  (2 other events, 1.6 us)

commit v6 on v5

--- a/solution.py
+++ b/solution.py
@@ -65,9 +65,9 @@
 
 
 def prepare(
-    dest, source, count, side, core_ref, order_col, features_hbm, self_weight_hbm, tiles_hbm,
-    near, own_pre,
-    cells, hub_cells, pick, features, self_weight, tiles, sems,
+    dest, source, count, side, core_ref, order, features_hbm, self_weight_hbm, tiles_hbm,
+    near_hbm, own_pre,
+    near, cells, hub_cells, place, features, self_weight, tiles, sems,
 ):
     copies = [
         pltpu.make_async_copy(*refs, sems.at[n])
@@ -78,10 +78,10 @@
     live, flip, core = count[0], 4 * side[0], core_ref[0]
     for r in range(2):
         for x in range(N_X):
-            ids = hub_of(lax.broadcasted_iota(jnp.int32, (BLK, BLK), 1) + (2 * x + (core ^ r)) * BLK)
+            ids = hub_of(lax.broadcasted_iota(jnp.int32, (BLK, BLK), 0) + (2 * x + (core ^ r)) * BLK)
             for j in range(8):
-                rows = pl.ds(j * BLK, BLK)
-                pick[r, rows, pl.ds(x * BLK, BLK)] = (order_col[rows, :] == ids).astype(F32).astype(BF)
+                columns = pl.ds(j * BLK, BLK)
+                place[r, pl.ds(x * BLK, BLK), columns] = (ids == order[:, columns]).astype(F32).astype(BF)
     cells[...] = jnp.zeros_like(cells)
     for copy in copies:
         copy.wait()
@@ -99,16 +99,19 @@
         return carry
 
     lax.fori_loop(0, (live + 3) // 4, add, 0)
-    for p in range(8):
+    stores = [pltpu.make_async_copy(near.at[p], near_hbm.at[p], sems.at[3 + p]) for p in range(8)]
+    for j in range(8):
+        hub_cells[:, pl.ds(j * BLK, BLK)] = cells[6 + j // 4, j % 4].astype(BF)
+    for r in range(2):
+        near[6 + r] = dot(hub_cells[...], place[r], 1, 1).astype(BF)
+        stores[6 + r].start()
+    for p in range(6):
         for j in range(4):
-            cell = cells[p, j].astype(BF)
-            if p < 6:
-                near[p, :, pl.ds(j * BLK, BLK)] = cell
-            else:
-                hub_cells[:, pl.ds(((p - 6) * 4 + j) * BLK, BLK)] = cell
-    for r in range(2):
-        near[6 + r] = dot(hub_cells[...], pick[r]).astype(BF)
+            near[p, :, pl.ds(j * BLK, BLK)] = cells[p, j].astype(BF)
+        stores[p].start()
     own_pre[...] = dot(features[...], self_weight[...])
+    for store in stores:
+        store.wait()
 
 
 def ahead(
@@ -228,33 +231,36 @@
 
     own_other = to_side(features)
     off_other = to_off(features)
-    on_same = to_core(features)
     hubs = spread(hub_features, WIDE, N_WIDE)
     pieces = shape((8, rows, width), BF)
     near, own_pre = pl.pallas_call(
         prepare,
         in_specs=[smem] * 5 + [vmem] + [hbm] * 3,
-        out_specs=[vmem] * 2,
+        out_specs=[hbm, vmem],
         out_shape=[pieces, shape((rows, width), F32)],
         scratch_shapes=[
+            pltpu.VMEM((8, rows, width), BF),
             pltpu.VMEM((8, 4, rows, BLK), F32),
             pltpu.VMEM((rows, 8 * BLK), BF),
-            pltpu.VMEM((2, 8 * BLK, 4 * BLK), BF),
+            pltpu.VMEM((2, 4 * BLK, 8 * BLK), BF),
             pltpu.VMEM((rows, width), BF),
             pltpu.VMEM((width, width), BF),
             pltpu.VMEM(tile_values.shape, BF),
-            pltpu.SemaphoreType.DMA((3,)),
+            pltpu.SemaphoreType.DMA((11,)),
         ],
         compiler_params=params,
         cost_estimate=pl.CostEstimate(flops=13 * 10**8, bytes_accessed=9 * 10**6, transcendentals=0),
         name="prepare",
-    )(tile_dest, tile_source, tile_count, side, core, hub_order.reshape(-1, 1), features, self_weight, tile_values)
-    own_other, off_other, on_same, hubs, near, own_pre = barrier((own_other, off_other, on_same, hubs, near, own_pre))
+    )(tile_dest, tile_source, tile_count, side, core, hub_order.reshape(1, -1), features, self_weight, tile_values)
+    own_other, off_other, hubs, near, own_pre, rows_here = barrier((own_other, off_other, hubs, near, own_pre, features))
+    on_same = to_core(rows_here)
     off_same_low = to_side(off_other[:rows // 2])
     off_same_high = to_off(own_other[rows // 2:])
     on_other = to_core(own_other)
     hubs = spread(hubs, ("x",), N_X)
-    hubs, off_same_low, off_same_high, on_other = barrier((hubs, off_same_low, off_same_high, on_other))
+    hubs, off_same_low, off_same_high, on_same, on_other = barrier(
+        (hubs, off_same_low, off_same_high, on_same, on_other)
+    )
     hubs_there = to_core(hubs)
 
     embedding, slope, back, send, *kept = pl.pallas_call(

time: 135 us -> 132 us (0.978)
  starting transfers between devices: 68 us -> 64.5 us
  waiting for transfers between devices: 27.2 us -> 29.7 us
  local copies, waits for them, and re-layouts: 7.44 us -> 4.99 us
    all_to_all x3, waiting for transfers between devices: 0.89 us -> 3.52 us  [spread(): lax.all_to_all(copies, axes, 0, 0, tiled=True).reshape(-1, value.shape[-1])]
    all_to_all x1, starting transfers between devices: 8.8 us -> 6.23 us  [local(): lax.all_to_all(w.reshape(N_WIDE, 4, width), WIDE, 0, 0, tiled=True)]
    all_to_all x1, waiting for transfers between devices: 9.23 us -> 7.49 us  [local(): lax.all_to_all(w.reshape(N_WIDE, 4, width), WIDE, 0, 0, tiled=True)]
    ppermute x6, waiting for transfers between devices: 0.58 us -> 2.32 us  [to_x(): return lax.ppermute(value, 'x', [(x, x ^ flip) for x in range(N_X)])]
    reshape x1 -> x0, local copies, waits for them, and re-layouts: 1.71 us -> none  [local(): hub_order.reshape(-1, 1)]
  transfers between devices with their start and end apart: 24 -> 24, of which waited for: 9 -> 12; matrix products, arithmetic and copies ran while one was open for 9% -> 8% of each run, Pallas kernels for 9% -> 9%
where the time goes in v6:
time: 132 us; the launch traced here: 131 us
  starting transfers between devices  64.5 us (49%)
  waiting for transfers between devices  29.7 us (22%)
  Pallas kernels  19.8 us (15%)
  other arithmetic  10.1 us (8%)
  local copies, waits for them, and re-layouts  4.99 us (4%)
  between operations  1.6 us (1%)
    all_to_all x3, starting transfers between devices, spread(): lax.all_to_all(copies, axes, 0, 0, tiled=True).reshape(-1, value.shape[-1])  17.4 us
    ppermute x3, starting transfers between devices, to_off(): return lax.ppermute(value, AXES, pairs)  15.1 us
    ppermute x6, starting transfers between devices, to_x(): return lax.ppermute(value, 'x', [(x, x ^ flip) for x in range(N_X)])  10.4 us
    ppermute x3, waiting for transfers between devices, to_off(): return lax.ppermute(value, AXES, pairs)  10.3 us
    ppermute x6, starting transfers between devices, to_core(): return lax.ppermute(value, AXES, [(d, d ^ 2) for d in range(DEVICES)])  9.23 us
    all_to_all x1, waiting for transfers between devices, local(): lax.all_to_all(w.reshape(N_WIDE, 4, width), WIDE, 0, 0, tiled=True)  7.49 us
    pallas_call x1, Pallas kernels, local(): pl.pallas_call(ahead, in_specs=[smem] * 2 + [hbm] * 13, out_specs=[vmem]...  7.44 us
    pallas_call x1, Pallas kernels, local(): pl.pallas_call(prepare, in_specs=[smem] * 5 + [vmem] + [hbm] * 3, out_spe...  6.87 us
  transfers between devices with their start and end apart: 24, of which 12 were waited for; matrix products, arithmetic and copies ran while one was open for 8% of the time, Pallas kernels for 9%

profile of v6, /device:TPU:1, one launch (start us, length us, event | category | flops | bytes accessed | tf_op | source)
XLA Modules:
  0.0 130.6 jit_solution(13207759106802907787)
XLA Ops:
  0.6 2.2 %collective-permute-start = (bf16[512,512]{1,0:T(8,128)(2,1)}, bf16[512,512]{1,0:T(8,128)(2,1)S(1)}, u32[]{:S(2)}, u32[]{:S(2)}) collective-permute-start(bf16[512,512]{1,0:T(8,128)(2,1)} %features.1), channel_id=1, source_target_pairs={{0,1},{1,0},{2,3},{3,2},{4,5},{5,4},{6,7},{7,6},{8,9},{9,8},{10,11... | collective-permute-start | bytes 1572872 | tf_op jit(solution)/shard_map/ppermute | solution.py:26
  2.9 4.6 %collective-permute-start.1 = (bf16[512,512]{1,0:T(8,128)(2,1)}, bf16[512,512]{1,0:T(8,128)(2,1)S(1)}, u32[]{:S(2)}, u32[]{:S(2)}) collective-permute-start(bf16[512,512]{1,0:T(8,128)(2,1)} %features.1), channel_id=1, source_target_pairs={{2,5},{3,4},{4,3},{5,2},{6,9},{7,8},{8,7},{9,6},{10,13},{11,12},{1... | collective-permute-start | bytes 1572872 | tf_op jit(solution)/shard_map/ppermute | solution.py:36
  7.5 1.4 %broadcast_in_dim.82 = bf16[32,4,512]{2,1,0:T(4,128)(2,1)} broadcast(bf16[4,512]{1,0:T(4,128)(2,1)} %param.11), dimensions={1,2} | broadcast | bytes 135168 | tf_op jit(solution)/shard_map/broadcast_in_dim | solution.py:40
  8.9 9.5 %all-to-all-start = ((bf16[32,4,512]{2,1,0:T(4,128)(2,1)}), bf16[32,4,512]{2,1,0:T(4,128)(2,1)S(1)}, u32[]{:S(2)}, u32[]{:S(2)}) async-start(bf16[32,4,512]{2,1,0:T(4,128)(2,1)} %broadcast_in_dim.82), calls=%async_computation | async-start | bytes 262144 | tf_op jit(solution)/shard_map/all_to_all | solution.py:41
  19.1 6.9 %prepare.1 = (bf16[8,512,512]{2,1,0:T(8,128)(2,1)}, f32[512,512]{1,0:T(8,128)}) custom-call(s32[1,64]{1,0:T(1,128)} %dest.1, s32[1,64]{1,0:T(1,128)} %source.1, s32[1]{0:T(128)S(6)} %copy.15.count, s32[1]{0:T(128)} %bitcast.2.side, s32[1]{0:T(128)} %bitcast.core_ref, s32[1,1024]{1,0:T(1,128)} %bitcast.30, bf16[512,512]{1,0:T(8,128)(2,1)} %features.1, ...), custom_call_target="tpu_custom_call" | custom-call | flops 1300000000 | bytes 9000000 | tf_op jit(solution)/shard_map/prepare/pallas_call | solution.py:236
  25.9 2.5 %all-to-all-done = bf16[32,4,512]{2,1,0:T(4,128)(2,1)S(1)} async-done(((bf16[32,4,512]{2,1,0:T(4,128)(2,1)}), bf16[32,4,512]{2,1,0:T(4,128)(2,1)S(1)}, u32[]{:S(2)}, u32[]{:S(2)}) %all-to-all-start) | async-done | bytes 131104 | tf_op jit(solution)/shard_map/all_to_all | solution.py:41
  28.5 1.6 %collective-permute-start.5 = (bf16[512,512]{1,0:T(8,128)(2,1)S(1)}, bf16[512,512]{1,0:T(8,128)(2,1)S(1)}, u32[]{:S(2)}, u32[]{:S(2)}) collective-permute-start(bf16[512,512]{1,0:T(8,128)(2,1)S(1)} %collective-permute-done.own_other), channel_id=1, source_target_pairs={{0,2},{1,3},{2,0},{3,1},{4,6},{5,7},{6,4},{7,5},{8,10},{9,11},{10,... | collective-permute-start | bytes 1572872 | tf_op jit(solution)/shard_map/ppermute | solution.py:22
  31.0 4.0 %all-to-all-start.1 = ((bf16[4,128,512]{2,1,0:T(8,128)(2,1)}), bf16[4,128,512]{2,1,0:T(8,128)(2,1)S(1)}, u32[]{:S(2)}, u32[]{:S(2)}) async-start(bf16[4,128,512]{2,1,0:T(8,128)(2,1)} %broadcast_in_dim.83), calls=%async_computation.1 | async-start | bytes 1048576 | tf_op jit(solution)/shard_map/all_to_all | solution.py:41
  35.0 3.4 %collective-permute-start.3 = (bf16[256,512]{1,0:T(8,128)(2,1)S(1)}, bf16[256,512]{1,0:T(8,128)(2,1)S(1)}, u32[]{:S(2)}, u32[]{:S(2)}) collective-permute-start(bf16[256,512]{1,0:T(8,128)(2,1)S(1)} %slice.59), channel_id=1, source_target_pairs={{2,5},{3,4},{4,3},{5,2},{6,9},{7,8},{8,7},{9,6},{10,13},{11,12},{1... | collective-permute-start | bytes 786440 | tf_op jit(solution)/shard_map/ppermute | solution.py:36
  38.5 6.0 %collective-permute-done.3.off_same_high = bf16[256,512]{1,0:T(8,128)(2,1)S(1)} collective-permute-done((bf16[256,512]{1,0:T(8,128)(2,1)S(1)}, bf16[256,512]{1,0:T(8,128)(2,1)S(1)}, u32[]{:S(2)}, u32[]{:S(2)}) %collective-permute-start.3) | collective-permute-done | bytes 262176 | tf_op jit(solution)/shard_map/ppermute | solution.py:36
  45.6 1.6 %collective-permute-done.6.hubs_there = bf16[512,512]{1,0:T(8,128)(2,1)S(1)} collective-permute-done((bf16[512,512]{1,0:T(8,128)(2,1)S(1)}, bf16[512,512]{1,0:T(8,128)(2,1)S(1)}, u32[]{:S(2)}, u32[]{:S(2)}) %collective-permute-start.6) | collective-permute-done | bytes 524320 | tf_op jit(solution)/shard_map/ppermute | solution.py:22
  48.0 7.4 %ahead.1 = (bf16[512,512]{1,0:T(8,128)(2,1)}, bf16[512,512]{1,0:T(8,128)(2,1)}, bf16[512,512]{1,0:T(8,128)(2,1)}, bf16[1024,512]{1,0:T(8,128)(2,1)}, bf16[128,51...) custom-call(s32[1]{0:T(128)} %bitcast.core_ref, ...), custom_call_target="tpu_custom_call" | custom-call | flops 4000000000 | bytes 12000000 | tf_op jit(solution)/shard_map/ahead/pallas_call | solution.py:266
  55.9 2.5 %collective-permute-done.7 = bf16[1024,512]{1,0:T(8,128)(2,1)S(1)} collective-permute-done((bf16[1024,512]{1,0:T(8,128)(2,1)}, bf16[1024,512]{1,0:T(8,128)(2,1)S(1)}, u32[]{:S(2)}, u32[]{:S(2)}) %collective-permute-start.7) | collective-permute-done | bytes 1048608 | tf_op jit(solution)/shard_map/ppermute | solution.py:22
  58.4 1.6 %add_convert_fusion.4 = (bf16[128,512]{1,0:T(8,128)(2,1)S(1)}, bf16[128,512]{1,0:T(8,128)(2,1)S(1)}, bf16[128,512]{1,0:T(8,128)(2,1)S(1)}, bf16[128,512]{1,0:T(8...) fusion(bf16[128,512]{1,0:T(8,128)(2,1)} %get-tuple-element.83, ...), kind=kLoop, calls=%fused_computation.11 | loop fusion | flops 2097152 | bytes 3145728 | tf_op jit(solution)/shard_map/convert_element_type | solution.py:204
  60.0 5.2 %collective-permute-start.10 = (bf16[128,512]{1,0:T(8,128)(2,1)S(1)}, bf16[128,512]{1,0:T(8,128)(2,1)S(1)}, u32[]{:S(2)}, u32[]{:S(2)}) collective-permute-start(bf16[128,512]{1,0:T(8,128)(2,1)S(1)} %get-tuple-element.92), channel_id=1, source_target_pairs={{0,192},{64,128},{128,64},{192,0},{1,193},{65,129},{129,65},{193,1... | collective-permute-start | bytes 393224 | tf_op jit(solution)/shard_map/ppermute | solution.py:45
  65.2 1.3 collective-permute-start.9
  66.5 5.5 %behind.1 = (f32[512,512]{1,0:T(8,128)}, bf16[512,512]{1,0:T(8,128)(2,1)}, bf16[1024,512]{1,0:T(8,128)(2,1)}, bf16[512,512]{1,0:T(8,128)(2,1)}, bf16[512,512]{1,0:T(8,128)(2,1)}) custom-call(bf16[8,512,512]{2,1,0:T(8,128)(2,1)} %get-tuple-element.63.near_hbm, bf16[512,512]{1,0:T(8,128)(2,1)} %get-tuple-element.86.back_hbm, ...), custom_call_target="tpu_custom_call" | custom-call | flops 2000000000 | bytes 8000000 | tf_op jit(solution)/shard_map/behind/pallas_call | solution.py:294
  72.6 1.3 collective-permute-start.14
  74.3 3.4 %collective-permute-start.12 = (bf16[128,512]{1,0:T(8,128)(2,1)S(1)}, bf16[128,512]{1,0:T(8,128)(2,1)S(1)}, u32[]{:S(2)}, u32[]{:S(2)}) collective-permute-start(bf16[128,512]{1,0:T(8,128)(2,1)S(1)} %get-tuple-element.104), channel_id=1, source_target_pairs={{0,128},{64,192},{128,0},{192,64},{1,129},{65,193},{129,1},{193,65... | collective-permute-start | bytes 393224 | tf_op jit(solution)/shard_map/ppermute | solution.py:45
  78.5 6.2 %all-to-all-start.2 = ((bf16[32,4,512]{2,1,0:T(4,128)(2,1)}), bf16[32,4,512]{2,1,0:T(4,128)(2,1)S(1)}, u32[]{:S(2)}, u32[]{:S(2)}) async-start(bf16[32,4,512]{2,1,0:T(4,128)(2,1)} %reshape.70), calls=%async_computation.2 | async-start | bytes 262144 | tf_op jit(solution)/shard_map/all_to_all | solution.py:315
  84.7 1.8 %collective-permute-done.13 = bf16[128,512]{1,0:T(8,128)(2,1)S(1)} collective-permute-done((bf16[128,512]{1,0:T(8,128)(2,1)S(1)}, bf16[128,512]{1,0:T(8,128)(2,1)S(1)}, u32[]{:S(2)}, u32[]{:S(2)}) %collective-permute-start.13) | collective-permute-done | bytes 131104 | tf_op jit(solution)/shard_map/ppermute | solution.py:45
  86.6 7.5 %all-to-all-done.2 = bf16[32,4,512]{2,1,0:T(4,128)(2,1)S(1)} async-done(((bf16[32,4,512]{2,1,0:T(4,128)(2,1)}), bf16[32,4,512]{2,1,0:T(4,128)(2,1)S(1)}, u32[]{:S(2)}, u32[]{:S(2)}) %all-to-all-start.2) | async-done | bytes 131104 | tf_op jit(solution)/shard_map/all_to_all | solution.py:315
  95.1 3.9 %all-to-all-start.3 = ((bf16[32,8,512]{2,1,0:T(8,128)(2,1)}), bf16[32,8,512]{2,1,0:T(8,128)(2,1)S(1)}, u32[]{:S(2)}, u32[]{:S(2)}) async-start(bf16[32,8,512]{2,1,0:T(8,128)(2,1)} %pad_maximum_fusion), calls=%async_computation.3 | async-start | bytes 524288 | tf_op jit(solution)/shard_map/all_to_all | solution.py:326
  99.0 2.0 %add_convert_fusion = bf16[512,512]{1,0:T(8,128)(2,1)} fusion(bf16[512,512]{1,0:T(8,128)(2,1)S(1)} %collective-permute-done.15, bf16[512,512]{1,0:T(8,128)(2,1)} %get-tuple-element.112), kind=kLoop, calls=%fused_computation.1 | loop fusion | flops 1048576 | bytes 1572864 | tf_op jit(solution)/shard_map/convert_element_type | solution.py:204
  100.9 7.1 %collective-permute-start.17 = (bf16[512,512]{1,0:T(8,128)(2,1)}, bf16[512,512]{1,0:T(8,128)(2,1)S(1)}, u32[]{:S(2)}, u32[]{:S(2)}) collective-permute-start(bf16[512,512]{1,0:T(8,128)(2,1)} %add_convert_fusion), channel_id=1, source_target_pairs={{2,5},{3,4},{4,3},{5,2},{6,9},{7,8},{8,7},{9,6},{10,13},{11,12},{1... | collective-permute-start | bytes 1572872 | tf_op jit(solution)/shard_map/ppermute | solution.py:36
  108.0 0.9 add_convert_fusion.1
  110.5 3.8 %all-to-all-start.4 = ((bf16[4,128,512]{2,1,0:T(8,128)(2,1)}), bf16[4,128,512]{2,1,0:T(8,128)(2,1)S(1)}, u32[]{:S(2)}, u32[]{:S(2)}) async-start(bf16[4,128,512]{2,1,0:T(8,128)(2,1)} %broadcast_in_dim.86), calls=%async_computation.4 | async-start | bytes 1048576 | tf_op jit(solution)/shard_map/all_to_all | solution.py:41
  115.1 4.3 %collective-permute-done.17 = bf16[512,512]{1,0:T(8,128)(2,1)S(1)} collective-permute-done((bf16[512,512]{1,0:T(8,128)(2,1)}, bf16[512,512]{1,0:T(8,128)(2,1)S(1)}, u32[]{:S(2)}, u32[]{:S(2)}) %collective-permute-start.17) | collective-permute-done | bytes 524320 | tf_op jit(solution)/shard_map/ppermute | solution.py:36
  120.2 1.1 all-to-all-done.4
  121.3 5.4 %collective-permute-start.18 = (bf16[512,512]{1,0:T(8,128)(2,1)S(1)}, bf16[512,512]{1,0:T(8,128)(2,1)S(1)}, u32[]{:S(2)}, u32[]{:S(2)}) collective-permute-start(bf16[512,512]{1,0:T(8,128)(2,1)S(1)} %bitcast.22), channel_id=1, source_target_pairs={{0,2},{1,3},{2,0},{3,1},{4,6},{5,7},{6,4},{7,5},{8,10},{9,11},{10,... | collective-permute-start | bytes 1572872 | tf_op jit(solution)/shard_map/ppermute | solution.py:22
  126.7 2.3 %convert_add_fusion = f32[512,512]{1,0:T(8,128)} fusion(bf16[512,512]{1,0:T(8,128)(2,1)S(1)} %collective-permute-done.17, bf16[512,512]{1,0:T(8,128)(2,1)} %collective-permute-done.16, f32[512,512]{1,0:T(8,128)S(1)} %copy-done, bf16[1024,512]{1,0:T(8,128)(2,1)S(1)} %collective-permute-done.14), kind=kLoop, calls=%fused_computation | loop fusion | flops 1572864 | bytes 3670016 | tf_op jit(solution)/shard_map/add | solution.py:332
  129.1 1.5 %fusion = (f32[512,512]{1,0:T(8,128)}, f32[512,512]{1,0:T(8,128)}) fusion(pred[512]{0:T(512)(128)(4,1)S(1)} %broadcast_in_dim.88, bf16[2,128,512]{2,1,0:T(8,128)(2,1)S(1)} %bitcast.26, bf16[2,128,512]{2,1,0:T(8,128)(2,1)S(1)} %bitcast.24, bf16[2,128,512]{2,1,0:T(8,128)(2,1)S(1)} %bitcast.27, bf16[2,128,512]{2,1,0:T(8,128)(2,1)S(1)} %bitcast.25), kind=kLoop, calls=%fused_computation.4 | loop fusion | flops 1048576 | bytes 3146240 | tf_op jit(solution)/shard_map/convert_element_type | solution.py:336
  (65 shorter events, 9.3 us)
Async XLA Ops:
  0.6 29.4 %copy-start.5 = (bf16[512,512]{1,0:T(8,128)(2,1)S(1)}, bf16[512,512]{1,0:T(8,128)(2,1)}, u32[]{:S(2)}) copy-start(bf16[512,512]{1,0:T(8,128)(2,1)} %features.1) | copy-start | bytes 1572868
  0.6 27.8 %collective-permute-start = (bf16[512,512]{1,0:T(8,128)(2,1)}, bf16[512,512]{1,0:T(8,128)(2,1)S(1)}, u32[]{:S(2)}, u32[]{:S(2)}) collective-permute-start(bf16[512,512]{1,0:T(8,128)(2,1)} %features.1), channel_id=1, source_target_pairs={{0,1},{1,0},{2,3},{3,2},{4,5},{5,4},{6,7},{7,6},{8,9},{9,8},{10,11... | collective-permute-start | bytes 1572872 | tf_op jit(solution)/shard_map/ppermute | solution.py:26
  2.9 25.6 %collective-permute-start.1 = (bf16[512,512]{1,0:T(8,128)(2,1)}, bf16[512,512]{1,0:T(8,128)(2,1)S(1)}, u32[]{:S(2)}, u32[]{:S(2)}) collective-permute-start(bf16[512,512]{1,0:T(8,128)(2,1)} %features.1), channel_id=1, source_target_pairs={{2,5},{3,4},{4,3},{5,2},{6,9},{7,8},{8,7},{9,6},{10,13},{11,12},{1... | collective-permute-start | bytes 1572872 | tf_op jit(solution)/shard_map/ppermute | solution.py:36
  8.9 19.5 %all-to-all-start = ((bf16[32,4,512]{2,1,0:T(4,128)(2,1)}), bf16[32,4,512]{2,1,0:T(4,128)(2,1)S(1)}, u32[]{:S(2)}, u32[]{:S(2)}) async-start(bf16[32,4,512]{2,1,0:T(4,128)(2,1)} %broadcast_in_dim.82), calls=%async_computation | async-start | bytes 262144 | tf_op jit(solution)/shard_map/all_to_all | solution.py:41
  28.5 18.7 %copy-start.3 = (bf16[512,512]{1,0:T(8,128)(2,1)}, bf16[512,512]{1,0:T(8,128)(2,1)S(1)}, u32[]{:S(2)}) copy-start(bf16[512,512]{1,0:T(8,128)(2,1)S(1)} %collective-permute-done.own_other) | copy-start | bytes 1572868
  28.5 18.7 %copy-start.4 = (bf16[512,512]{1,0:T(8,128)(2,1)}, bf16[512,512]{1,0:T(8,128)(2,1)S(1)}, u32[]{:S(2)}) copy-start(bf16[512,512]{1,0:T(8,128)(2,1)S(1)} %collective-permute-done.1.off_other) | copy-start | bytes 1572868
  28.5 16.6 %collective-permute-start.5 = (bf16[512,512]{1,0:T(8,128)(2,1)S(1)}, bf16[512,512]{1,0:T(8,128)(2,1)S(1)}, u32[]{:S(2)}, u32[]{:S(2)}) collective-permute-start(bf16[512,512]{1,0:T(8,128)(2,1)S(1)} %collective-permute-done.own_other), channel_id=1, source_target_pairs={{0,2},{1,3},{2,0},{3,1},{4,6},{5,7},{6,4},{7,5},{8,10},{9,11},{10,... | collective-permute-start | bytes 1572872 | tf_op jit(solution)/shard_map/ppermute | solution.py:22
  30.1 15.1 %collective-permute-start.4 = (bf16[512,512]{1,0:T(8,128)(2,1)S(1)}, bf16[512,512]{1,0:T(8,128)(2,1)S(1)}, u32[]{:S(2)}, u32[]{:S(2)}) collective-permute-start(bf16[512,512]{1,0:T(8,128)(2,1)S(1)} %copy-done.5), channel_id=1, source_target_pairs={{0,2},{1,3},{2,0},{3,1},{4,6},{5,7},{6,4},{7,5},{8,10},{9,11},{10,... | collective-permute-start | bytes 1572872 | tf_op jit(solution)/shard_map/ppermute | solution.py:22
  31.0 14.1 %all-to-all-start.1 = ((bf16[4,128,512]{2,1,0:T(8,128)(2,1)}), bf16[4,128,512]{2,1,0:T(8,128)(2,1)S(1)}, u32[]{:S(2)}, u32[]{:S(2)}) async-start(bf16[4,128,512]{2,1,0:T(8,128)(2,1)} %broadcast_in_dim.83), calls=%async_computation.1 | async-start | bytes 1048576 | tf_op jit(solution)/shard_map/all_to_all | solution.py:41
  35.0 9.5 %collective-permute-start.3 = (bf16[256,512]{1,0:T(8,128)(2,1)S(1)}, bf16[256,512]{1,0:T(8,128)(2,1)S(1)}, u32[]{:S(2)}, u32[]{:S(2)}) collective-permute-start(bf16[256,512]{1,0:T(8,128)(2,1)S(1)} %slice.59), channel_id=1, source_target_pairs={{2,5},{3,4},{4,3},{5,2},{6,9},{7,8},{8,7},{9,6},{10,13},{11,12},{1... | collective-permute-start | bytes 786440 | tf_op jit(solution)/shard_map/ppermute | solution.py:36
  38.4 6.7 %collective-permute-start.2 = (bf16[256,512]{1,0:T(8,128)(2,1)S(1)}, bf16[256,512]{1,0:T(8,128)(2,1)}, u32[]{:S(2)}, u32[]{:S(2)}) collective-permute-start(bf16[256,512]{1,0:T(8,128)(2,1)S(1)} %slice.58), channel_id=1, source_target_pairs={{0,1},{1,0},{2,3},{3,2},{4,5},{5,4},{6,7},{7,6},{8,9},{9,8},{10,11... | collective-permute-start | bytes 786440 | tf_op jit(solution)/shard_map/ppermute | solution.py:26
  44.5 2.6 %copy-start.9 = (bf16[256,512]{1,0:T(8,128)(2,1)}, bf16[256,512]{1,0:T(8,128)(2,1)S(1)}, u32[]{:S(2)}) copy-start(bf16[256,512]{1,0:T(8,128)(2,1)S(1)} %collective-permute-done.3.off_same_high) | copy-start | bytes 786436
  45.1 2.1 %copy-start.2 = (bf16[4,128,512]{2,1,0:T(8,128)(2,1)}, bf16[4,128,512]{2,1,0:T(8,128)(2,1)S(1)}, u32[]{:S(2)}) copy-start(bf16[4,128,512]{2,1,0:T(8,128)(2,1)S(1)} %all-to-all-done.1) | copy-start | bytes 1572868
  45.1 2.1 %copy-start.6 = (bf16[512,512]{1,0:T(8,128)(2,1)}, bf16[512,512]{1,0:T(8,128)(2,1)S(1)}, u32[]{:S(2)}) copy-start(bf16[512,512]{1,0:T(8,128)(2,1)S(1)} %collective-permute-done.5.on_other) | copy-start | bytes 1572868
  45.2 2.0 %collective-permute-start.6 = (bf16[512,512]{1,0:T(8,128)(2,1)S(1)}, bf16[512,512]{1,0:T(8,128)(2,1)S(1)}, u32[]{:S(2)}, u32[]{:S(2)}) collective-permute-start(bf16[512,512]{1,0:T(8,128)(2,1)S(1)} %bitcast.28), channel_id=1, source_target_pairs={{0,2},{1,3},{2,0},{3,1},{4,6},{5,7},{6,4},{7,5},{8,10},{9,11},{10,... | collective-permute-start | bytes 1572872 | tf_op jit(solution)/shard_map/ppermute | solution.py:22
  55.5 3.0 %collective-permute-start.7 = (bf16[1024,512]{1,0:T(8,128)(2,1)}, bf16[1024,512]{1,0:T(8,128)(2,1)S(1)}, u32[]{:S(2)}, u32[]{:S(2)}) collective-permute-start(bf16[1024,512]{1,0:T(8,128)(2,1)} %get-tuple-element.76), channel_id=1, source_target_pairs={{0,2},{1,3},{2,0},{3,1},{4,6},{5,7},{6,4},{7,5},{8,10},{9,11},{10,... | collective-permute-start | bytes 3145736 | tf_op jit(solution)/shard_map/ppermute | solution.py:22
  60.0 12.0 %collective-permute-start.10 = (bf16[128,512]{1,0:T(8,128)(2,1)S(1)}, bf16[128,512]{1,0:T(8,128)(2,1)S(1)}, u32[]{:S(2)}, u32[]{:S(2)}) collective-permute-start(bf16[128,512]{1,0:T(8,128)(2,1)S(1)} %get-tuple-element.92), channel_id=1, source_target_pairs={{0,192},{64,128},{128,64},{192,0},{1,193},{65,129},{129,65},{193,1... | collective-permute-start | bytes 393224 | tf_op jit(solution)/shard_map/ppermute | solution.py:45
  65.2 6.8 %collective-permute-start.8 = (bf16[128,512]{1,0:T(8,128)(2,1)S(1)}, bf16[128,512]{1,0:T(8,128)(2,1)S(1)}, u32[]{:S(2)}, u32[]{:S(2)}) collective-permute-start(bf16[128,512]{1,0:T(8,128)(2,1)S(1)} %get-tuple-element.90), channel_id=1, source_target_pairs={{0,64},{64,0},{128,192},{192,128},{1,65},{65,1},{129,193},{193,129... | collective-permute-start | bytes 393224 | tf_op jit(solution)/shard_map/ppermute | solution.py:45
  65.2 7.3 %collective-permute-start.9 = (bf16[128,512]{1,0:T(8,128)(2,1)S(1)}, bf16[128,512]{1,0:T(8,128)(2,1)S(1)}, u32[]{:S(2)}, u32[]{:S(2)}) collective-permute-start(bf16[128,512]{1,0:T(8,128)(2,1)S(1)} %get-tuple-element.91), channel_id=1, source_target_pairs={{0,128},{64,192},{128,0},{192,64},{1,129},{65,193},{129,1},{193,65... | collective-permute-start | bytes 393224 | tf_op jit(solution)/shard_map/ppermute | solution.py:45
  72.0 36.0 %copy-start.1 = (bf16[512,512]{1,0:T(8,128)(2,1)S(1)}, bf16[512,512]{1,0:T(8,128)(2,1)}, u32[]{:S(2)}) copy-start(bf16[512,512]{1,0:T(8,128)(2,1)} %get-tuple-element.111) | copy-start | bytes 1572868
  72.6 21.5 %collective-permute-start.14 = (bf16[1024,512]{1,0:T(8,128)(2,1)}, bf16[1024,512]{1,0:T(8,128)(2,1)S(1)}, u32[]{:S(2)}, u32[]{:S(2)}) collective-permute-start(bf16[1024,512]{1,0:T(8,128)(2,1)} %get-tuple-element.106), channel_id=1, source_target_pairs={{0,2},{1,3},{2,0},{3,1},{4,6},{5,7},{6,4},{7,5},{8,10},{9,11},{10,... | collective-permute-start | bytes 3145736 | tf_op jit(solution)/shard_map/ppermute | solution.py:22
  73.9 20.2 %collective-permute-start.15 = (bf16[512,512]{1,0:T(8,128)(2,1)}, bf16[512,512]{1,0:T(8,128)(2,1)S(1)}, u32[]{:S(2)}, u32[]{:S(2)}) collective-permute-start(bf16[512,512]{1,0:T(8,128)(2,1)} %get-tuple-element.107), channel_id=1, source_target_pairs={{0,1},{1,0},{2,3},{3,2},{4,5},{5,4},{6,7},{7,6},{8,9},{9,8},{10,11... | collective-permute-start | bytes 1572872 | tf_op jit(solution)/shard_map/ppermute | solution.py:26
  73.9 10.8 %collective-permute-start.11 = (bf16[128,512]{1,0:T(8,128)(2,1)S(1)}, bf16[128,512]{1,0:T(8,128)(2,1)S(1)}, u32[]{:S(2)}, u32[]{:S(2)}) collective-permute-start(bf16[128,512]{1,0:T(8,128)(2,1)S(1)} %get-tuple-element.103), channel_id=1, source_target_pairs={{0,64},{64,0},{128,192},{192,128},{1,65},{65,1},{129,193},{193,129... | collective-permute-start | bytes 393224 | tf_op jit(solution)/shard_map/ppermute | solution.py:45
  74.3 10.5 %collective-permute-start.12 = (bf16[128,512]{1,0:T(8,128)(2,1)S(1)}, bf16[128,512]{1,0:T(8,128)(2,1)S(1)}, u32[]{:S(2)}, u32[]{:S(2)}) collective-permute-start(bf16[128,512]{1,0:T(8,128)(2,1)S(1)} %get-tuple-element.104), channel_id=1, source_target_pairs={{0,128},{64,192},{128,0},{192,64},{1,129},{65,193},{129,1},{193,65... | collective-permute-start | bytes 393224 | tf_op jit(solution)/shard_map/ppermute | solution.py:45
  77.7 8.8 %collective-permute-start.13 = (bf16[128,512]{1,0:T(8,128)(2,1)S(1)}, bf16[128,512]{1,0:T(8,128)(2,1)S(1)}, u32[]{:S(2)}, u32[]{:S(2)}) collective-permute-start(bf16[128,512]{1,0:T(8,128)(2,1)S(1)} %get-tuple-element.105), channel_id=1, source_target_pairs={{0,192},{64,128},{128,64},{192,0},{1,193},{65,129},{129,65},{193,1... | collective-permute-start | bytes 393224 | tf_op jit(solution)/shard_map/ppermute | solution.py:45
  78.5 15.6 %all-to-all-start.2 = ((bf16[32,4,512]{2,1,0:T(4,128)(2,1)}), bf16[32,4,512]{2,1,0:T(4,128)(2,1)S(1)}, u32[]{:S(2)}, u32[]{:S(2)}) async-start(bf16[32,4,512]{2,1,0:T(4,128)(2,1)} %reshape.70), calls=%async_computation.2 | async-start | bytes 262144 | tf_op jit(solution)/shard_map/all_to_all | solution.py:315
  86.6 40.2 %copy-start = (f32[512,512]{1,0:T(8,128)S(1)}, f32[512,512]{1,0:T(8,128)}, u32[]{:S(2)}) copy-start(f32[512,512]{1,0:T(8,128)} %get-tuple-element.88) | copy-start | bytes 3145732
  95.1 14.5 %all-to-all-start.3 = ((bf16[32,8,512]{2,1,0:T(8,128)(2,1)}), bf16[32,8,512]{2,1,0:T(8,128)(2,1)S(1)}, u32[]{:S(2)}, u32[]{:S(2)}) async-start(bf16[32,8,512]{2,1,0:T(8,128)(2,1)} %pad_maximum_fusion), calls=%async_computation.3 | async-start | bytes 524288 | tf_op jit(solution)/shard_map/all_to_all | solution.py:326
  100.9 18.5 %collective-permute-start.17 = (bf16[512,512]{1,0:T(8,128)(2,1)}, bf16[512,512]{1,0:T(8,128)(2,1)S(1)}, u32[]{:S(2)}, u32[]{:S(2)}) collective-permute-start(bf16[512,512]{1,0:T(8,128)(2,1)} %add_convert_fusion), channel_id=1, source_target_pairs={{2,5},{3,4},{4,3},{5,2},{6,9},{7,8},{8,7},{9,6},{10,13},{11,12},{1... | collective-permute-start | bytes 1572872 | tf_op jit(solution)/shard_map/ppermute | solution.py:36
  109.0 11.2 %collective-permute-start.16 = (bf16[512,512]{1,0:T(8,128)(2,1)}, bf16[512,512]{1,0:T(8,128)(2,1)}, u32[]{:S(2)}, u32[]{:S(2)}) collective-permute-start(bf16[512,512]{1,0:T(8,128)(2,1)} %add_convert_fusion.1), channel_id=1, source_target_pairs={{0,1},{1,0},{2,3},{3,2},{4,5},{5,4},{6,7},{7,6},{8,9},{9,8},{10,11... | collective-permute-start | bytes 1572872 | tf_op jit(solution)/shard_map/ppermute | solution.py:26
  110.5 10.8 %all-to-all-start.4 = ((bf16[4,128,512]{2,1,0:T(8,128)(2,1)}), bf16[4,128,512]{2,1,0:T(8,128)(2,1)S(1)}, u32[]{:S(2)}, u32[]{:S(2)}) async-start(bf16[4,128,512]{2,1,0:T(8,128)(2,1)} %broadcast_in_dim.86), calls=%async_computation.4 | async-start | bytes 1048576 | tf_op jit(solution)/shard_map/all_to_all | solution.py:41
  121.3 7.8 %collective-permute-start.18 = (bf16[512,512]{1,0:T(8,128)(2,1)S(1)}, bf16[512,512]{1,0:T(8,128)(2,1)S(1)}, u32[]{:S(2)}, u32[]{:S(2)}) collective-permute-start(bf16[512,512]{1,0:T(8,128)(2,1)S(1)} %bitcast.22), channel_id=1, source_target_pairs={{0,2},{1,3},{2,0},{3,1},{4,6},{5,7},{6,4},{7,5},{8,10},{9,11},{10,... | collective-permute-start | bytes 1572872 | tf_op jit(solution)/shard_map/ppermute | solution.py:22
  (2 other events, 2.9 us)
